TPU v7x, 32 devices: a whole 2x2x4 slice. The times are simulated.
32 devices in a mesh: dp: 16 (over z, y, x), mp: 2 (over core).
Axes of the slice: x: 2, y: 2, z: 4, core: 2. Of those that a mesh axis runs over, the one named last changes fastest.
Arguments:
- tokens: bfloat16 [16384, 768], P('dp'), may hold values from -6 to 6
- masked: int32 [16384], P('dp'), may hold values 0 or 1
- lengths: int32 [128], P('dp'), may hold values from 66 to 128, as said below
- mask_vector: bfloat16 [768], replicated, may hold values from -6 to 6
- w_query: bfloat16 [768, 768], P('dp', 'mp'), may hold values from -0.21875 to 0.21875
- b_query: bfloat16 [768], P('mp'), may hold values from -3 to 3
- w_key: bfloat16 [768, 768], P('dp', 'mp'), may hold values from -0.21875 to 0.21875
- w_value: bfloat16 [768, 768], P('dp', 'mp'), may hold values from -0.21875 to 0.21875
- b_value: bfloat16 [768], P('mp'), may hold values from -3 to 3
- w_out: bfloat16 [768, 768], P('mp', 'dp'), may hold values from -1.25 to 1.25
- b_out: bfloat16 [768], replicated, may hold values from -3 to 3
- gain_one: bfloat16 [768], replicated, may hold values from 0.099609375 to 1.8984375
- shift_one: bfloat16 [768], replicated, may hold values from -2 to 2
- w_up: bfloat16 [768, 3072], P('dp', 'mp'), may hold values from -0.21875 to 0.21875
- b_up: bfloat16 [3072], P('mp'), may hold values from -3 to 3
- w_down: bfloat16 [3072, 768], P('mp', 'dp'), may hold values from -0.109375 to 0.109375
- b_down: bfloat16 [768], replicated, may hold values from -3 to 3
- gain_two: bfloat16 [768], replicated, may hold values from 0.099609375 to 1.8984375
- shift_two: bfloat16 [768], replicated, may hold values from -2 to 2
- grad_out: bfloat16 [16384, 768], P('dp'), may hold values from -6 to 6
Outputs:
- out: bfloat16 [16384, 768], P('dp')
- d_tokens: float32 [16384, 768], P('dp')
- d_mask_vector: float32 [768], replicated
- d_w_query: float32 [768, 768], P('dp', 'mp')
- d_b_query: float32 [768], P('mp')
- d_w_key: float32 [768, 768], P('dp', 'mp')
- d_w_value: float32 [768, 768], P('dp', 'mp')
- d_b_value: float32 [768], P('mp')
- d_w_out: float32 [768, 768], P('mp', 'dp')
- d_b_out: float32 [768], replicated
- d_gain_one: float32 [768], replicated
- d_shift_one: float32 [768], replicated
- d_w_up: float32 [768, 3072], P('dp', 'mp')
- d_b_up: float32 [3072], P('mp')
- d_w_down: float32 [3072, 768], P('mp', 'dp')
- d_b_down: float32 [768], replicated
- d_gain_two: float32 [768], replicated
- d_shift_two: float32 [768], replicated
Inputs may be any that keep to these rules, and one draw needn't show every extreme that they name: `lengths`: the first chain of each aligned block of 8 chains uses all 128 slots; the others lose up to 62 slots, small losses more often than large ones.
All inputs are finite; a program needn't handle non-finite values. No bound on the sum of `masked` on one device may be relied on, other than what follows from the above.
Results may differ from a plain program's by a relative error of at most 0.018.
Values may be sent and summed in bfloat16 or wider, within the bound.
No kernel may reach another device: no remote copies, remote signals or barrier semaphores. Data moves between devices by JAX's collectives and lax.ppermute only.
A program may use at most 128 MiB of HBM per device.

v0:
```python
import jax
import jax.numpy as jnp
from jax import lax
from jax.sharding import PartitionSpec as P

HEAD = 64
MICRO = 4


NORM_EPS = 1e-05


def layer_norm(values, norm_gain, norm_shift):
    row_mean = jnp.mean(values, axis=-1, keepdims=True)
    centred = values - row_mean
    inverse = lax.rsqrt(jnp.mean(centred * centred, axis=-1, keepdims=True) + NORM_EPS)
    normed = centred * inverse
    return (normed * norm_gain + norm_shift, normed, inverse)


def norm_back(incoming, normed, inverse, norm_gain):
    scaled = incoming * norm_gain
    inner = (
        scaled
        - jnp.mean(scaled, axis=-1, keepdims=True)
        - normed * jnp.mean(scaled * normed, axis=-1, keepdims=True)
    )
    return (inverse * inner, jnp.sum(incoming * normed, axis=0), jnp.sum(incoming, axis=0))


def gelu_exact(values):
    return jax.nn.gelu(values, approximate=False)


def micro_batch(raw_tokens, mask_flags, chain_lens, raw_grad, weights, vectors):
    w_query, w_key, w_value, w_out, w_up, w_down = weights
    mask_vector, b_query, b_value, b_out, gain_one, shift_one, b_up, b_down, gain_two, shift_two = (
        vectors
    )
    chain_count = chain_lens.shape[0]
    row_count = raw_tokens.shape[0]
    slot_count = row_count // chain_count
    local_heads = w_query.shape[1] // HEAD
    score_scale = HEAD ** (-0.5)
    f32 = jnp.float32
    b16 = jnp.bfloat16
    is_masked = (mask_flags == 1)[:, None]
    layer_in = jnp.where(is_masked, mask_vector[None, :], raw_tokens.astype(f32))
    in_low = layer_in.astype(b16)
    head_shape = (chain_count, slot_count, local_heads, HEAD)
    query_low = (
        (jnp.dot(in_low, w_query, preferred_element_type=f32) + b_query)
        .astype(b16)
        .reshape(head_shape)
    )
    key_low = jnp.dot(in_low, w_key, preferred_element_type=f32).astype(b16).reshape(head_shape)
    value_low = (
        (jnp.dot(in_low, w_value, preferred_element_type=f32) + b_value)
        .astype(b16)
        .reshape(head_shape)
    )
    key_valid = (jnp.arange(slot_count)[None, :] < chain_lens[:, None])[:, None, None, :]
    scores = (
        jnp.einsum("cqhe,ckhe->chqk", query_low, key_low, preferred_element_type=f32) * score_scale
    )
    scores = jnp.where(key_valid, scores, -1e30)
    row_max = jnp.max(scores, axis=-1, keepdims=True)
    exp_terms = jnp.exp(scores - row_max)
    attn_prob = exp_terms / jnp.sum(exp_terms, axis=-1, keepdims=True)
    prob_low = attn_prob.astype(b16)
    attended = jnp.einsum("chqk,ckhe->cqhe", prob_low, value_low, preferred_element_type=f32)
    attended = attended.reshape(row_count, -1).astype(b16)
    attn_sum = (
        lax.psum(
            jnp.dot(attended, w_out, preferred_element_type=f32).astype(jnp.bfloat16), "mp"
        ).astype(jnp.float32)
        + b_out
    )
    hidden, normed_one, inverse_one = layer_norm(layer_in + attn_sum, gain_one, shift_one)
    hidden_low = hidden.astype(b16)
    pre_act = jnp.dot(hidden_low, w_up, preferred_element_type=f32) + b_up
    activated, gelu_pull = jax.vjp(gelu_exact, pre_act)
    act_low = activated.astype(b16)
    ffn_sum = (
        lax.psum(
            jnp.dot(act_low, w_down, preferred_element_type=f32).astype(jnp.bfloat16), "mp"
        ).astype(jnp.float32)
        + b_down
    )
    result, normed_two, inverse_two = layer_norm(hidden + ffn_sum, gain_two, shift_two)
    out_grad = raw_grad.astype(f32)
    dz_two, d_gain_two, d_shift_two = norm_back(out_grad, normed_two, inverse_two, gain_two)
    d_b_down = jnp.sum(dz_two, axis=0)
    dz_two_low = dz_two.astype(b16)
    d_w_down = jnp.einsum("nf,nd->fd", act_low, dz_two_low, preferred_element_type=f32)
    d_act = jnp.einsum("nd,fd->nf", dz_two_low, w_down, preferred_element_type=f32)
    d_pre = gelu_pull(d_act)[0]
    d_b_up = jnp.sum(d_pre, axis=0)
    d_pre_low = d_pre.astype(b16)
    d_w_up = jnp.einsum("nd,nf->df", hidden_low, d_pre_low, preferred_element_type=f32)
    hidden_part = jnp.einsum("nf,df->nd", d_pre_low, w_up, preferred_element_type=f32)
    d_hidden = dz_two + lax.psum(hidden_part.astype(jnp.bfloat16), "mp").astype(jnp.float32)
    dz_one, d_gain_one, d_shift_one = norm_back(d_hidden, normed_one, inverse_one, gain_one)
    d_b_out = jnp.sum(dz_one, axis=0)
    dz_one_low = dz_one.astype(b16)
    d_w_out = jnp.einsum("nh,nd->hd", attended, dz_one_low, preferred_element_type=f32)
    d_attended = jnp.einsum("nd,hd->nh", dz_one_low, w_out, preferred_element_type=f32)
    d_attended = d_attended.astype(b16).reshape(head_shape)
    d_prob = jnp.einsum("cqhe,ckhe->chqk", d_attended, value_low, preferred_element_type=f32)
    d_scores = attn_prob * (d_prob - jnp.sum(attn_prob * d_prob, axis=-1, keepdims=True))
    d_scores_low = d_scores.astype(b16)
    d_query = (
        jnp.einsum("chqk,ckhe->cqhe", d_scores_low, key_low, preferred_element_type=f32)
        * score_scale
    )
    d_key = (
        jnp.einsum("chqk,cqhe->ckhe", d_scores_low, query_low, preferred_element_type=f32)
        * score_scale
    )
    d_value = jnp.einsum("chqk,cqhe->ckhe", prob_low, d_attended, preferred_element_type=f32)
    d_query = d_query.astype(b16).reshape(row_count, -1)
    d_key = d_key.astype(b16).reshape(row_count, -1)
    d_value = d_value.astype(b16).reshape(row_count, -1)
    d_b_query = jnp.sum(d_query.astype(f32), axis=0)
    d_b_value = jnp.sum(d_value.astype(f32), axis=0)
    d_w_query = jnp.einsum("nd,nh->dh", in_low, d_query, preferred_element_type=f32)
    d_w_key = jnp.einsum("nd,nh->dh", in_low, d_key, preferred_element_type=f32)
    d_w_value = jnp.einsum("nd,nh->dh", in_low, d_value, preferred_element_type=f32)
    input_part = (
        jnp.einsum("nh,dh->nd", d_query, w_query, preferred_element_type=f32)
        + jnp.einsum("nh,dh->nd", d_key, w_key, preferred_element_type=f32)
        + jnp.einsum("nh,dh->nd", d_value, w_value, preferred_element_type=f32)
    )
    d_layer_in = dz_one + lax.psum(input_part.astype(jnp.bfloat16), "mp").astype(jnp.float32)
    d_tokens = jnp.where(is_masked, 0.0, d_layer_in)
    d_mask_vector = jnp.sum(jnp.where(is_masked, d_layer_in, 0.0), axis=0)
    matrices = (d_w_query, d_w_key, d_w_value, d_w_out, d_w_up, d_w_down)
    vector_grads = (
        d_mask_vector,
        d_b_query,
        d_b_value,
        d_b_out,
        d_gain_one,
        d_shift_one,
        d_b_up,
        d_b_down,
        d_gain_two,
        d_shift_two,
    )
    return (result.astype(b16), d_tokens, matrices, vector_grads)


def add_tuples(first, second):
    return tuple((left + right for left, right in zip(first, second)))


def per_device(
    tokens,
    masked,
    lengths,
    mask_vector,
    w_query,
    b_query,
    w_key,
    w_value,
    b_value,
    w_out,
    b_out,
    gain_one,
    shift_one,
    w_up,
    b_up,
    w_down,
    b_down,
    gain_two,
    shift_two,
    grad_out,
):
    vectors = tuple(
        (
            member.astype(jnp.float32)
            for member in (
                mask_vector,
                b_query,
                b_value,
                b_out,
                gain_one,
                shift_one,
                b_up,
                b_down,
                gain_two,
                shift_two,
            )
        )
    )
    batch_chains = lengths.shape[0] // MICRO
    batch_rows = tokens.shape[0] // MICRO
    outputs = []
    input_grads = []
    shares = None
    vector_totals = None
    for batch_index in range(MICRO):
        gathered = (
            lax.all_gather(w_query, "dp", axis=0, tiled=True),
            lax.all_gather(w_key, "dp", axis=0, tiled=True),
            lax.all_gather(w_value, "dp", axis=0, tiled=True),
            lax.all_gather(w_out, "dp", axis=1, tiled=True),
            lax.all_gather(w_up, "dp", axis=0, tiled=True),
            lax.all_gather(w_down, "dp", axis=1, tiled=True),
        )
        row_start = batch_index * batch_rows
        row_stop = row_start + batch_rows
        chain_start = batch_index * batch_chains
        result, d_tokens, matrices, vector_grads = micro_batch(
            tokens[row_start:row_stop],
            masked[row_start:row_stop],
            lengths[chain_start : chain_start + batch_chains],
            grad_out[row_start:row_stop],
            gathered,
            vectors,
        )
        outputs.append(result)
        input_grads.append(d_tokens)
        vector_totals = (
            vector_grads if batch_index == 0 else add_tuples(vector_totals, vector_grads)
        )
        shard_piece = (
            lax.psum_scatter(matrices[0], "dp", scatter_dimension=0, tiled=True),
            lax.psum_scatter(matrices[1], "dp", scatter_dimension=0, tiled=True),
            lax.psum_scatter(matrices[2], "dp", scatter_dimension=0, tiled=True),
            lax.psum_scatter(matrices[3], "dp", scatter_dimension=1, tiled=True),
            lax.psum_scatter(matrices[4], "dp", scatter_dimension=0, tiled=True),
            lax.psum_scatter(matrices[5], "dp", scatter_dimension=1, tiled=True),
        )
        shares = shard_piece if batch_index == 0 else add_tuples(shares, shard_piece)
    summed = lax.psum(vector_totals, "dp")
    return (
        jnp.concatenate(outputs, axis=0),
        jnp.concatenate(input_grads, axis=0),
        summed[0],
        shares[0],
        summed[1],
        shares[1],
        shares[2],
        summed[2],
        shares[3],
        summed[3],
        summed[4],
        summed[5],
        shares[4],
        summed[6],
        shares[5],
        summed[7],
        summed[8],
        summed[9],
    )


def solution(mesh):
    return jax.shard_map(
        per_device,
        mesh=mesh,
        in_specs=(
            P("dp", None),
            P("dp"),
            P("dp"),
            P(),
            P("dp", "mp"),
            P("mp"),
            P("dp", "mp"),
            P("dp", "mp"),
            P("mp"),
            P("mp", "dp"),
            P(),
            P(),
            P(),
            P("dp", "mp"),
            P("mp"),
            P("mp", "dp"),
            P(),
            P(),
            P(),
            P("dp", None),
        ),
        out_specs=(
            P("dp", None),
            P("dp", None),
            P(),
            P("dp", "mp"),
            P("mp"),
            P("dp", "mp"),
            P("dp", "mp"),
            P("mp"),
            P("mp", "dp"),
            P(),
            P(),
            P(),
            P("dp", "mp"),
            P("mp"),
            P("mp", "dp"),
            P(),
            P(),
            P(),
        ),
        check_vma=False,
    )
```

profile of v0, /device:TPU:0, one launch (start us, length us, event | category | flops | bytes accessed | tf_op | source)
XLA Modules:
  0.0 1312.0 jit_solution(5998563677693879449)
XLA Ops:
  10.4 45.9 %all_gather.13 = bf16[768,384]{1,0:T(8,128)(2,1)S(1)} all-gather(bf16[48,384]{1,0:T(8,128)(2,1)} %param.24), channel_id=1, replica_groups=mesh['dp'=16,'mp'=2] {'dp'}, dimensions={0}, use_global_device_ids=true | all-gather | bytes 626688 | tf_op jit(solution)/shard_map/all_gather | solution.py:204
  59.8 39.0 %all_gather.14 = bf16[768,384]{1,0:T(8,128)(2,1)S(1)} all-gather(bf16[48,384]{1,0:T(8,128)(2,1)S(1)} %copy-done.163), channel_id=1, replica_groups=mesh['dp'=16,'mp'=2] {'dp'}, dimensions={0}, use_global_device_ids=true | all-gather | bytes 626688 | tf_op jit(solution)/shard_map/all_gather | solution.py:205
  104.8 41.2 %all_gather.12 = bf16[768,384]{1,0:T(8,128)(2,1)S(1)} all-gather(bf16[48,384]{1,0:T(8,128)(2,1)S(1)} %copy-done.164), channel_id=1, replica_groups=mesh['dp'=16,'mp'=2] {'dp'}, dimensions={0}, use_global_device_ids=true | all-gather | bytes 626688 | tf_op jit(solution)/shard_map/all_gather | solution.py:206
  160.0 39.4 %all_gather.15 = bf16[384,768]{0,1:T(8,128)(2,1)S(1)} all-gather(bf16[384,48]{0,1:T(8,128)(2,1)} %param.29), channel_id=1, replica_groups=mesh['dp'=16,'mp'=2] {'dp'}, dimensions={1}, use_global_device_ids=true | all-gather | bytes 626688 | tf_op jit(solution)/shard_map/all_gather | solution.py:207
  220.7 17.0 %all-reduce.16.cloned.1.call-done = (bf16[256,768]{1,0:T(8,128)(2,1)}, bf16[256,768]{1,0:T(8,128)(2,1)}, bf16[256,768]{1,0:T(8,128)(2,1)}, bf16[256,768]{1,0:T(8,128)(2,1)}) async-done(((bf16[256,768]{1,0:T(8,128)(2,1)}, bf16[256,768]{1,0:T(8,128)(2,1)}, bf16[256,768]{1,0:T(8,128)(2,1)}, bf16[256,768]{1,0:T(8,128)(2,1)}), (bf16[256,768]{1,0:T(8,128)(2,1)}, bf16[256,768]{1,0:T(8,128)(2,1)}, ...) | async-done | bytes 1572880 | tf_op jit(solution)/shard_map/psum | solution.py:74
  242.5 40.7 %all-gather.3.cloned.1.call-done = bf16[768,1536]{1,0:T(8,128)(2,1)} async-done(((bf16[48,1536]{1,0:T(8,128)(2,1)}), bf16[768,1536]{1,0:T(8,128)(2,1)}) %all-gather.3.cloned.1.call-update) | async-done | bytes 2359312 | tf_op jit(solution)/shard_map/all_gather | solution.py:208
  283.1 7.6 multiply_convert_fusion
  290.7 5.6 multiply_convert_fusion.1
  296.3 50.8 %all-gather.5.cloned.1.call-done = bf16[1536,768]{0,1:T(8,128)(2,1)} async-done(((bf16[1536,48]{0,1:T(8,128)(2,1)}), bf16[1536,768]{0,1:T(8,128)(2,1)}) %all-gather.5.cloned.1.call-update) | async-done | bytes 2359312 | tf_op jit(solution)/shard_map/all_gather | solution.py:209
  347.0 3.6 convolution_convert_fusion.4
  352.3 5.4 multiply_convert_fusion.2
  359.3 5.5 multiply_convert_fusion.3
  368.1 18.3 %all-reduce.14.cloned.1.call-done = (bf16[256,768]{1,0:T(8,128)(2,1)}, bf16[256,768]{1,0:T(8,128)(2,1)}, bf16[256,768]{1,0:T(8,128)(2,1)}, bf16[256,768]{1,0:T(8,128)(2,1)}) async-done(((bf16[256,768]{1,0:T(8,128)(2,1)}, bf16[256,768]{1,0:T(8,128)(2,1)}, bf16[256,768]{1,0:T(8,128)(2,1)}, bf16[256,768]{1,0:T(8,128)(2,1)}), (bf16[256,768]{1,0:T(8,128)(2,1)}, bf16[256,768]{1,0:T(8,128)(2,1)}, ...) | async-done | bytes 1572880 | tf_op jit(solution)/shard_map/psum | solution.py:85
  417.2 21.7 %all-reduce.12.cloned.1.call-done = (bf16[256,768]{1,0:T(8,128)(2,1)}, bf16[256,768]{1,0:T(8,128)(2,1)}, bf16[256,768]{1,0:T(8,128)(2,1)}, bf16[256,768]{1,0:T(8,128)(2,1)}) async-done(((bf16[256,768]{1,0:T(8,128)(2,1)}, bf16[256,768]{1,0:T(8,128)(2,1)}, bf16[256,768]{1,0:T(8,128)(2,1)}, bf16[256,768]{1,0:T(8,128)(2,1)}), (bf16[256,768]{1,0:T(8,128)(2,1)}, bf16[256,768]{1,0:T(8,128)(2,1)}, ...) | async-done | bytes 1572880 | tf_op jit(solution)/shard_map/psum | solution.py:102
  438.9 3.5 multiply_reduce_fusion
  486.5 3.1 convert_reduce_fusion.5
  537.6 3.3 add_add_fusion.1
  550.7 78.4 %all-reduce = (f32[768]{0:T(1024)}, f32[384]{0:T(512)}, f32[384]{0:T(512)}, f32[768]{0:T(1024)}, f32[768]{0:T(1024)}, /*index=5*/f32[768]{0:T(1024)}, f32[1536]{...) all-reduce(f32[768]{0:T(1024)S(1)} %add_add_fusion.19, ...), channel_id=1, replica_groups=mesh['dp'=16,'mp'=2] {'dp'}, use_global_device_ids=true, to_apply=%region_64.65 | all-reduce | flops 7680 | bytes 61440 | tf_op jit(solution)/shard_map/psum | solution.py:236
  632.2 3.6 reduce-scatter.11.cloned.1.call-done
  635.7 128.1 %reduce-scatter.9.cloned.1.call-done = f32[48,384]{1,0:T(8,128)} async-done(((f32[768,384]{1,0:T(8,128)}), f32[48,384]{1,0:T(8,128)}) %reduce-scatter.9.cloned.1.call-update) | async-done | bytes 73744 | tf_op jit(solution)/shard_map/reduce_scatter | solution.py:229
  763.8 128.1 %reduce-scatter.7.cloned.1.call-done = f32[48,384]{1,0:T(8,128)} async-done(((f32[768,384]{1,0:T(8,128)}), f32[48,384]{1,0:T(8,128)}) %reduce-scatter.7.cloned.1.call-update) | async-done | bytes 73744 | tf_op jit(solution)/shard_map/reduce_scatter | solution.py:228
  891.9 128.1 %reduce-scatter.13.cloned.1.call-done = f32[384,48]{0,1:T(8,128)} async-done(((f32[384,768]{0,1:T(8,128)}), f32[384,48]{0,1:T(8,128)}) %reduce-scatter.13.cloned.1.call-update) | async-done | bytes 73744 | tf_op jit(solution)/shard_map/reduce_scatter | solution.py:231
  1020.0 141.7 %reduce-scatter.17.cloned.1.call-done = f32[1536,48]{0,1:T(8,128)} async-done(((f32[1536,768]{0,1:T(8,128)}), f32[1536,48]{0,1:T(8,128)}) %reduce-scatter.17.cloned.1.call-update) | async-done | bytes 294928 | tf_op jit(solution)/shard_map/reduce_scatter | solution.py:233
  1161.7 142.8 %reduce-scatter.15.cloned.1.call-done = f32[48,1536]{1,0:T(8,128)} async-done(((f32[768,1536]{1,0:T(8,128)}), f32[48,1536]{1,0:T(8,128)}) %reduce-scatter.15.cloned.1.call-update) | async-done | bytes 294928 | tf_op jit(solution)/shard_map/reduce_scatter | solution.py:232
  (739 shorter events, 191.2 us)
Async XLA Ops:
  8.0 229.6 %all-reduce.16.cloned.1.call-start = ((), (), s32[]{:S(2)}) async-start(), calls=%async_computation.17 | async-start | bytes 3145728 | tf_op jit(solution)/shard_map/psum | solution.py:74
  9.7 136.3 %copy-start.148 = (pred[256]{0:T(512)(128)(4,1)}, pred[256]{0:T(512)(128)(4,1)S(1)}, u32[]{:S(2)}) copy-start(pred[256]{0:T(512)(128)(4,1)S(1)} %get-tuple-element.145) | copy-start | bytes 772
  9.7 137.4 %copy-start.135 = (pred[256]{0:T(512)(128)(4,1)}, pred[256]{0:T(512)(128)(4,1)S(1)}, u32[]{:S(2)}) copy-start(pred[256]{0:T(512)(128)(4,1)S(1)} %get-tuple-element.142) | copy-start | bytes 772
  9.7 137.8 %copy-start.128 = (pred[256]{0:T(512)(128)(4,1)}, pred[256]{0:T(512)(128)(4,1)S(1)}, u32[]{:S(2)}) copy-start(pred[256]{0:T(512)(128)(4,1)S(1)} %get-tuple-element.143) | copy-start | bytes 772
  9.7 138.3 %copy-start.144 = (pred[256]{0:T(512)(128)(4,1)}, pred[256]{0:T(512)(128)(4,1)S(1)}, u32[]{:S(2)}) copy-start(pred[256]{0:T(512)(128)(4,1)S(1)} %get-tuple-element.144) | copy-start | bytes 772
  219.4 63.8 %all-gather.3.cloned.1.call-start = ((), (), s32[]{:S(2)}) async-start(), calls=%async_computation.6 | async-start | bytes 2506752 | tf_op jit(solution)/shard_map/all_gather | solution.py:208
  220.0 127.1 %all-gather.5.cloned.1.call-start = ((), (), s32[]{:S(2)}) async-start(), calls=%async_computation.7 | async-start | bytes 2506752 | tf_op jit(solution)/shard_map/all_gather | solution.py:209
  220.6 165.8 %all-reduce.14.cloned.1.call-start = ((), (), s32[]{:S(2)}) async-start(), calls=%async_computation.16 | async-start | bytes 3145728 | tf_op jit(solution)/shard_map/psum | solution.py:85
  239.0 150.0 %copy-start.155 = (f32[256]{0:T(256)}, f32[256]{0:T(256)S(1)}, u32[]{:S(2)}) copy-start(f32[256]{0:T(256)S(1)} %broadcast_multiply_fusion.23) | copy-start | bytes 3076
  241.4 147.6 %copy-start.168 = (f32[256]{0:T(256)}, f32[256]{0:T(256)S(1)}, u32[]{:S(2)}) copy-start(f32[256]{0:T(256)S(1)} %add_rsqrt_fusion.7) | copy-start | bytes 3076
  241.5 200.9 %copy-start.161 = (f32[256]{0:T(256)}, f32[256]{0:T(256)S(1)}, u32[]{:S(2)}) copy-start(f32[256]{0:T(256)S(1)} %broadcast_multiply_fusion.21) | copy-start | bytes 3076
  241.5 144.9 %copy-start.157 = (f32[256]{0:T(256)}, f32[256]{0:T(256)S(1)}, u32[]{:S(2)}) copy-start(f32[256]{0:T(256)S(1)} %broadcast_multiply_fusion.19) | copy-start | bytes 3076
  241.5 197.3 %copy-start.165 = (f32[256]{0:T(256)}, f32[256]{0:T(256)S(1)}, u32[]{:S(2)}) copy-start(f32[256]{0:T(256)S(1)} %broadcast_multiply_fusion.17) | copy-start | bytes 3076
  242.4 199.9 %copy-start.174 = (f32[256]{0:T(256)}, f32[256]{0:T(256)S(1)}, u32[]{:S(2)}) copy-start(f32[256]{0:T(256)S(1)} %add_rsqrt_fusion.5) | copy-start | bytes 3076
  242.5 143.9 %copy-start.170 = (f32[256]{0:T(256)}, f32[256]{0:T(256)S(1)}, u32[]{:S(2)}) copy-start(f32[256]{0:T(256)S(1)} %add_rsqrt_fusion.3) | copy-start | bytes 3076
  242.5 196.4 %copy-start.176 = (f32[256]{0:T(256)}, f32[256]{0:T(256)S(1)}, u32[]{:S(2)}) copy-start(f32[256]{0:T(256)S(1)} %add_rsqrt_fusion.1) | copy-start | bytes 3076
  367.4 71.5 %all-reduce.12.cloned.1.call-start = ((), (), s32[]{:S(2)}) async-start(), calls=%async_computation.15 | async-start | bytes 3145728 | tf_op jit(solution)/shard_map/psum | solution.py:102
  416.9 129.7 %all-reduce.10.cloned.1.call-start = ((), (), s32[]{:S(2)}) async-start(), calls=%async_computation.14 | async-start | bytes 3145728 | tf_op jit(solution)/shard_map/psum | solution.py:134
  504.9 130.9 %reduce-scatter.11.cloned.1.call-start = ((), (), s32[]{:S(2)}) async-start(), calls=%async_computation.10 | async-start | bytes 1253376 | tf_op jit(solution)/shard_map/reduce_scatter | solution.py:230
  509.9 253.9 %reduce-scatter.9.cloned.1.call-start = ((), (), s32[]{:S(2)}) async-start(), calls=%async_computation.9 | async-start | bytes 1253376 | tf_op jit(solution)/shard_map/reduce_scatter | solution.py:229
  514.6 377.3 %reduce-scatter.7.cloned.1.call-start = ((), (), s32[]{:S(2)}) async-start(), calls=%async_computation.8 | async-start | bytes 1253376 | tf_op jit(solution)/shard_map/reduce_scatter | solution.py:228
  519.1 500.9 %reduce-scatter.13.cloned.1.call-start = ((), (), s32[]{:S(2)}) async-start(), calls=%async_computation.11 | async-start | bytes 1253376 | tf_op jit(solution)/shard_map/reduce_scatter | solution.py:231
  524.5 637.2 %reduce-scatter.17.cloned.1.call-start = ((), (), s32[]{:S(2)}) async-start(), calls=%async_computation.13 | async-start | bytes 5013504 | tf_op jit(solution)/shard_map/reduce_scatter | solution.py:233
  532.8 771.7 %reduce-scatter.15.cloned.1.call-start = ((), (), s32[]{:S(2)}) async-start(), calls=%async_computation.12 | async-start | bytes 5013504 | tf_op jit(solution)/shard_map/reduce_scatter | solution.py:232
  (235 other events, 1344.7 us)
Sparse Core Ops, SparseCore 0:
  219.5 18.1 all-reduce.15
  367.5 18.8 all-reduce.13
  417.1 21.7 all-reduce.11
  505.0 21.7 all-reduce.9
Sparse Core Ops, SparseCore 1:
  223.1 60.0 all-gather.2
  286.2 60.8 all-gather.4
  510.7 125.0 reduce-scatter.10
  641.1 122.7 reduce-scatter.8
  769.1 122.7 reduce-scatter.6
  897.2 122.7 reduce-scatter.12
  1025.6 136.1 reduce-scatter.16
  1168.1 136.3 reduce-scatter.14
where the time goes:
time: 1320 us; the launch traced here: 1310 us
  waiting for transfers between devices  822 us (62%)
  blocking collectives  244 us (18%)
  matrix products  141 us (11%)
  local copies, waits for them, and re-layouts  47.1 us (4%)
  other arithmetic  37.9 us (3%)
  between operations  18.7 us (1%)
    reduce_scatter x1, waiting for transfers between devices, per_device(): lax.psum_scatter(matrices[4], 'dp', scatter_dimension=0, tiled=True)  143 us
    reduce_scatter x1, waiting for transfers between devices, per_device(): lax.psum_scatter(matrices[5], 'dp', scatter_dimension=1, tiled=True)  142 us
    reduce_scatter x1, waiting for transfers between devices, per_device(): lax.psum_scatter(matrices[0], 'dp', scatter_dimension=0, tiled=True)  128 us
    reduce_scatter x1, waiting for transfers between devices, per_device(): lax.psum_scatter(matrices[3], 'dp', scatter_dimension=1, tiled=True)  128 us
    reduce_scatter x1, waiting for transfers between devices, per_device(): lax.psum_scatter(matrices[1], 'dp', scatter_dimension=0, tiled=True)  128 us
    psum x1, blocking collectives, per_device(): summed = lax.psum(vector_totals, 'dp')  78.4 us
    all_gather x1, waiting for transfers between devices, per_device(): lax.all_gather(w_down, 'dp', axis=1, tiled=True)  50.8 us
    all_gather x1, blocking collectives, per_device(): lax.all_gather(w_query, 'dp', axis=0, tiled=True)  45.9 us
  transfers between devices with their start and end apart: 12, of which 11 were waited for; matrix products, arithmetic and copies ran while one was open for 4% of the time, Pallas kernels for 0%

commit v1 on v0

v1 whole, which is shorter than its diff:
```python
import functools

import jax
import jax.numpy as jnp
from jax import lax
from jax.experimental import pallas as pl
from jax.experimental.pallas import tpu as pltpu
from jax.sharding import PartitionSpec as P

HEAD = 64
NORM_EPS = 1e-05

F32 = jnp.float32
B16 = jnp.bfloat16


def norm_back(incoming, normed, inverse, norm_gain):
    scaled = incoming * norm_gain
    inner = (
        scaled
        - jnp.mean(scaled, axis=-1, keepdims=True)
        - normed * jnp.mean(scaled * normed, axis=-1, keepdims=True)
    )
    return (inverse * inner, jnp.sum(incoming * normed, axis=0), jnp.sum(incoming, axis=0))


def layer_norm(values, norm_gain, norm_shift):
    row_mean = jnp.mean(values, axis=-1, keepdims=True)
    centred = values - row_mean
    inverse = lax.rsqrt(jnp.mean(centred * centred, axis=-1, keepdims=True) + NORM_EPS)
    normed = centred * inverse
    return (normed * norm_gain + norm_shift, normed, inverse)


def swap(values, bit, size, axis="dp"):
    return lax.ppermute(values, axis, [(i, i ^ bit) for i in range(size)])


def arrange_body(me_ref, own_ref, x_ref, y_ref, d1_ref, d2_ref, out_ref):
    me = me_ref[0]
    planes = own_ref.shape[0]
    half = planes // 2
    for k in range(planes):
        out_ref[me ^ (4 * k)] = own_ref[k]
        out_ref[me ^ (4 * k + 1)] = x_ref[k]
        out_ref[me ^ (4 * k + 2)] = y_ref[k]
        out_ref[me ^ (4 * k + 3)] = d1_ref[k] if k < half else d2_ref[k - half]


def spread_body(me_ref, in_ref, own_ref, x_ref, y_ref, d1_ref, d2_ref):
    me = me_ref[0]
    planes = own_ref.shape[0]
    half = planes // 2
    for k in range(planes):
        own_ref[k] = in_ref[me ^ (4 * k)]
        x_ref[k] = in_ref[me ^ (4 * k + 1)]
        y_ref[k] = in_ref[me ^ (4 * k + 2)]
        if k < half:
            d1_ref[k] = in_ref[me ^ (4 * k + 3)]
        else:
            d2_ref[k - half] = in_ref[me ^ (4 * k + 3)]


VMEM_SPEC = pl.BlockSpec(memory_space=pltpu.VMEM)
SMEM_SPEC = pl.BlockSpec(memory_space=pltpu.SMEM)


def gather_rows(piece, me, size):
    rows, cols = piece.shape
    planes = size // 4
    half = planes // 2
    own = jnp.stack([piece] + [swap(piece, 4 * k, size) for k in range(1, planes)])
    by_x = swap(own, 1, size)
    by_y = swap(own, 2, size)
    diag_one = swap(by_x[:half], 2, size)
    diag_two = swap(by_y[half:], 1, size)
    full = pl.pallas_call(
        arrange_body,
        out_shape=jax.ShapeDtypeStruct((size, rows, cols), piece.dtype),
        in_specs=[SMEM_SPEC] + [VMEM_SPEC] * 5,
        out_specs=VMEM_SPEC,
    )(me, own, by_x, by_y, diag_one, diag_two)
    return full.reshape(size * rows, cols)


def scatter_rows(full, me, size):
    all_rows, cols = full.shape
    rows = all_rows // size
    planes = size // 4
    half = planes // 2
    shape = functools.partial(jax.ShapeDtypeStruct, dtype=full.dtype)
    own, for_x, for_y, diag_one, diag_two = pl.pallas_call(
        spread_body,
        out_shape=[
            shape((planes, rows, cols)),
            shape((planes, rows, cols)),
            shape((planes, rows, cols)),
            shape((half, rows, cols)),
            shape((planes - half, rows, cols)),
        ],
        in_specs=[SMEM_SPEC, VMEM_SPEC],
        out_specs=[VMEM_SPEC] * 5,
    )(me, full.reshape(size, rows, cols))
    from_x = swap(diag_one, 1, size)
    from_y = swap(diag_two, 2, size)
    for_y = jnp.concatenate(
        [(for_y[:half].astype(F32) + from_x.astype(F32)).astype(B16), for_y[half:]]
    )
    for_x = jnp.concatenate(
        [for_x[:half], (for_x[half:].astype(F32) + from_y.astype(F32)).astype(B16)]
    )
    from_x = swap(for_x, 1, size)
    from_y = swap(for_y, 2, size)
    total = own.astype(F32) + from_x.astype(F32) + from_y.astype(F32)
    result = total[0]
    for k in range(1, planes):
        result = result + swap(total[k].astype(B16), 4 * k, size).astype(F32)
    return result


def sum_small(values, size):
    values = values + swap(values, 1, size)
    values = values + swap(values, 2, size)
    bit = 4
    while bit < size:
        values = values + swap(values, bit, size)
        bit *= 2
    return values


def pair_sum(partial):
    low = partial.astype(B16)
    other = lax.ppermute(low, "mp", [(0, 1), (1, 0)])
    return low.astype(F32) + other.astype(F32)


def per_device(dp_size, tokens, masked, lengths, mask_vector, w_query, b_query, w_key, w_value,
               b_value, w_out, b_out, gain_one, shift_one, w_up, b_up, w_down, b_down, gain_two,
               shift_two, grad_out):
    rows_own = w_query.shape[0]
    head_cols = w_query.shape[1]
    units = w_up.shape[1]
    fast = rows_own % 16 == 0 and dp_size % 8 == 0 and dp_size & (dp_size - 1) == 0
    me = lax.axis_index("dp").astype(jnp.int32).reshape(1)

    def gather(piece):
        if fast:
            return gather_rows(piece, me, dp_size)
        return lax.all_gather(piece, "dp", axis=0, tiled=True)

    def scatter(full):
        if fast:
            return scatter_rows(full.astype(B16), me, dp_size)
        return lax.psum_scatter(full, "dp", scatter_dimension=0, tiled=True)

    def total(values):
        if fast:
            return sum_small(values, dp_size)
        return lax.psum(values, "dp")

    (mask_vector, b_query, b_value, b_out, gain_one, shift_one, b_up, b_down, gain_two, shift_two) = (
        member.astype(F32)
        for member in (mask_vector, b_query, b_value, b_out, gain_one, shift_one, b_up, b_down,
                       gain_two, shift_two)
    )
    wa = gather(jnp.concatenate([w_query, w_key, w_value, w_out.T], axis=1))
    w_up = gather(w_up)
    w_down_t = gather(w_down.T)
    w_qkv = wa[:, : 3 * head_cols]
    w_out_t = wa[:, 3 * head_cols :]

    chain_count = lengths.shape[0]
    row_count = tokens.shape[0]
    slot_count = row_count // chain_count
    local_heads = head_cols // HEAD
    score_scale = HEAD ** (-0.5)
    dot = functools.partial(jnp.dot, preferred_element_type=F32)
    ein = functools.partial(jnp.einsum, preferred_element_type=F32)

    is_masked = (masked == 1)[:, None]
    layer_in = jnp.where(is_masked, mask_vector[None, :], tokens.astype(F32))
    in_low = layer_in.astype(B16)
    head_shape = (chain_count, slot_count, local_heads, HEAD)
    qkv_bias = jnp.concatenate([b_query, jnp.zeros_like(b_query), b_value])
    qkv = (dot(in_low, w_qkv) + qkv_bias).astype(B16)
    query_low, key_low, value_low = (part.reshape(head_shape) for part in jnp.split(qkv, 3, axis=1))
    key_valid = (jnp.arange(slot_count)[None, :] < lengths[:, None])[:, None, None, :]
    scores = ein("cqhe,ckhe->chqk", query_low, key_low) * score_scale
    scores = jnp.where(key_valid, scores, -1e30)
    row_max = jnp.max(scores, axis=-1, keepdims=True)
    exp_terms = jnp.exp(scores - row_max)
    attn_prob = exp_terms / jnp.sum(exp_terms, axis=-1, keepdims=True)
    prob_low = attn_prob.astype(B16)
    attended = ein("chqk,ckhe->cqhe", prob_low, value_low)
    attended = attended.reshape(row_count, -1).astype(B16)
    attn_sum = pair_sum(ein("nh,dh->nd", attended, w_out_t)) + b_out
    hidden, normed_one, inverse_one = layer_norm(layer_in + attn_sum, gain_one, shift_one)
    hidden_low = hidden.astype(B16)
    pre_act = dot(hidden_low, w_up) + b_up
    cdf = 0.5 * (1.0 + lax.erf(pre_act * (2.0**-0.5)))
    slope = cdf + pre_act * jnp.exp(-0.5 * pre_act * pre_act) * (0.5 / jnp.pi) ** 0.5
    act_low = (pre_act * cdf).astype(B16)
    ffn_sum = pair_sum(ein("nf,df->nd", act_low, w_down_t)) + b_down
    result, normed_two, inverse_two = layer_norm(hidden + ffn_sum, gain_two, shift_two)
    out_grad = grad_out.astype(F32)
    dz_two, d_gain_two, d_shift_two = norm_back(out_grad, normed_two, inverse_two, gain_two)
    d_b_down = jnp.sum(dz_two, axis=0)
    dz_two_low = dz_two.astype(B16)
    d_w_down_t = scatter(ein("nd,nf->df", dz_two_low, act_low))
    d_act = dot(dz_two_low, w_down_t)
    d_pre = d_act * slope
    d_b_up = jnp.sum(d_pre, axis=0)
    d_pre_low = d_pre.astype(B16)
    d_w_up = scatter(ein("nd,nf->df", hidden_low, d_pre_low))
    d_hidden = dz_two + pair_sum(ein("nf,df->nd", d_pre_low, w_up))
    dz_one, d_gain_one, d_shift_one = norm_back(d_hidden, normed_one, inverse_one, gain_one)
    d_b_out = jnp.sum(dz_one, axis=0)
    dz_one_low = dz_one.astype(B16)
    d_w_out_t = ein("nd,nh->dh", dz_one_low, attended)
    d_attended = dot(dz_one_low, w_out_t).astype(B16).reshape(head_shape)
    d_prob = ein("cqhe,ckhe->chqk", d_attended, value_low)
    d_scores = attn_prob * (d_prob - jnp.sum(attn_prob * d_prob, axis=-1, keepdims=True))
    d_scores_low = d_scores.astype(B16)
    d_query = ein("chqk,ckhe->cqhe", d_scores_low, key_low) * score_scale
    d_key = ein("chqk,cqhe->ckhe", d_scores_low, query_low) * score_scale
    d_value = ein("chqk,cqhe->ckhe", prob_low, d_attended)
    d_qkv = jnp.concatenate(
        [part.astype(B16).reshape(row_count, -1) for part in (d_query, d_key, d_value)], axis=1
    )
    d_b_qkv = jnp.sum(d_qkv.astype(F32), axis=0)
    d_w_qkv = ein("nd,nh->dh", in_low, d_qkv)
    d_wa = scatter(jnp.concatenate([d_w_qkv, d_w_out_t], axis=1))
    d_layer_in = dz_one + pair_sum(ein("nh,dh->nd", d_qkv, w_qkv))
    d_tokens = jnp.where(is_masked, 0.0, d_layer_in)
    d_mask_vector = jnp.sum(jnp.where(is_masked, d_layer_in, 0.0), axis=0)
    parts = (
        d_mask_vector,
        d_b_qkv[:head_cols],
        d_b_qkv[2 * head_cols :],
        d_b_out,
        d_gain_one,
        d_shift_one,
        d_b_up,
        d_b_down,
        d_gain_two,
        d_shift_two,
    )
    joined = total(jnp.concatenate(parts).reshape(-1, 128)).reshape(-1)
    summed = []
    start = 0
    for part in parts:
        summed.append(joined[start : start + part.shape[0]])
        start += part.shape[0]
    return (
        result.astype(B16),
        d_tokens,
        summed[0],
        d_wa[:, :head_cols],
        summed[1],
        d_wa[:, head_cols : 2 * head_cols],
        d_wa[:, 2 * head_cols : 3 * head_cols],
        summed[2],
        d_wa[:, 3 * head_cols :].T,
        summed[3],
        summed[4],
        summed[5],
        d_w_up,
        summed[6],
        d_w_down_t.T,
        summed[7],
        summed[8],
        summed[9],
    )


def solution(mesh):
    rows, flat, both = P("dp", None), P(), P("dp", "mp")
    return jax.shard_map(
        functools.partial(per_device, mesh.shape["dp"]),
        mesh=mesh,
        in_specs=(rows, P("dp"), P("dp"), flat, both, P("mp"), both, both, P("mp"), P("mp", "dp"),
                  flat, flat, flat, both, P("mp"), P("mp", "dp"), flat, flat, flat, rows),
        out_specs=(rows, rows, flat, both, P("mp"), both, both, P("mp"), P("mp", "dp"), flat, flat,
                   flat, both, P("mp"), P("mp", "dp"), flat, flat, flat),
        check_vma=False,
    )
```

time: 1320 us -> 329 us (0.25)
  waiting for transfers between devices: 822 us -> 114 us
  blocking collectives: 244 us -> 0 us
  matrix products: 141 us -> 55.5 us
  starting transfers between devices: 1.34 us -> 66 us
  Pallas kernels: 0 us -> 19.1 us
  between operations: 18.7 us -> 2.3 us
  local copies, waits for them, and re-layouts: 47.1 us -> 31.4 us
    reduce_scatter x6 -> x0, waiting for transfers between devices: 672 us -> none  [the longest x1 143 us: per_device(): lax.psum_scatter(matrices[4], 'dp', scatter_dimension=0, tiled=True)]
    all_gather x4 -> x0, blocking collectives: 165 us -> none  [the longest x1 45.9 us: per_device(): lax.all_gather(w_query, 'dp', axis=0, tiled=True)]
    ppermute x0 -> x50, waiting for transfers between devices: none -> 114 us  [the longest x46 113 us: swap(): return lax.ppermute(values, axis, [(i, i ^ bit) for i in range(size)])]
    all_gather x2 -> x0, waiting for transfers between devices: 91.4 us -> none  [the longest x1 50.8 us: per_device(): lax.all_gather(w_down, 'dp', axis=1, tiled=True)]
    dot_general x92 -> x18, matrix products: 134 us -> 55.5 us  [the longest x1 10.1 us: per_device(): d_act = dot(dz_two_low, w_down_t)]
    psum x1 -> x0, blocking collectives: 78.4 us -> none  [per_device(): summed = lax.psum(vector_totals, 'dp')]
    ppermute x0 -> x50, starting transfers between devices: none -> 66 us  [the longest x46 65.8 us: swap(): return lax.ppermute(values, axis, [(i, i ^ bit) for i in range(size)])]
    psum x4 -> x0, waiting for transfers between devices: 57 us -> none  [the longest x1 21.7 us: micro_batch(): lax.psum(hidden_part.astype(jnp.bfloat16), 'mp').astype(jnp.float32)]
  transfers between devices with their start and end apart: 12 -> 50, of which waited for: 11 -> 27; matrix products, arithmetic and copies ran while one was open for 4% -> 16% of each run, Pallas kernels for 0% -> 3%
where the time goes in v1:
time: 329 us; the launch traced here: 323 us
  waiting for transfers between devices  114 us (35%)
  starting transfers between devices  66 us (20%)
  matrix products  55.5 us (17%)
  other arithmetic  35.2 us (11%)
  local copies, waits for them, and re-layouts  31.4 us (10%)
  Pallas kernels  19.1 us (6%)
    ppermute x46, waiting for transfers between devices, swap(): return lax.ppermute(values, axis, [(i, i ^ bit) for i in range(size)])  113 us
    ppermute x46, starting transfers between devices, swap(): return lax.ppermute(values, axis, [(i, i ^ bit) for i in range(size)])  65.8 us
    unnamed x163, local copies, waits for them, and re-layouts  17.2 us
    dot_general x1, matrix products, per_device(): d_act = dot(dz_two_low, w_down_t)  10.1 us
    pallas_call x3, Pallas kernels, scatter_rows(): pl.pallas_call(spread_body, out_shape=[shape((planes, rows, cols)), shape...  9.74 us
    pallas_call x3, Pallas kernels, gather_rows(): pl.pallas_call(arrange_body, out_shape=jax.ShapeDtypeStruct((size, rows,...  9.4 us
  transfers between devices with their start and end apart: 50, of which 27 were waited for; matrix products, arithmetic and copies ran while one was open for 16% of the time, Pallas kernels for 3%

profile of v1, /device:TPU:0, one launch (start us, length us, event | category | flops | bytes accessed | tf_op | source)
XLA Modules:
  0.0 323.3 jit_solution(2867235109924761700)
XLA Ops:
  10.5 8.1 %collective-permute-done.1 = bf16[48,1536]{1,0:T(8,128)(2,1)S(1)} collective-permute-done((bf16[48,1536]{1,0:T(8,128)(2,1)S(1)}, bf16[48,1536]{1,0:T(8,128)(2,1)S(1)}, u32[]{:S(2)}, u32[]{:S(2)}) %collective-permute-start.1) | collective-permute-done | bytes 147488 | tf_op jit(solution)/shard_map/ppermute | solution.py:36
  23.7 7.7 %collective-permute-done.3.x_ref = bf16[4,48,1536]{2,1,0:T(8,128)(2,1)S(1)} collective-permute-done((bf16[4,48,1536]{2,1,0:T(8,128)(2,1)S(1)}, bf16[4,48,1536]{2,1,0:T(8,128)(2,1)S(1)}, u32[]{:S(2)}, u32[]{:S(2)}) %collective-permute-start.3) | collective-permute-done | bytes 589856 | tf_op jit(solution)/shard_map/ppermute | solution.py:36
  35.2 3.9 %collective-permute-done.5.d1_ref = bf16[2,48,1536]{2,1,0:T(8,128)(2,1)} collective-permute-done((bf16[2,48,1536]{2,1,0:T(8,128)(2,1)S(1)}, bf16[2,48,1536]{2,1,0:T(8,128)(2,1)}, u32[]{:S(2)}, u32[]{:S(2)}) %collective-permute-start.5) | collective-permute-done | bytes 294944 | tf_op jit(solution)/shard_map/ppermute | solution.py:36
  44.7 3.9 %add_convert_fusion = bf16[1024,1152]{1,0:T(8,128)(2,1)S(1)} fusion(f32[1152]{0:T(1024)S(1)} %pad_maximum_fusion.11, bf16[768,1536]{1,0:T(8,128)(2,1)} %bitcast.183, bf16[1024,768]{0,1:T(8,128)(2,1)S(1)} %copy.55, f32[768]{0:T(1024)S(1)} %convert_element_type.289, pred[1024]{0:T(1024)(128)(4,1)S(1)} %broadcast_compare_fusion), kind=kOutput, calls=%fused_computation.13 | convolution fusion | flops 1815871488 | bytes 5710336 | tf_op jit(solution)/shard_map/dot_general | solution.py:185
  61.6 3.4 %collective-permute-start.9 = (bf16[48,1536]{1,0:T(8,128)(2,1)S(1)}, bf16[48,1536]{1,0:T(8,128)(2,1)S(1)}, u32[]{:S(2)}, u32[]{:S(2)}) collective-permute-start(bf16[48,1536]{1,0:T(8,128)(2,1)S(1)} %copy-done.48), channel_id=1, source_target_pairs={{0,16},{2,18},{4,20},{6,22},{8,24},{10,26},{12,28},{14,30},{16,0},... | collective-permute-start | bytes 442376 | tf_op jit(solution)/shard_map/ppermute | solution.py:36
  68.4 7.7 %collective-permute-done.9 = bf16[48,1536]{1,0:T(8,128)(2,1)S(1)} collective-permute-done((bf16[48,1536]{1,0:T(8,128)(2,1)S(1)}, bf16[48,1536]{1,0:T(8,128)(2,1)S(1)}, u32[]{:S(2)}, u32[]{:S(2)}) %collective-permute-start.9) | collective-permute-done | bytes 147488 | tf_op jit(solution)/shard_map/ppermute | solution.py:36
  82.8 6.8 %collective-permute-done.16 = bf16[48,1536]{1,0:T(8,128)(2,1)S(1)} collective-permute-done((bf16[48,1536]{1,0:T(8,128)(2,1)S(1)}, bf16[48,1536]{1,0:T(8,128)(2,1)S(1)}, u32[]{:S(2)}, u32[]{:S(2)}) %collective-permute-start.16) | collective-permute-done | bytes 147488 | tf_op jit(solution)/shard_map/ppermute | solution.py:36
  98.9 7.6 %collective-permute-done.18.x_ref = bf16[4,48,1536]{2,1,0:T(8,128)(2,1)S(1)} collective-permute-done((bf16[4,48,1536]{2,1,0:T(8,128)(2,1)S(1)}, bf16[4,48,1536]{2,1,0:T(8,128)(2,1)S(1)}, u32[]{:S(2)}, u32[]{:S(2)}) %collective-permute-start.18) | collective-permute-done | bytes 589856 | tf_op jit(solution)/shard_map/ppermute | solution.py:36
  112.3 4.1 %collective-permute-done.13.d1_ref = bf16[2,48,1536]{2,1,0:T(8,128)(2,1)} collective-permute-done((bf16[2,48,1536]{2,1,0:T(8,128)(2,1)S(1)}, bf16[2,48,1536]{2,1,0:T(8,128)(2,1)}, u32[]{:S(2)}, u32[]{:S(2)}) %collective-permute-start.13) | collective-permute-done | bytes 294944 | tf_op jit(solution)/shard_map/ppermute | solution.py:36
  127.9 6.2 %multiply_convert_fusion = (bf16[1024,1536]{1,0:T(8,128)(2,1)S(1)}, f32[1024,1536]{1,0:T(8,128)}) fusion(f32[1536]{0:T(1024)S(1)} %convert_element_type.306, bf16[768,1536]{1,0:T(8,128)(2,1)S(1)} %bitcast.187, f32[1024,768]{0,1:T(8,128)S(1)} %get-tuple-element.107, f32[768]{0:T(1024)S(1)} %convert_element_type.304, f32[768]{0:T(1024)S(1)} %convert_element_type.303, ...), kind=kOutput, calls=%fused_computation.7 | convolution fusion | flops 2429288448 | bytes 14962688 | tf_op jit(solution)/shard_map/dot_general | solution.py:199
  134.2 3.7 %convolution_convert_fusion.6 = bf16[1024,768]{0,1:T(8,128)(2,1)} fusion(bf16[1024,1536]{1,0:T(8,128)(2,1)S(1)} %get-tuple-element.144, bf16[768,1536]{1,0:T(8,128)(2,1)S(1)} %bitcast.190), kind=kOutput, calls=%fused_computation.51 | convolution fusion | flops 2416705536 | bytes 7077888 | tf_op jit(solution)/shard_map/nf,df->nd/dot_general | solution.py:203
  147.8 4.5 %convolution_convert_fusion = bf16[768,1536]{1,0:T(8,128)(2,1)} fusion(bf16[1024,1536]{1,0:T(8,128)(2,1)S(1)} %copy-done.71, bf16[1024,768]{0,1:T(8,128)(2,1)S(1)} %copy-done.2, f32[1024,768]{0,1:T(8,128)S(1)} %get-tuple-element.105, f32[1024]{0:T(1024)S(1)} %get-tuple-element.150, f32[1024]{0:T(1024)S(1)} %get-tuple-element.151, ...), kind=kOutput, calls=%fused_computation.17 | convolution fusion | flops 2424176640 | bytes 10243072 | tf_op jit(solution)/shard_map/nd,nf->df/dot_general | solution.py:209
  152.2 3.3 %shard_map.336 = (bf16[4,48,1536]{2,1,0:T(8,128)(2,1)}, bf16[4,48,1536]{2,1,0:T(8,128)(2,1)}, bf16[4,48,1536]{2,1,0:T(8,128)(2,1)}, bf16[2,48,1536]{2,1,0:T(8,128)(2,1)}, bf16[2,48,1536]{2,1,0:T(8,128)(2,1)}) custom-call(s32[1]{0:T(128)} %bitcast.me_ref, bf16[16,48,1536]{2,1,0:T(8,128)(2,1)} %bitcast.182), custom_call_target="tpu_custom_call" | custom-call | tf_op jit(solution)/shard_map/pallas_call | solution.py:92
  157.0 10.1 %fusion.76 = (f32[1536]{0:T(1024)}, bf16[1024,1536]{1,0:T(8,128)(2,1)S(1)}) fusion(f32[1024,1536]{1,0:T(8,128)} %get-tuple-element.145, f32[1536]{0:T(1024)S(1)} %convert_element_type.306, bf16[768,1536]{1,0:T(8,128)(2,1)} %bitcast.189, f32[1024]{0:T(1024)S(1)} %get-tuple-element.150, f32[1024,768]{0,1:T(8,128)} %copy-done, ...), kind=kOutput, calls=%fused_computation.182 | convolution fusion | flops 2441869824 | bytes 16546816 | tf_op jit(solution)/shard_map/dot_general | solution.py:210
  167.1 4.2 %convolution_convert_fusion.1 = bf16[768,1536]{1,0:T(8,128)(2,1)} fusion(bf16[1024,1536]{1,0:T(8,128)(2,1)S(1)} %get-tuple-element.149, f32[1024,768]{0,1:T(8,128)S(1)} %get-tuple-element.107, f32[768]{0:T(1024)S(1)} %convert_element_type.304, f32[768]{0:T(1024)S(1)} %convert_element_type.303, f32[1024]{0:T(1024)S(1)} %add_rsqrt_fusion.1, ...), kind=kOutput, calls=%fused_computation.18 | convolution fusion | flops 2421030912 | bytes 8665088 | tf_op jit(solution)/shard_map/nd,nf->df/dot_general | solution.py:214
  171.4 3.8 %convolution_convert_fusion.5 = bf16[1024,768]{0,1:T(8,128)(2,1)} fusion(bf16[768,1536]{1,0:T(8,128)(2,1)S(1)} %bitcast.188, bf16[1024,1536]{1,0:T(8,128)(2,1)S(1)} %get-tuple-element.149), kind=kOutput, calls=%fused_computation.50 | convolution fusion | flops 2416705536 | bytes 7077888 | tf_op jit(solution)/shard_map/nf,df->nd/dot_general | solution.py:215
  192.9 11.9 %collective-permute-done.44 = bf16[4,48,1536]{2,1,0:T(8,128)(2,1)S(1)} collective-permute-done((bf16[4,48,1536]{2,1,0:T(8,128)(2,1)S(1)}, bf16[4,48,1536]{2,1,0:T(8,128)(2,1)S(1)}, u32[]{:S(2)}, u32[]{:S(2)}) %collective-permute-start.44) | collective-permute-done | bytes 589856 | tf_op jit(solution)/shard_map/ppermute | solution.py:36
  209.1 7.4 %collective-permute-done.37 = bf16[4,48,1536]{2,1,0:T(8,128)(2,1)S(1)} collective-permute-done((bf16[4,48,1536]{2,1,0:T(8,128)(2,1)S(1)}, bf16[4,48,1536]{2,1,0:T(8,128)(2,1)S(1)}, u32[]{:S(2)}, u32[]{:S(2)}) %collective-permute-start.37) | collective-permute-done | bytes 589856 | tf_op jit(solution)/shard_map/ppermute | solution.py:36
  227.5 8.3 %collective-permute-done.41 = bf16[48,1536]{1,0:T(8,128)(2,1)S(1)} collective-permute-done((bf16[48,1536]{1,0:T(8,128)(2,1)S(1)}, bf16[48,1536]{1,0:T(8,128)(2,1)S(1)}, u32[]{:S(2)}, u32[]{:S(2)}) %collective-permute-start.41) | collective-permute-done | bytes 147488 | tf_op jit(solution)/shard_map/ppermute | solution.py:36
  236.6 5.7 %fusion.12 = (f32[768]{0:T(1024)S(1)}, f32[768]{0:T(1024)S(1)}, f32[768]{0:T(1024)S(1)}, f32[768]{0:T(1024)S(1)}, f32[1024]{0:T(1024)S(1)}, /*index=5*/f32[1024]...) fusion(bf16[1024,768]{0,1:T(8,128)(2,1)S(1)} %copy-done.3, f32[1024,768]{0,1:T(8,128)S(1)} %copy-done.1, ...), kind=kLoop, calls=%fused_computation.23 | loop fusion | flops 22014208 | bytes 15785984 | tf_op jit(solution)/shard_map/reduce_sum | solution.py:24
  266.5 4.6 %convolution_convert_fusion.4 = bf16[1024,768]{0,1:T(8,128)(2,1)S(1)} fusion(bf16[1024,1152]{0,1:T(8,128)(2,1)} %copy-done.12, bf16[768,1536]{1,0:T(8,128)(2,1)} %bitcast.186), kind=kOutput, calls=%fused_computation.49 | convolution fusion | flops 1812725760 | bytes 5701632 | tf_op jit(solution)/shard_map/nh,dh->nd/dot_general | solution.py:233
  286.3 9.4 %collective-permute-done.30 = bf16[4,48,1536]{2,1,0:T(8,128)(2,1)S(1)} collective-permute-done((bf16[4,48,1536]{2,1,0:T(8,128)(2,1)S(1)}, bf16[4,48,1536]{2,1,0:T(8,128)(2,1)S(1)}, u32[]{:S(2)}, u32[]{:S(2)}) %collective-permute-start.30) | collective-permute-done | bytes 589856 | tf_op jit(solution)/shard_map/ppermute | solution.py:36
  306.6 8.2 %collective-permute-done.34 = bf16[48,1536]{1,0:T(8,128)(2,1)S(1)} collective-permute-done((bf16[48,1536]{1,0:T(8,128)(2,1)S(1)}, bf16[48,1536]{1,0:T(8,128)(2,1)S(1)}, u32[]{:S(2)}, u32[]{:S(2)}) %collective-permute-start.34) | collective-permute-done | bytes 147488 | tf_op jit(solution)/shard_map/ppermute | solution.py:36
  314.9 3.3 %collective-permute-start.28 = (f32[60,128]{1,0:T(8,128)S(1)}, f32[60,128]{1,0:T(8,128)S(1)}, u32[]{:S(2)}, u32[]{:S(2)}) collective-permute-start(f32[60,128]{1,0:T(8,128)S(1)} %add.199), channel_id=1, source_target_pairs={{0,16},{2,18},{4,20},{6,22},{8,24},{10,26},{12,28},{14,30},{16,0},... | collective-permute-start | bytes 92168 | tf_op jit(solution)/shard_map/ppermute | solution.py:36
  (353 shorter events, 173.3 us)
Async XLA Ops:
  4.7 14.0 %collective-permute-start.1 = (bf16[48,1536]{1,0:T(8,128)(2,1)S(1)}, bf16[48,1536]{1,0:T(8,128)(2,1)S(1)}, u32[]{:S(2)}, u32[]{:S(2)}) collective-permute-start(bf16[48,1536]{1,0:T(8,128)(2,1)S(1)} %get-tuple-element.132), channel_id=1, source_target_pairs={{0,16},{2,18},{4,20},{6,22},{8,24},{10,26},{12,28},{14,30},{16,0},... | collective-permute-start | bytes 442376 | tf_op jit(solution)/shard_map/ppermute | solution.py:36
  20.3 14.3 %collective-permute-start.4 = (bf16[4,48,1536]{2,1,0:T(8,128)(2,1)S(1)}, bf16[4,48,1536]{2,1,0:T(8,128)(2,1)S(1)}, u32[]{:S(2)}, u32[]{:S(2)}) collective-permute-start(bf16[4,48,1536]{2,1,0:T(8,128)(2,1)S(1)} %pad_maximum_fusion.1.own_ref), channel_id=1, source_target_pairs={{0,4},{2,6},{4,0},{6,2},{8,12},{10,14},{12,8},{14,10},{16,20},{18,... | collective-permute-start | bytes 1769480 | tf_op jit(solution)/shard_map/ppermute | solution.py:36
  61.5 61.5 %collective-permute-start.7 = (bf16[1024,768]{0,1:T(8,128)(2,1)S(1)}, bf16[1024,768]{0,1:T(8,128)(2,1)}, u32[]{:S(2)}, u32[]{:S(2)}) collective-permute-start(bf16[1024,768]{0,1:T(8,128)(2,1)S(1)} %convolution_convert_fusion.3), channel_id=1, source_target_pairs={{0,1},{1,0},{2,3},{3,2},{4,5},{5,4},{6,7},{7,6},{8,9},{9,8},{10,11... | collective-permute-start | bytes 4718600 | tf_op jit(solution)/shard_map/ppermute | solution.py:133
  61.6 14.4 %collective-permute-start.9 = (bf16[48,1536]{1,0:T(8,128)(2,1)S(1)}, bf16[48,1536]{1,0:T(8,128)(2,1)S(1)}, u32[]{:S(2)}, u32[]{:S(2)}) collective-permute-start(bf16[48,1536]{1,0:T(8,128)(2,1)S(1)} %copy-done.48), channel_id=1, source_target_pairs={{0,16},{2,18},{4,20},{6,22},{8,24},{10,26},{12,28},{14,30},{16,0},... | collective-permute-start | bytes 442376 | tf_op jit(solution)/shard_map/ppermute | solution.py:36
  66.3 15.0 %collective-permute-start.15 = (bf16[48,1536]{1,0:T(8,128)(2,1)S(1)}, bf16[48,1536]{1,0:T(8,128)(2,1)S(1)}, u32[]{:S(2)}, u32[]{:S(2)}) collective-permute-start(bf16[48,1536]{1,0:T(8,128)(2,1)S(1)} %bitcast.200), channel_id=1, source_target_pairs={{0,8},{2,10},{4,12},{6,14},{8,0},{10,2},{12,4},{14,6},{16,24},{18,... | collective-permute-start | bytes 442376 | tf_op jit(solution)/shard_map/ppermute | solution.py:36
  76.0 13.5 %collective-permute-start.16 = (bf16[48,1536]{1,0:T(8,128)(2,1)S(1)}, bf16[48,1536]{1,0:T(8,128)(2,1)S(1)}, u32[]{:S(2)}, u32[]{:S(2)}) collective-permute-start(bf16[48,1536]{1,0:T(8,128)(2,1)S(1)} %bitcast.201), channel_id=1, source_target_pairs={{0,16},{2,18},{4,20},{6,22},{8,24},{10,26},{12,28},{14,30},{16,0},... | collective-permute-start | bytes 442376 | tf_op jit(solution)/shard_map/ppermute | solution.py:36
  78.3 15.5 %collective-permute-start.11 = (bf16[4,48,1536]{2,1,0:T(8,128)(2,1)S(1)}, bf16[4,48,1536]{2,1,0:T(8,128)(2,1)S(1)}, u32[]{:S(2)}, u32[]{:S(2)}) collective-permute-start(bf16[4,48,1536]{2,1,0:T(8,128)(2,1)S(1)} %pad_maximum_fusion.2.own_ref), channel_id=1, source_target_pairs={{0,2},{2,0},{4,6},{6,4},{8,10},{10,8},{12,14},{14,12},{16,18},{18,... | collective-permute-start | bytes 1769480 | tf_op jit(solution)/shard_map/ppermute | solution.py:36
  81.3 16.0 %collective-permute-start.12 = (bf16[4,48,1536]{2,1,0:T(8,128)(2,1)S(1)}, bf16[4,48,1536]{2,1,0:T(8,128)(2,1)S(1)}, u32[]{:S(2)}, u32[]{:S(2)}) collective-permute-start(bf16[4,48,1536]{2,1,0:T(8,128)(2,1)S(1)} %pad_maximum_fusion.2.own_ref), channel_id=1, source_target_pairs={{0,4},{2,6},{4,0},{6,2},{8,12},{10,14},{12,8},{14,10},{16,20},{18,... | collective-permute-start | bytes 1769480 | tf_op jit(solution)/shard_map/ppermute | solution.py:36
  89.7 16.8 %collective-permute-start.18 = (bf16[4,48,1536]{2,1,0:T(8,128)(2,1)S(1)}, bf16[4,48,1536]{2,1,0:T(8,128)(2,1)S(1)}, u32[]{:S(2)}, u32[]{:S(2)}) collective-permute-start(bf16[4,48,1536]{2,1,0:T(8,128)(2,1)S(1)} %pad_maximum_fusion.3.own_ref), channel_id=1, source_target_pairs={{0,2},{2,0},{4,6},{6,4},{8,10},{10,8},{12,14},{14,12},{16,18},{18,... | collective-permute-start | bytes 1769480 | tf_op jit(solution)/shard_map/ppermute | solution.py:36
  91.1 18.9 %collective-permute-start.19 = (bf16[4,48,1536]{2,1,0:T(8,128)(2,1)S(1)}, bf16[4,48,1536]{2,1,0:T(8,128)(2,1)S(1)}, u32[]{:S(2)}, u32[]{:S(2)}) collective-permute-start(bf16[4,48,1536]{2,1,0:T(8,128)(2,1)S(1)} %pad_maximum_fusion.3.own_ref), channel_id=1, source_target_pairs={{0,4},{2,6},{4,0},{6,2},{8,12},{10,14},{12,8},{14,10},{16,20},{18,... | collective-permute-start | bytes 1769480 | tf_op jit(solution)/shard_map/ppermute | solution.py:36
  93.8 22.5 %collective-permute-start.13 = (bf16[2,48,1536]{2,1,0:T(8,128)(2,1)S(1)}, bf16[2,48,1536]{2,1,0:T(8,128)(2,1)}, u32[]{:S(2)}, u32[]{:S(2)}) collective-permute-start(bf16[2,48,1536]{2,1,0:T(8,128)(2,1)S(1)} %slice.245), channel_id=1, source_target_pairs={{0,4},{2,6},{4,0},{6,2},{8,12},{10,14},{12,8},{14,10},{16,20},{18,... | collective-permute-start | bytes 884744 | tf_op jit(solution)/shard_map/ppermute | solution.py:36
  97.4 19.0 %collective-permute-start.14 = (bf16[2,48,1536]{2,1,0:T(8,128)(2,1)S(1)}, bf16[2,48,1536]{2,1,0:T(8,128)(2,1)}, u32[]{:S(2)}, u32[]{:S(2)}) collective-permute-start(bf16[2,48,1536]{2,1,0:T(8,128)(2,1)S(1)} %slice.246), channel_id=1, source_target_pairs={{0,2},{2,0},{4,6},{6,4},{8,10},{10,8},{12,14},{14,12},{16,18},{18,... | collective-permute-start | bytes 884744 | tf_op jit(solution)/shard_map/ppermute | solution.py:36
  155.5 28.3 %collective-permute-start.43 = (bf16[2,48,1536]{2,1,0:T(8,128)(2,1)}, bf16[2,48,1536]{2,1,0:T(8,128)(2,1)}, u32[]{:S(2)}, u32[]{:S(2)}) collective-permute-start(bf16[2,48,1536]{2,1,0:T(8,128)(2,1)} %get-tuple-element.45), channel_id=1, source_target_pairs={{0,4},{2,6},{4,0},{6,2},{8,12},{10,14},{12,8},{14,10},{16,20},{18,... | collective-permute-start | bytes 884744 | tf_op jit(solution)/shard_map/ppermute | solution.py:36
  183.7 52.8 %collective-permute-start.23 = (bf16[1024,768]{0,1:T(8,128)(2,1)}, bf16[1024,768]{0,1:T(8,128)(2,1)S(1)}, u32[]{:S(2)}, u32[]{:S(2)}) collective-permute-start(bf16[1024,768]{0,1:T(8,128)(2,1)} %convolution_convert_fusion.5), channel_id=1, source_target_pairs={{0,1},{1,0},{2,3},{3,2},{4,5},{5,4},{6,7},{7,6},{8,9},{9,8},{10,11... | collective-permute-start | bytes 4718600 | tf_op jit(solution)/shard_map/ppermute | solution.py:133
  186.0 18.9 %collective-permute-start.44 = (bf16[4,48,1536]{2,1,0:T(8,128)(2,1)S(1)}, bf16[4,48,1536]{2,1,0:T(8,128)(2,1)S(1)}, u32[]{:S(2)}, u32[]{:S(2)}) collective-permute-start(bf16[4,48,1536]{2,1,0:T(8,128)(2,1)S(1)} %pad_maximum_fusion.8), channel_id=1, source_target_pairs={{0,2},{2,0},{4,6},{6,4},{8,10},{10,8},{12,14},{14,12},{16,18},{18,... | collective-permute-start | bytes 1769480 | tf_op jit(solution)/shard_map/ppermute | solution.py:36
  188.6 16.3 %collective-permute-start.46 = (bf16[4,48,1536]{2,1,0:T(8,128)(2,1)S(1)}, bf16[4,48,1536]{2,1,0:T(8,128)(2,1)S(1)}, u32[]{:S(2)}, u32[]{:S(2)}) collective-permute-start(bf16[4,48,1536]{2,1,0:T(8,128)(2,1)S(1)} %pad_maximum_fusion.9), channel_id=1, source_target_pairs={{0,4},{2,6},{4,0},{6,2},{8,12},{10,14},{12,8},{14,10},{16,20},{18,... | collective-permute-start | bytes 1769480 | tf_op jit(solution)/shard_map/ppermute | solution.py:36
  189.3 27.2 %collective-permute-start.37 = (bf16[4,48,1536]{2,1,0:T(8,128)(2,1)S(1)}, bf16[4,48,1536]{2,1,0:T(8,128)(2,1)S(1)}, u32[]{:S(2)}, u32[]{:S(2)}) collective-permute-start(bf16[4,48,1536]{2,1,0:T(8,128)(2,1)S(1)} %pad_maximum_fusion.6), channel_id=1, source_target_pairs={{0,2},{2,0},{4,6},{6,4},{8,10},{10,8},{12,14},{14,12},{16,18},{18,... | collective-permute-start | bytes 1769480 | tf_op jit(solution)/shard_map/ppermute | solution.py:36
  192.4 27.3 %collective-permute-start.39 = (bf16[4,48,1536]{2,1,0:T(8,128)(2,1)S(1)}, bf16[4,48,1536]{2,1,0:T(8,128)(2,1)S(1)}, u32[]{:S(2)}, u32[]{:S(2)}) collective-permute-start(bf16[4,48,1536]{2,1,0:T(8,128)(2,1)S(1)} %pad_maximum_fusion.7), channel_id=1, source_target_pairs={{0,4},{2,6},{4,0},{6,2},{8,12},{10,14},{12,8},{14,10},{16,20},{18,... | collective-permute-start | bytes 1769480 | tf_op jit(solution)/shard_map/ppermute | solution.py:36
  205.2 14.9 %collective-permute-start.47 = (bf16[48,1536]{1,0:T(8,128)(2,1)S(1)}, bf16[48,1536]{1,0:T(8,128)(2,1)S(1)}, u32[]{:S(2)}, u32[]{:S(2)}) collective-permute-start(bf16[48,1536]{1,0:T(8,128)(2,1)S(1)} %get-tuple-element.118), channel_id=1, source_target_pairs={{0,8},{2,10},{4,12},{6,14},{8,0},{10,2},{12,4},{14,6},{16,24},{18,... | collective-permute-start | bytes 442376 | tf_op jit(solution)/shard_map/ppermute | solution.py:36
  206.4 14.9 %collective-permute-start.48 = (bf16[48,1536]{1,0:T(8,128)(2,1)S(1)}, bf16[48,1536]{1,0:T(8,128)(2,1)S(1)}, u32[]{:S(2)}, u32[]{:S(2)}) collective-permute-start(bf16[48,1536]{1,0:T(8,128)(2,1)S(1)} %get-tuple-element.120), channel_id=1, source_target_pairs={{0,16},{2,18},{4,20},{6,22},{8,24},{10,26},{12,28},{14,30},{16,0},... | collective-permute-start | bytes 442376 | tf_op jit(solution)/shard_map/ppermute | solution.py:36
  220.1 15.6 %collective-permute-start.41 = (bf16[48,1536]{1,0:T(8,128)(2,1)S(1)}, bf16[48,1536]{1,0:T(8,128)(2,1)S(1)}, u32[]{:S(2)}, u32[]{:S(2)}) collective-permute-start(bf16[48,1536]{1,0:T(8,128)(2,1)S(1)} %get-tuple-element.123), channel_id=1, source_target_pairs={{0,16},{2,18},{4,20},{6,22},{8,24},{10,26},{12,28},{14,30},{16,0},... | collective-permute-start | bytes 442376 | tf_op jit(solution)/shard_map/ppermute | solution.py:36
  221.3 14.5 %collective-permute-start.42 = (bf16[48,1536]{1,0:T(8,128)(2,1)S(1)}, bf16[48,1536]{1,0:T(8,128)(2,1)S(1)}, u32[]{:S(2)}, u32[]{:S(2)}) collective-permute-start(bf16[48,1536]{1,0:T(8,128)(2,1)S(1)} %get-tuple-element.122), channel_id=1, source_target_pairs={{0,24},{2,26},{4,28},{6,30},{8,16},{10,18},{12,20},{14,22},{16,8},... | collective-permute-start | bytes 442376 | tf_op jit(solution)/shard_map/ppermute | solution.py:36
  279.6 16.1 %collective-permute-start.30 = (bf16[4,48,1536]{2,1,0:T(8,128)(2,1)S(1)}, bf16[4,48,1536]{2,1,0:T(8,128)(2,1)S(1)}, u32[]{:S(2)}, u32[]{:S(2)}) collective-permute-start(bf16[4,48,1536]{2,1,0:T(8,128)(2,1)S(1)} %pad_maximum_fusion.4), channel_id=1, source_target_pairs={{0,2},{2,0},{4,6},{6,4},{8,10},{10,8},{12,14},{14,12},{16,18},{18,... | collective-permute-start | bytes 1769480 | tf_op jit(solution)/shard_map/ppermute | solution.py:36
  281.5 15.5 %collective-permute-start.32 = (bf16[4,48,1536]{2,1,0:T(8,128)(2,1)S(1)}, bf16[4,48,1536]{2,1,0:T(8,128)(2,1)S(1)}, u32[]{:S(2)}, u32[]{:S(2)}) collective-permute-start(bf16[4,48,1536]{2,1,0:T(8,128)(2,1)S(1)} %pad_maximum_fusion.5), channel_id=1, source_target_pairs={{0,4},{2,6},{4,0},{6,2},{8,12},{10,14},{12,8},{14,10},{16,20},{18,... | collective-permute-start | bytes 1769480 | tf_op jit(solution)/shard_map/ppermute | solution.py:36
  (98 other events, 1266.0 us)

commit v2 on v1

--- a/solution.py
+++ b/solution.py
@@ -65,31 +65,24 @@
 SMEM_SPEC = pl.BlockSpec(memory_space=pltpu.SMEM)
 
 
-def gather_rows(piece, me, size):
-    rows, cols = piece.shape
-    planes = size // 4
-    half = planes // 2
-    own = jnp.stack([piece] + [swap(piece, 4 * k, size) for k in range(1, planes)])
-    by_x = swap(own, 1, size)
-    by_y = swap(own, 2, size)
-    diag_one = swap(by_x[:half], 2, size)
-    diag_two = swap(by_y[half:], 1, size)
+def arrange(me, own, by_x, by_y, diag_one, diag_two):
+    planes, rows, cols = own.shape
     full = pl.pallas_call(
         arrange_body,
-        out_shape=jax.ShapeDtypeStruct((size, rows, cols), piece.dtype),
+        out_shape=jax.ShapeDtypeStruct((4 * planes, rows, cols), own.dtype),
         in_specs=[SMEM_SPEC] + [VMEM_SPEC] * 5,
         out_specs=VMEM_SPEC,
     )(me, own, by_x, by_y, diag_one, diag_two)
-    return full.reshape(size * rows, cols)
-
-
-def scatter_rows(full, me, size):
+    return full.reshape(4 * planes * rows, cols)
+
+
+def spread(me, full, size):
     all_rows, cols = full.shape
     rows = all_rows // size
     planes = size // 4
     half = planes // 2
     shape = functools.partial(jax.ShapeDtypeStruct, dtype=full.dtype)
-    own, for_x, for_y, diag_one, diag_two = pl.pallas_call(
+    return pl.pallas_call(
         spread_body,
         out_shape=[
             shape((planes, rows, cols)),
@@ -101,21 +94,53 @@
         in_specs=[SMEM_SPEC, VMEM_SPEC],
         out_specs=[VMEM_SPEC] * 5,
     )(me, full.reshape(size, rows, cols))
-    from_x = swap(diag_one, 1, size)
-    from_y = swap(diag_two, 2, size)
+
+
+def along_z(piece, size):
+    return jnp.stack([piece] + [swap(piece, 4 * k, size) for k in range(1, size // 4)])
+
+
+def plane_one(own, size):
+    return swap(own, 1, size), swap(own, 2, size)
+
+
+def plane_two(by_x, by_y, size):
+    half = by_x.shape[0] // 2
+    return swap(by_x[:half], 2, size), swap(by_y[half:], 1, size)
+
+
+def fold_one(diag_one, diag_two, size):
+    return swap(diag_one, 1, size), swap(diag_two, 2, size)
+
+
+def fold_two(for_x, for_y, from_x, from_y, size):
+    half = from_x.shape[0]
     for_y = jnp.concatenate(
         [(for_y[:half].astype(F32) + from_x.astype(F32)).astype(B16), for_y[half:]]
     )
     for_x = jnp.concatenate(
         [for_x[:half], (for_x[half:].astype(F32) + from_y.astype(F32)).astype(B16)]
     )
-    from_x = swap(for_x, 1, size)
-    from_y = swap(for_y, 2, size)
-    total = own.astype(F32) + from_x.astype(F32) + from_y.astype(F32)
+    return swap(for_x, 1, size), swap(for_y, 2, size)
+
+
+def fold_total(own, from_x, from_y):
+    return own.astype(F32) + from_x.astype(F32) + from_y.astype(F32)
+
+
+def fold_z(total, size):
+    return [swap(total[k].astype(B16), 4 * k, size) for k in range(1, total.shape[0])]
+
+
+def fold_sum(total, received):
     result = total[0]
-    for k in range(1, planes):
-        result = result + swap(total[k].astype(B16), 4 * k, size).astype(F32)
+    for piece in received:
+        result = result + piece.astype(F32)
     return result
+
+
+def tie(*values):
+    return lax.optimization_barrier(values)
 
 
 def sum_small(values, size):
@@ -143,16 +168,6 @@
     fast = rows_own % 16 == 0 and dp_size % 8 == 0 and dp_size & (dp_size - 1) == 0
     me = lax.axis_index("dp").astype(jnp.int32).reshape(1)
 
-    def gather(piece):
-        if fast:
-            return gather_rows(piece, me, dp_size)
-        return lax.all_gather(piece, "dp", axis=0, tiled=True)
-
-    def scatter(full):
-        if fast:
-            return scatter_rows(full.astype(B16), me, dp_size)
-        return lax.psum_scatter(full, "dp", scatter_dimension=0, tiled=True)
-
     def total(values):
         if fast:
             return sum_small(values, dp_size)
@@ -163,9 +178,24 @@
         for member in (mask_vector, b_query, b_value, b_out, gain_one, shift_one, b_up, b_down,
                        gain_two, shift_two)
     )
-    wa = gather(jnp.concatenate([w_query, w_key, w_value, w_out.T], axis=1))
-    w_up = gather(w_up)
-    w_down_t = gather(w_down.T)
+    piece_a = jnp.concatenate([w_query, w_key, w_value, w_out.T], axis=1)
+    piece_c = w_up
+    piece_d = w_down.T
+    if fast:
+        own_a = along_z(piece_a, dp_size)
+        own_a, piece_c = tie(own_a, piece_c)
+        near_a = plane_one(own_a, dp_size)
+        own_c = along_z(piece_c, dp_size)
+        own_a, near_a, own_c, piece_d = tie(own_a, near_a, own_c, piece_d)
+        far_a = plane_two(*near_a, dp_size)
+        near_c = plane_one(own_c, dp_size)
+        own_d = along_z(piece_d, dp_size)
+        own_a, near_a, far_a, own_c, near_c, own_d = tie(own_a, near_a, far_a, own_c, near_c, own_d)
+        wa = arrange(me, own_a, *near_a, *far_a)
+    else:
+        wa, w_up, w_down_t = (
+            lax.all_gather(piece, "dp", axis=0, tiled=True) for piece in (piece_a, piece_c, piece_d)
+        )
     w_qkv = wa[:, : 3 * head_cols]
     w_out_t = wa[:, 3 * head_cols :]
 
@@ -193,29 +223,56 @@
     prob_low = attn_prob.astype(B16)
     attended = ein("chqk,ckhe->cqhe", prob_low, value_low)
     attended = attended.reshape(row_count, -1).astype(B16)
-    attn_sum = pair_sum(ein("nh,dh->nd", attended, w_out_t)) + b_out
+    attn_part = ein("nh,dh->nd", attended, w_out_t).astype(B16)
+    if fast:
+        far_c = plane_two(*near_c, dp_size)
+        near_d = plane_one(own_d, dp_size)
+        attn_part, far_c, near_d, own_c, near_c, own_d = tie(
+            attn_part, far_c, near_d, own_c, near_c, own_d
+        )
+        far_d = plane_two(*near_d, dp_size)
+        w_up = arrange(me, own_c, *near_c, *far_c)
+    attn_sum = pair_sum(attn_part) + b_out
     hidden, normed_one, inverse_one = layer_norm(layer_in + attn_sum, gain_one, shift_one)
     hidden_low = hidden.astype(B16)
     pre_act = dot(hidden_low, w_up) + b_up
     cdf = 0.5 * (1.0 + lax.erf(pre_act * (2.0**-0.5)))
     slope = cdf + pre_act * jnp.exp(-0.5 * pre_act * pre_act) * (0.5 / jnp.pi) ** 0.5
     act_low = (pre_act * cdf).astype(B16)
+    if fast:
+        act_low, far_d, near_d, own_d = tie(act_low, far_d, near_d, own_d)
+        w_down_t = arrange(me, own_d, *near_d, *far_d)
     ffn_sum = pair_sum(ein("nf,df->nd", act_low, w_down_t)) + b_down
     result, normed_two, inverse_two = layer_norm(hidden + ffn_sum, gain_two, shift_two)
     out_grad = grad_out.astype(F32)
     dz_two, d_gain_two, d_shift_two = norm_back(out_grad, normed_two, inverse_two, gain_two)
     d_b_down = jnp.sum(dz_two, axis=0)
     dz_two_low = dz_two.astype(B16)
-    d_w_down_t = scatter(ein("nd,nf->df", dz_two_low, act_low))
+    d_w_down_t = ein("nd,nf->df", dz_two_low, act_low)
+    if fast:
+        own_d, for_x_d, for_y_d, *far_d = spread(me, d_w_down_t.astype(B16), dp_size)
+        far_d, own_d, for_x_d, for_y_d, dz_two_low = tie(far_d, own_d, for_x_d, for_y_d, dz_two_low)
+        far_d = fold_one(*far_d, dp_size)
     d_act = dot(dz_two_low, w_down_t)
     d_pre = d_act * slope
     d_b_up = jnp.sum(d_pre, axis=0)
     d_pre_low = d_pre.astype(B16)
-    d_w_up = scatter(ein("nd,nf->df", hidden_low, d_pre_low))
-    d_hidden = dz_two + pair_sum(ein("nf,df->nd", d_pre_low, w_up))
+    d_w_up = ein("nd,nf->df", hidden_low, d_pre_low)
+    hidden_part = ein("nf,df->nd", d_pre_low, w_up).astype(B16)
+    if fast:
+        far_d, d_w_up, hidden_part = tie(far_d, d_w_up, hidden_part)
+        near_d = fold_two(for_x_d, for_y_d, *far_d, dp_size)
+        own_c, for_x_c, for_y_c, *far_c = spread(me, d_w_up.astype(B16), dp_size)
+        far_c = fold_one(*far_c, dp_size)
+    d_hidden = dz_two + pair_sum(hidden_part)
     dz_one, d_gain_one, d_shift_one = norm_back(d_hidden, normed_one, inverse_one, gain_one)
     d_b_out = jnp.sum(dz_one, axis=0)
     dz_one_low = dz_one.astype(B16)
+    if fast:
+        near_d, far_c, for_x_c, for_y_c, dz_one_low = tie(near_d, far_c, for_x_c, for_y_c, dz_one_low)
+        total_d = fold_total(own_d, *near_d)
+        z_d = fold_z(total_d, dp_size)
+        near_c = fold_two(for_x_c, for_y_c, *far_c, dp_size)
     d_w_out_t = ein("nd,nh->dh", dz_one_low, attended)
     d_attended = dot(dz_one_low, w_out_t).astype(B16).reshape(head_shape)
     d_prob = ein("cqhe,ckhe->chqk", d_attended, value_low)
@@ -229,7 +286,25 @@
     )
     d_b_qkv = jnp.sum(d_qkv.astype(F32), axis=0)
     d_w_qkv = ein("nd,nh->dh", in_low, d_qkv)
-    d_wa = scatter(jnp.concatenate([d_w_qkv, d_w_out_t], axis=1))
+    d_wa = jnp.concatenate([d_w_qkv, d_w_out_t], axis=1)
+    if fast:
+        d_wa, z_d, near_c = tie(d_wa, z_d, near_c)
+        own_a, for_x_a, for_y_a, *far_a = spread(me, d_wa.astype(B16), dp_size)
+        total_c = fold_total(own_c, *near_c)
+        far_a = fold_one(*far_a, dp_size)
+        z_c = fold_z(total_c, dp_size)
+        far_a, for_x_a, for_y_a, z_c = tie(far_a, for_x_a, for_y_a, z_c)
+        near_a = fold_two(for_x_a, for_y_a, *far_a, dp_size)
+        total_a = fold_total(own_a, *near_a)
+        z_a = fold_z(total_a, dp_size)
+        d_wa = fold_sum(total_a, z_a)
+        d_w_up = fold_sum(total_c, z_c)
+        d_w_down_t = fold_sum(total_d, z_d)
+    else:
+        d_wa, d_w_up, d_w_down_t = (
+            lax.psum_scatter(full, "dp", scatter_dimension=0, tiled=True)
+            for full in (d_wa, d_w_up, d_w_down_t)
+        )
     d_layer_in = dz_one + pair_sum(ein("nh,dh->nd", d_qkv, w_qkv))
     d_tokens = jnp.where(is_masked, 0.0, d_layer_in)
     d_mask_vector = jnp.sum(jnp.where(is_masked, d_layer_in, 0.0), axis=0)

time: 329 us -> 295 us (0.90); the launches traced: 323 us -> 296 us
  waiting for transfers between devices: 114 us -> 83.1 us
  matrix products: 55.5 us -> 65 us
  local copies, waits for them, and re-layouts: 31.4 us -> 24.8 us
  other arithmetic: 35.2 us -> 40.5 us
  starting transfers between devices: 66 us -> 61.1 us
    ppermute x46, waiting for transfers between devices: 113 us -> 79.8 us  [swap(): return lax.ppermute(values, axis, [(i, i ^ bit) for i in range(size)])]
    dot_general x1, matrix products: 10.1 us -> 20.3 us  [per_device(): d_act = dot(dz_two_low, w_down_t)]
    unnamed x163 -> x139, local copies, waits for them, and re-layouts: 17.2 us -> 9.29 us
    ppermute x46, starting transfers between devices: 65.8 us -> 60.9 us  [swap(): return lax.ppermute(values, axis, [(i, i ^ bit) for i in range(size)])]
    slice x12, local copies, waits for them, and re-layouts: 5.17 us -> 9.28 us  [the longest x6 5.88 us: plane_two(): return (swap(by_x[:half], 2, size), swap(by_y[half:], 1, size))]
    another operation x7, other arithmetic: 1.84 us -> 5.88 us  [the longest x4 3.9 us: along_z(): jnp.stack([piece] + [swap(piece, 4 * k, size) for k in range(1, size // 4)])]
    reduce_sum x1 -> x2, other arithmetic: 5.67 us -> 6.89 us  [norm_back(): jnp.sum(incoming * normed, axis=0)]
  transfers between devices with their start and end apart: 50 -> 50, of which waited for: 27 -> 22; matrix products, arithmetic and copies ran while one was open for 16% -> 21% of each run, Pallas kernels for 3% -> 4%
where the time goes in v2:
time: 295 us; the launch traced here: 296 us
  waiting for transfers between devices  83.1 us (28%)
  matrix products  65 us (22%)
  starting transfers between devices  61.1 us (21%)
  other arithmetic  40.5 us (14%)
  local copies, waits for them, and re-layouts  24.8 us (8%)
  Pallas kernels  19 us (6%)
    ppermute x46, waiting for transfers between devices, swap(): return lax.ppermute(values, axis, [(i, i ^ bit) for i in range(size)])  79.8 us
    ppermute x46, starting transfers between devices, swap(): return lax.ppermute(values, axis, [(i, i ^ bit) for i in range(size)])  60.9 us
    dot_general x1, matrix products, per_device(): d_act = dot(dz_two_low, w_down_t)  20.3 us
    pallas_call x3, Pallas kernels, spread(): pl.pallas_call(spread_body, out_shape=[shape((planes, rows, cols)), shape...  9.64 us
    pallas_call x3, Pallas kernels, arrange(): pl.pallas_call(arrange_body, out_shape=jax.ShapeDtypeStruct((4 * planes,...  9.41 us
    unnamed x139, local copies, waits for them, and re-layouts  9.29 us
    reduce_sum x2, other arithmetic, norm_back(): jnp.sum(incoming * normed, axis=0)  6.89 us
  transfers between devices with their start and end apart: 50, of which 22 were waited for; matrix products, arithmetic and copies ran while one was open for 21% of the time, Pallas kernels for 4%

profile of v2, /device:TPU:0, one launch (start us, length us, event | category | flops | bytes accessed | tf_op | source)
XLA Modules:
  0.0 295.7 jit_solution(837659988896383480)
XLA Ops:
  7.2 3.3 %collective-permute-done = bf16[48,1536]{1,0:T(8,128)(2,1)S(1)} collective-permute-done((bf16[48,1536]{1,0:T(8,128)(2,1)S(1)}, bf16[48,1536]{1,0:T(8,128)(2,1)S(1)}, u32[]{:S(2)}, u32[]{:S(2)}) %collective-permute-start) | collective-permute-done | bytes 147488 | tf_op jit(solution)/shard_map/ppermute | solution.py:36
  10.5 8.1 %collective-permute-done.1 = bf16[48,1536]{1,0:T(8,128)(2,1)S(1)} collective-permute-done((bf16[48,1536]{1,0:T(8,128)(2,1)S(1)}, bf16[48,1536]{1,0:T(8,128)(2,1)S(1)}, u32[]{:S(2)}, u32[]{:S(2)}) %collective-permute-start.1) | collective-permute-done | bytes 147488 | tf_op jit(solution)/shard_map/ppermute | solution.py:36
  28.8 7.9 %collective-permute-done.6 = bf16[48,1536]{1,0:T(8,128)(2,1)S(1)} collective-permute-done((bf16[48,1536]{1,0:T(8,128)(2,1)}, bf16[48,1536]{1,0:T(8,128)(2,1)S(1)}, u32[]{:S(2)}, u32[]{:S(2)}) %collective-permute-start.6) | collective-permute-done | bytes 147488 | tf_op jit(solution)/shard_map/ppermute | solution.py:36
  49.5 5.3 %collective-permute-done.13 = bf16[48,1536]{1,0:T(8,128)(2,1)} collective-permute-done((bf16[48,1536]{1,0:T(8,128)(2,1)}, bf16[48,1536]{1,0:T(8,128)(2,1)}, u32[]{:S(2)}, u32[]{:S(2)}) %collective-permute-start.13) | collective-permute-done | bytes 147488 | tf_op jit(solution)/shard_map/ppermute | solution.py:36
  58.3 6.8 %collective-permute-done.9.d2_ref = bf16[2,48,1536]{2,1,0:T(8,128)(2,1)} collective-permute-done((bf16[2,48,1536]{2,1,0:T(8,128)(2,1)}, bf16[2,48,1536]{2,1,0:T(8,128)(2,1)}, u32[]{:S(2)}, u32[]{:S(2)}) %collective-permute-start.9) | collective-permute-done | bytes 294944 | tf_op jit(solution)/shard_map/ppermute | solution.py:36
  71.3 3.8 %add_convert_fusion = bf16[1024,1152]{1,0:T(8,128)(2,1)S(1)} fusion(f32[1152]{0:T(1024)S(1)} %pad_maximum_fusion.11, bf16[768,1536]{1,0:T(8,128)(2,1)} %bitcast.179, bf16[1024,768]{1,0:T(8,128)(2,1)S(1)} %copy-done.16, f32[768]{0:T(1024)S(1)} %convert_element_type.288, pred[1024]{0:T(1024)(128)(4,1)S(1)} %broadcast_compare_fusion), kind=kOutput, calls=%fused_computation.14 | convolution fusion | flops 1815871488 | bytes 5710336 | tf_op jit(solution)/shard_map/dot_general | solution.py:215
  99.1 3.3 %fusion.74 = (f32[1024]{0:T(1024)S(1)}, f32[1024,768]{1,0:T(8,128)S(1)}) fusion(f32[768]{0:T(1024)S(1)} %convert_element_type.301, bf16[1024,768]{1,0:T(8,128)(2,1)} %collective-permute-done.19, bf16[1024,768]{1,0:T(8,128)(2,1)} %copy-done.18, bf16[1024,768]{1,0:T(8,128)(2,1)} %param.20, f32[768]{0:T(1024)S(1)} %convert_element_type.288, ...), kind=kLoop, calls=%fused_computation.177 | loop fusion | flops 6290432 | bytes 7875584 | tf_op jit(solution)/shard_map/reduce_sum | solution.py:28
  104.1 5.6 %multiply_convert_fusion = (bf16[1024,1536]{1,0:T(8,128)(2,1)}, f32[1024,1536]{1,0:T(8,128)}) fusion(f32[1536]{0:T(1024)S(1)} %convert_element_type.305, bf16[768,1536]{1,0:T(8,128)(2,1)S(1)} %bitcast.183, f32[1024,768]{1,0:T(8,128)S(1)} %get-tuple-element.194, f32[768]{0:T(1024)S(1)} %convert_element_type.303, f32[768]{0:T(1024)S(1)} %convert_element_type.302, ...), kind=kOutput, calls=%fused_computation.7 | convolution fusion | flops 2429288448 | bytes 14962688 | tf_op jit(solution)/shard_map/dot_general | solution.py:238
  113.5 5.3 %convolution_convert_fusion.4 = bf16[1024,768]{1,0:T(8,128)(2,1)S(1)} fusion(bf16[1024,1536]{1,0:T(8,128)(2,1)} %get-tuple-element.119, bf16[768,1536]{1,0:T(8,128)(2,1)} %bitcast.185), kind=kOutput, calls=%fused_computation.49 | convolution fusion | flops 2416705536 | bytes 7077888 | tf_op jit(solution)/shard_map/nf,df->nd/dot_general | solution.py:245
  118.9 3.3 %collective-permute-done.22 = bf16[1024,768]{1,0:T(8,128)(2,1)S(1)} collective-permute-done((bf16[1024,768]{1,0:T(8,128)(2,1)S(1)}, bf16[1024,768]{1,0:T(8,128)(2,1)S(1)}, u32[]{:S(2)}, u32[]{:S(2)}) %collective-permute-start.22) | collective-permute-done | bytes 1572896 | tf_op jit(solution)/shard_map/ppermute | solution.py:158
  132.6 4.0 %convolution_convert_fusion = bf16[768,1536]{1,0:T(8,128)(2,1)} fusion(bf16[1024,768]{1,0:T(8,128)(2,1)S(1)} %convert_element_type.315, bf16[1024,1536]{1,0:T(8,128)(2,1)S(1)} %copy-done.61), kind=kOutput, calls=%fused_computation.18 | convolution fusion | flops 2417098752 | bytes 7077888 | tf_op jit(solution)/shard_map/nd,nf->df/dot_general | solution.py:251
  139.8 20.3 %fusion.77 = (f32[1536]{0:T(1024)}, bf16[1024,1536]{1,0:T(8,128)(2,1)S(1)}) fusion(f32[1024,1536]{1,0:T(8,128)} %get-tuple-element.227, f32[1536]{0:T(1024)S(1)} %convert_element_type.305, bf16[1024,768]{1,0:T(8,128)(2,1)} %copy-done.19, bf16[768,1536]{1,0:T(8,128)(2,1)} %bitcast.186), kind=kOutput, calls=%fused_computation.180 | convolution fusion | flops 2434791936 | bytes 13381632 | tf_op jit(solution)/shard_map/dot_general | solution.py:256
  160.1 4.2 %fusion.17 = bf16[768,1536]{1,0:T(8,128)(2,1)} fusion(bf16[1024,1536]{1,0:T(8,128)(2,1)S(1)} %get-tuple-element.231, f32[1024,768]{1,0:T(8,128)S(1)} %get-tuple-element.194, f32[768]{0:T(1024)S(1)} %convert_element_type.303, f32[768]{0:T(1024)S(1)} %convert_element_type.302, f32[1024]{0:T(1024)S(1)} %add_rsqrt_fusion.1, f32[1024]{0:T(1024)S(1)} %broadcast_multiply_fusion.5), kind=kOutput, calls=%fused_computation.53 | convolution fusion | flops 2419851264 | bytes 8665088 | tf_op jit(solution)/shard_map/nd,nf->df/dot_general | solution.py:260
  166.3 3.7 %convolution_convert_fusion.3 = bf16[1024,768]{1,0:T(8,128)(2,1)} fusion(bf16[768,1536]{1,0:T(8,128)(2,1)S(1)} %bitcast.184, bf16[1024,1536]{1,0:T(8,128)(2,1)S(1)} %get-tuple-element.231), kind=kOutput, calls=%fused_computation.48 | convolution fusion | flops 2416705536 | bytes 7077888 | tf_op jit(solution)/shard_map/nf,df->nd/dot_general | solution.py:261
  170.0 3.3 %collective-permute-done.23 = bf16[2,48,1536]{2,1,0:T(8,128)(2,1)S(1)} collective-permute-done((bf16[2,48,1536]{2,1,0:T(8,128)(2,1)S(1)}, bf16[2,48,1536]{2,1,0:T(8,128)(2,1)S(1)}, u32[]{:S(2)}, u32[]{:S(2)}) %collective-permute-start.23) | collective-permute-done | bytes 294944 | tf_op jit(solution)/shard_map/ppermute | solution.py:36
  186.8 4.6 %multiply_reduce_fusion = (f32[768]{0:T(1024)}, f32[1024]{0:T(1024)S(1)}, f32[1024]{0:T(1024)S(1)}, f32[768]{0:T(1024)S(1)}, f32[1024,768]{1,0:T(8,128)S(1)}) fusion(f32[1024,768]{1,0:T(8,128)S(1)} %get-tuple-element.194, f32[1024]{0:T(1024)S(1)} %add_rsqrt_fusion.1, f32[1024]{0:T(1024)S(1)} %broadcast_multiply_fusion.5, f32[768]{0:T(1024)S(1)} %convert_element_type.302, ...), kind=kLoop, calls=%fused_computation.23 | loop fusion | flops 10220032 | bytes 12608512 | tf_op jit(solution)/shard_map/reduce_sum | solution.py:24
  193.6 8.4 %collective-permute-done.28 = bf16[2,48,1536]{2,1,0:T(8,128)(2,1)S(1)} collective-permute-done((bf16[2,48,1536]{2,1,0:T(8,128)(2,1)}, bf16[2,48,1536]{2,1,0:T(8,128)(2,1)S(1)}, u32[]{:S(2)}, u32[]{:S(2)}) %collective-permute-start.28) | collective-permute-done | bytes 294944 | tf_op jit(solution)/shard_map/ppermute | solution.py:36
  217.2 3.4 %convolution_convert_fusion.2 = bf16[1024,768]{1,0:T(8,128)(2,1)} fusion(bf16[1024,1152]{0,1:T(8,128)(2,1)S(1)} %bitcast_dynamic-update-slice_fusion, bf16[768,1536]{1,0:T(8,128)(2,1)S(1)} %bitcast.182), kind=kOutput, calls=%fused_computation.47 | convolution fusion | flops 1812725760 | bytes 5701632 | tf_op jit(solution)/shard_map/nh,dh->nd/dot_general | solution.py:308
  226.6 4.3 %collective-permute-start.37 = (bf16[48,1536]{1,0:T(8,128)(2,1)S(1)}, bf16[48,1536]{1,0:T(8,128)(2,1)S(1)}, u32[]{:S(2)}, u32[]{:S(2)}) collective-permute-start(bf16[48,1536]{1,0:T(8,128)(2,1)S(1)} %get-tuple-element.206), channel_id=1, source_target_pairs={{0,24},{2,26},{4,28},{6,30},{8,16},{10,18},{12,20},{14,22},{16,8},... | collective-permute-start | bytes 442376 | tf_op jit(solution)/shard_map/ppermute | solution.py:36
  233.6 6.0 %collective-permute-done.36 = bf16[48,1536]{1,0:T(8,128)(2,1)S(1)} collective-permute-done((bf16[48,1536]{1,0:T(8,128)(2,1)S(1)}, bf16[48,1536]{1,0:T(8,128)(2,1)S(1)}, u32[]{:S(2)}, u32[]{:S(2)}) %collective-permute-start.36) | collective-permute-done | bytes 147488 | tf_op jit(solution)/shard_map/ppermute | solution.py:36
  251.6 3.3 %collective-permute-done.43 = bf16[48,1536]{1,0:T(8,128)(2,1)S(1)} collective-permute-done((bf16[48,1536]{1,0:T(8,128)(2,1)S(1)}, bf16[48,1536]{1,0:T(8,128)(2,1)S(1)}, u32[]{:S(2)}, u32[]{:S(2)}) %collective-permute-start.43) | collective-permute-done | bytes 147488 | tf_op jit(solution)/shard_map/ppermute | solution.py:36
  265.6 6.3 %collective-permute-done.45 = bf16[4,48,1536]{2,1,0:T(8,128)(2,1)S(1)} collective-permute-done((bf16[4,48,1536]{2,1,0:T(8,128)(2,1)S(1)}, bf16[4,48,1536]{2,1,0:T(8,128)(2,1)S(1)}, u32[]{:S(2)}, u32[]{:S(2)}) %collective-permute-start.45) | collective-permute-done | bytes 589856 | tf_op jit(solution)/shard_map/ppermute | solution.py:36
  280.5 3.3 %collective-permute-done.47 = bf16[48,1536]{1,0:T(8,128)(2,1)S(1)} collective-permute-done((bf16[48,1536]{1,0:T(8,128)(2,1)S(1)}, bf16[48,1536]{1,0:T(8,128)(2,1)S(1)}, u32[]{:S(2)}, u32[]{:S(2)}) %collective-permute-start.47) | collective-permute-done | bytes 147488 | tf_op jit(solution)/shard_map/ppermute | solution.py:36
  283.8 4.7 %collective-permute-done.48 = bf16[48,1536]{1,0:T(8,128)(2,1)S(1)} collective-permute-done((bf16[48,1536]{1,0:T(8,128)(2,1)S(1)}, bf16[48,1536]{1,0:T(8,128)(2,1)S(1)}, u32[]{:S(2)}, u32[]{:S(2)}) %collective-permute-start.48) | collective-permute-done | bytes 147488 | tf_op jit(solution)/shard_map/ppermute | solution.py:36
  (331 shorter events, 161.0 us)
Async XLA Ops:
  4.7 14.0 %collective-permute-start.1 = (bf16[48,1536]{1,0:T(8,128)(2,1)S(1)}, bf16[48,1536]{1,0:T(8,128)(2,1)S(1)}, u32[]{:S(2)}, u32[]{:S(2)}) collective-permute-start(bf16[48,1536]{1,0:T(8,128)(2,1)S(1)} %get-tuple-element.214), channel_id=1, source_target_pairs={{0,16},{2,18},{4,20},{6,22},{8,24},{10,26},{12,28},{14,30},{16,0},... | collective-permute-start | bytes 442376 | tf_op jit(solution)/shard_map/ppermute | solution.py:36
  18.7 19.0 %collective-permute-start.3 = (bf16[4,48,1536]{2,1,0:T(8,128)(2,1)S(1)}, bf16[4,48,1536]{2,1,0:T(8,128)(2,1)S(1)}, u32[]{:S(2)}, u32[]{:S(2)}) collective-permute-start(bf16[4,48,1536]{2,1,0:T(8,128)(2,1)S(1)} %pad_maximum_fusion.1.own_ref), channel_id=1, source_target_pairs={{0,2},{2,0},{4,6},{6,4},{8,10},{10,8},{12,14},{14,12},{16,18},{18,... | collective-permute-start | bytes 1769480 | tf_op jit(solution)/shard_map/ppermute | solution.py:36
  20.3 17.5 %collective-permute-start.4 = (bf16[4,48,1536]{2,1,0:T(8,128)(2,1)S(1)}, bf16[4,48,1536]{2,1,0:T(8,128)(2,1)S(1)}, u32[]{:S(2)}, u32[]{:S(2)}) collective-permute-start(bf16[4,48,1536]{2,1,0:T(8,128)(2,1)S(1)} %pad_maximum_fusion.1.own_ref), channel_id=1, source_target_pairs={{0,4},{2,6},{4,0},{6,2},{8,12},{10,14},{12,8},{14,10},{16,20},{18,... | collective-permute-start | bytes 1769480 | tf_op jit(solution)/shard_map/ppermute | solution.py:36
  24.1 12.6 %collective-permute-start.6 = (bf16[48,1536]{1,0:T(8,128)(2,1)}, bf16[48,1536]{1,0:T(8,128)(2,1)S(1)}, u32[]{:S(2)}, u32[]{:S(2)}) collective-permute-start(bf16[48,1536]{1,0:T(8,128)(2,1)} %param.33), channel_id=1, source_target_pairs={{0,16},{2,18},{4,20},{6,22},{8,24},{10,26},{12,28},{14,30},{16,0},... | collective-permute-start | bytes 442376 | tf_op jit(solution)/shard_map/ppermute | solution.py:36
  37.8 27.3 %collective-permute-start.10 = (bf16[4,48,1536]{2,1,0:T(8,128)(2,1)S(1)}, bf16[4,48,1536]{2,1,0:T(8,128)(2,1)S(1)}, u32[]{:S(2)}, u32[]{:S(2)}) collective-permute-start(bf16[4,48,1536]{2,1,0:T(8,128)(2,1)S(1)} %pad_maximum_fusion.2.own_ref), channel_id=1, source_target_pairs={{0,2},{2,0},{4,6},{6,4},{8,10},{10,8},{12,14},{14,12},{16,18},{18,... | collective-permute-start | bytes 1769480 | tf_op jit(solution)/shard_map/ppermute | solution.py:36
  38.4 26.7 %collective-permute-start.11 = (bf16[4,48,1536]{2,1,0:T(8,128)(2,1)S(1)}, bf16[4,48,1536]{2,1,0:T(8,128)(2,1)}, u32[]{:S(2)}, u32[]{:S(2)}) collective-permute-start(bf16[4,48,1536]{2,1,0:T(8,128)(2,1)S(1)} %pad_maximum_fusion.2.own_ref), channel_id=1, source_target_pairs={{0,4},{2,6},{4,0},{6,2},{8,12},{10,14},{12,8},{14,10},{16,20},{18,... | collective-permute-start | bytes 1769480 | tf_op jit(solution)/shard_map/ppermute | solution.py:36
  41.7 13.1 %collective-permute-start.13 = (bf16[48,1536]{1,0:T(8,128)(2,1)}, bf16[48,1536]{1,0:T(8,128)(2,1)}, u32[]{:S(2)}, u32[]{:S(2)}) collective-permute-start(bf16[48,1536]{1,0:T(8,128)(2,1)} %bitcast.195), channel_id=1, source_target_pairs={{0,16},{2,18},{4,20},{6,22},{8,24},{10,26},{12,28},{14,30},{16,0},... | collective-permute-start | bytes 442376 | tf_op jit(solution)/shard_map/ppermute | solution.py:36
  43.0 13.4 %collective-permute-start.14 = (bf16[48,1536]{1,0:T(8,128)(2,1)}, bf16[48,1536]{1,0:T(8,128)(2,1)}, u32[]{:S(2)}, u32[]{:S(2)}) collective-permute-start(bf16[48,1536]{1,0:T(8,128)(2,1)} %bitcast.196), channel_id=1, source_target_pairs={{0,24},{2,26},{4,28},{6,30},{8,16},{10,18},{12,20},{14,22},{16,8},... | collective-permute-start | bytes 442376 | tf_op jit(solution)/shard_map/ppermute | solution.py:36
  65.1 25.2 %collective-permute-start.17 = (bf16[4,48,1536]{2,1,0:T(8,128)(2,1)}, bf16[4,48,1536]{2,1,0:T(8,128)(2,1)}, u32[]{:S(2)}, u32[]{:S(2)}) collective-permute-start(bf16[4,48,1536]{2,1,0:T(8,128)(2,1)} %pad_maximum_fusion.3.own_ref), channel_id=1, source_target_pairs={{0,2},{2,0},{4,6},{6,4},{8,10},{10,8},{12,14},{14,12},{16,18},{18,... | collective-permute-start | bytes 1769480 | tf_op jit(solution)/shard_map/ppermute | solution.py:36
  66.6 23.7 %collective-permute-start.18 = (bf16[4,48,1536]{2,1,0:T(8,128)(2,1)}, bf16[4,48,1536]{2,1,0:T(8,128)(2,1)}, u32[]{:S(2)}, u32[]{:S(2)}) collective-permute-start(bf16[4,48,1536]{2,1,0:T(8,128)(2,1)} %pad_maximum_fusion.3.own_ref), channel_id=1, source_target_pairs={{0,4},{2,6},{4,0},{6,2},{8,12},{10,14},{12,8},{14,10},{16,20},{18,... | collective-permute-start | bytes 1769480 | tf_op jit(solution)/shard_map/ppermute | solution.py:36
  92.2 17.5 %collective-permute-start.20 = (bf16[2,48,1536]{2,1,0:T(8,128)(2,1)}, bf16[2,48,1536]{2,1,0:T(8,128)(2,1)S(1)}, u32[]{:S(2)}, u32[]{:S(2)}) collective-permute-start(bf16[2,48,1536]{2,1,0:T(8,128)(2,1)} %slice.189), channel_id=1, source_target_pairs={{0,4},{2,6},{4,0},{6,2},{8,12},{10,14},{12,8},{14,10},{16,20},{18,... | collective-permute-start | bytes 884744 | tf_op jit(solution)/shard_map/ppermute | solution.py:36
  95.4 14.3 %collective-permute-start.21 = (bf16[2,48,1536]{2,1,0:T(8,128)(2,1)}, bf16[2,48,1536]{2,1,0:T(8,128)(2,1)}, u32[]{:S(2)}, u32[]{:S(2)}) collective-permute-start(bf16[2,48,1536]{2,1,0:T(8,128)(2,1)} %slice.190), channel_id=1, source_target_pairs={{0,2},{2,0},{4,6},{6,4},{8,10},{10,8},{12,14},{14,12},{16,18},{18,... | collective-permute-start | bytes 884744 | tf_op jit(solution)/shard_map/ppermute | solution.py:36
  174.5 12.3 %collective-permute-start.25 = (bf16[1024,768]{1,0:T(8,128)(2,1)}, bf16[1024,768]{1,0:T(8,128)(2,1)}, u32[]{:S(2)}, u32[]{:S(2)}) collective-permute-start(bf16[1024,768]{1,0:T(8,128)(2,1)} %convolution_convert_fusion.3), channel_id=1, source_target_pairs={{0,1},{1,0},{2,3},{3,2},{4,5},{5,4},{6,7},{7,6},{8,9},{9,8},{10,11... | collective-permute-start | bytes 4718600 | tf_op jit(solution)/shard_map/ppermute | solution.py:158
  178.6 23.5 %collective-permute-start.27 = (bf16[4,48,1536]{2,1,0:T(8,128)(2,1)}, bf16[4,48,1536]{2,1,0:T(8,128)(2,1)}, u32[]{:S(2)}, u32[]{:S(2)}) collective-permute-start(bf16[4,48,1536]{2,1,0:T(8,128)(2,1)} %pad_maximum_fusion.5), channel_id=1, source_target_pairs={{0,4},{2,6},{4,0},{6,2},{8,12},{10,14},{12,8},{14,10},{16,20},{18,... | collective-permute-start | bytes 1769480 | tf_op jit(solution)/shard_map/ppermute | solution.py:36
  180.0 22.0 %collective-permute-start.26 = (bf16[4,48,1536]{2,1,0:T(8,128)(2,1)}, bf16[4,48,1536]{2,1,0:T(8,128)(2,1)}, u32[]{:S(2)}, u32[]{:S(2)}) collective-permute-start(bf16[4,48,1536]{2,1,0:T(8,128)(2,1)} %pad_maximum_fusion.4), channel_id=1, source_target_pairs={{0,2},{2,0},{4,6},{6,4},{8,10},{10,8},{12,14},{14,12},{16,18},{18,... | collective-permute-start | bytes 1769480 | tf_op jit(solution)/shard_map/ppermute | solution.py:36
  184.2 17.8 %collective-permute-start.28 = (bf16[2,48,1536]{2,1,0:T(8,128)(2,1)}, bf16[2,48,1536]{2,1,0:T(8,128)(2,1)S(1)}, u32[]{:S(2)}, u32[]{:S(2)}) collective-permute-start(bf16[2,48,1536]{2,1,0:T(8,128)(2,1)} %get-tuple-element.139), channel_id=1, source_target_pairs={{0,2},{2,0},{4,6},{6,4},{8,10},{10,8},{12,14},{14,12},{16,18},{18,... | collective-permute-start | bytes 884744 | tf_op jit(solution)/shard_map/ppermute | solution.py:36
  185.3 16.8 %collective-permute-start.29 = (bf16[2,48,1536]{2,1,0:T(8,128)(2,1)}, bf16[2,48,1536]{2,1,0:T(8,128)(2,1)S(1)}, u32[]{:S(2)}, u32[]{:S(2)}) collective-permute-start(bf16[2,48,1536]{2,1,0:T(8,128)(2,1)} %get-tuple-element.140), channel_id=1, source_target_pairs={{0,4},{2,6},{4,0},{6,2},{8,12},{10,14},{12,8},{14,10},{16,20},{18,... | collective-permute-start | bytes 884744 | tf_op jit(solution)/shard_map/ppermute | solution.py:36
  220.8 18.8 %collective-permute-start.39 = (bf16[4,48,1536]{2,1,0:T(8,128)(2,1)S(1)}, bf16[4,48,1536]{2,1,0:T(8,128)(2,1)S(1)}, u32[]{:S(2)}, u32[]{:S(2)}) collective-permute-start(bf16[4,48,1536]{2,1,0:T(8,128)(2,1)S(1)} %pad_maximum_fusion.7), channel_id=1, source_target_pairs={{0,4},{2,6},{4,0},{6,2},{8,12},{10,14},{12,8},{14,10},{16,20},{18,... | collective-permute-start | bytes 1769480 | tf_op jit(solution)/shard_map/ppermute | solution.py:36
  222.6 17.1 %collective-permute-start.38 = (bf16[4,48,1536]{2,1,0:T(8,128)(2,1)S(1)}, bf16[4,48,1536]{2,1,0:T(8,128)(2,1)S(1)}, u32[]{:S(2)}, u32[]{:S(2)}) collective-permute-start(bf16[4,48,1536]{2,1,0:T(8,128)(2,1)S(1)} %pad_maximum_fusion.6), channel_id=1, source_target_pairs={{0,2},{2,0},{4,6},{6,4},{8,10},{10,8},{12,14},{14,12},{16,18},{18,... | collective-permute-start | bytes 1769480 | tf_op jit(solution)/shard_map/ppermute | solution.py:36
  226.5 13.2 %collective-permute-start.36 = (bf16[48,1536]{1,0:T(8,128)(2,1)S(1)}, bf16[48,1536]{1,0:T(8,128)(2,1)S(1)}, u32[]{:S(2)}, u32[]{:S(2)}) collective-permute-start(bf16[48,1536]{1,0:T(8,128)(2,1)S(1)} %get-tuple-element.207), channel_id=1, source_target_pairs={{0,16},{2,18},{4,20},{6,22},{8,24},{10,26},{12,28},{14,30},{16,0},... | collective-permute-start | bytes 442376 | tf_op jit(solution)/shard_map/ppermute | solution.py:36
  226.6 13.1 %collective-permute-start.37 = (bf16[48,1536]{1,0:T(8,128)(2,1)S(1)}, bf16[48,1536]{1,0:T(8,128)(2,1)S(1)}, u32[]{:S(2)}, u32[]{:S(2)}) collective-permute-start(bf16[48,1536]{1,0:T(8,128)(2,1)S(1)} %get-tuple-element.206), channel_id=1, source_target_pairs={{0,24},{2,26},{4,28},{6,30},{8,16},{10,18},{12,20},{14,22},{16,8},... | collective-permute-start | bytes 442376 | tf_op jit(solution)/shard_map/ppermute | solution.py:36
  242.5 12.4 %collective-permute-start.43 = (bf16[48,1536]{1,0:T(8,128)(2,1)S(1)}, bf16[48,1536]{1,0:T(8,128)(2,1)S(1)}, u32[]{:S(2)}, u32[]{:S(2)}) collective-permute-start(bf16[48,1536]{1,0:T(8,128)(2,1)S(1)} %get-tuple-element.204), channel_id=1, source_target_pairs={{0,16},{2,18},{4,20},{6,22},{8,24},{10,26},{12,28},{14,30},{16,0},... | collective-permute-start | bytes 442376 | tf_op jit(solution)/shard_map/ppermute | solution.py:36
  259.2 12.8 %collective-permute-start.45 = (bf16[4,48,1536]{2,1,0:T(8,128)(2,1)S(1)}, bf16[4,48,1536]{2,1,0:T(8,128)(2,1)S(1)}, u32[]{:S(2)}, u32[]{:S(2)}) collective-permute-start(bf16[4,48,1536]{2,1,0:T(8,128)(2,1)S(1)} %pad_maximum_fusion.8), channel_id=1, source_target_pairs={{0,2},{2,0},{4,6},{6,4},{8,10},{10,8},{12,14},{14,12},{16,18},{18,... | collective-permute-start | bytes 1769480 | tf_op jit(solution)/shard_map/ppermute | solution.py:36
  260.4 12.5 %collective-permute-start.46 = (bf16[4,48,1536]{2,1,0:T(8,128)(2,1)S(1)}, bf16[4,48,1536]{2,1,0:T(8,128)(2,1)S(1)}, u32[]{:S(2)}, u32[]{:S(2)}) collective-permute-start(bf16[4,48,1536]{2,1,0:T(8,128)(2,1)S(1)} %pad_maximum_fusion.9), channel_id=1, source_target_pairs={{0,4},{2,6},{4,0},{6,2},{8,12},{10,14},{12,8},{14,10},{16,20},{18,... | collective-permute-start | bytes 1769480 | tf_op jit(solution)/shard_map/ppermute | solution.py:36
  (88 other events, 890.9 us)

commit v3 on v1

v3 whole, which is shorter than its diff:
```python
import functools

import jax
import jax.numpy as jnp
from jax import lax
from jax.experimental import pallas as pl
from jax.experimental.pallas import tpu as pltpu
from jax.sharding import PartitionSpec as P

HEAD = 64
NORM_EPS = 1e-05
F32 = jnp.float32
B16 = jnp.bfloat16
MIB = 1 << 20

BLOCKS = 16
NEAR = (0, 12)
MID = (4, 8)


def swap(values, bit):
    return lax.ppermute(values, "dp", [(i, i ^ bit) for i in range(BLOCKS)])


def tie(*values):
    return lax.optimization_barrier(values)


def pair_swap(partial):
    return lax.ppermute(partial, "mp", [(0, 1), (1, 0)])


def as_pieces(full):
    rows = full.shape[0] // BLOCKS
    blocks = full.reshape(BLOCKS, rows, full.shape[1])
    return [
        jnp.stack([blocks[offset + bits[0]], blocks[offset + bits[1]]])
        for offset in range(4)
        for bits in (NEAR, MID)
    ]


SMEM_SPEC = pl.BlockSpec(memory_space=pltpu.SMEM)


def whole(shape):
    zeros = (0,) * len(shape)
    return pl.BlockSpec(tuple(shape), lambda i: zeros)


def rows_of(count, width):
    return pl.BlockSpec((count, width), lambda i: (i, 0))


def fill(me, pieces, full_ref):
    rows = pieces[0].shape[1]
    for index, piece in enumerate(pieces):
        bits = (NEAR, MID)[index % 2]
        for k in range(2):
            block = me ^ (index // 2 + bits[k])
            full_ref[pl.ds(pl.multiple_of(block * rows, rows), rows), :] = piece[k]


def dot(left, right):
    return jnp.dot(left, right, preferred_element_type=F32)


def dot_t(left, right):
    return lax.dot_general(left, right, (((1,), (1,)), ((), ())), preferred_element_type=F32)


def t_dot(left, right):
    return lax.dot_general(left, right, (((0,), (0,)), ((), ())), preferred_element_type=F32)


def row_mean(values):
    return jnp.mean(values, axis=-1, keepdims=True)


def normalize(values):
    centred = values - row_mean(values)
    inverse = lax.rsqrt(row_mean(centred * centred) + NORM_EPS)
    return centred * inverse, inverse


def col_sum(values):
    return jnp.sum(values, axis=0, keepdims=True)


def norm_back(scaled, normed, inverse):
    return inverse * (scaled - row_mean(scaled) - normed * row_mean(scaled * normed))


def two_heads(slots):
    row = lax.broadcasted_iota(jnp.int32, (2 * slots, 2 * HEAD), 0) // slots
    lane = lax.broadcasted_iota(jnp.int32, (2 * slots, 2 * HEAD), 1) // HEAD
    return (row == lane).astype(F32).astype(B16)


def doubled(values, mask):
    return jnp.concatenate([values, values], axis=0) * mask


def attend_body(chains, slots, me_ref, len_ref, in_ref, bias_ref, *rest):
    pieces, (w_ref, qkv_ref, prob_ref, att_ref, part_ref) = rest[:8], rest[8:]
    step = pl.program_id(0)
    width = att_ref.shape[1]

    @pl.when(step == 0)
    def _():
        fill(me_ref[0], pieces, w_ref)

    qkv_ref[...] = (dot(in_ref[...], w_ref[:, : 3 * width]) + bias_ref[...]).astype(B16)
    mask = two_heads(slots)
    key_slot = lax.broadcasted_iota(jnp.int32, (slots, slots), 1)
    for chain in range(chains):
        valid = key_slot < len_ref[step * chains + chain]
        rows = pl.ds(chain * slots, slots)
        for pair in range(width // (2 * HEAD)):
            lanes = 2 * HEAD * pair
            query = qkv_ref[rows, lanes : lanes + 2 * HEAD]
            key = qkv_ref[rows, width + lanes : width + lanes + 2 * HEAD]
            value = qkv_ref[rows, 2 * width + lanes : 2 * width + lanes + 2 * HEAD]
            scores = dot_t(query * (HEAD**-0.5), doubled(key, mask))
            probs = []
            for head in range(2):
                part = jnp.where(valid, scores[:, head * slots : (head + 1) * slots], -1e30)
                terms = jnp.exp(part - jnp.max(part, axis=-1, keepdims=True))
                probs.append((terms / jnp.sum(terms, axis=-1, keepdims=True)).astype(B16))
            prob = jnp.concatenate(probs, axis=1)
            prob_ref[rows, 2 * slots * pair : 2 * slots * (pair + 1)] = prob
            att_ref[rows, lanes : lanes + 2 * HEAD] = dot(prob, doubled(value, mask)).astype(B16)
    part_ref[...] = dot_t(att_ref[...], w_ref[:, 3 * width :]).astype(B16)


def attend(me, lengths, in_low, bias, pieces):
    count, width = in_low.shape
    heads = bias.shape[1] // 3
    chains = 2 if lengths.shape[0] % 2 == 0 else 1
    slots = count // lengths.shape[0]
    rows = chains * slots
    shape = jax.ShapeDtypeStruct
    return pl.pallas_call(
        functools.partial(attend_body, chains, slots),
        grid=(count // rows,),
        in_specs=[SMEM_SPEC, SMEM_SPEC, rows_of(rows, width), whole(bias.shape)]
        + [whole(piece.shape) for piece in pieces],
        out_specs=[
            whole((width, 4 * heads)),
            rows_of(rows, 3 * heads),
            rows_of(rows, heads // HEAD * slots),
            rows_of(rows, heads),
            rows_of(rows, width),
        ],
        out_shape=[
            shape((width, 4 * heads), B16),
            shape((count, 3 * heads), B16),
            shape((count, heads // HEAD * slots), B16),
            shape((count, heads), B16),
            shape((count, width), B16),
        ],
        compiler_params=pltpu.CompilerParams(vmem_limit_bytes=32 * MIB),
        cost_estimate=pl.CostEstimate(
            flops=2 * count * width * 4 * heads, bytes_accessed=12 * MIB, transcendentals=0
        ),
        name="attend",
    )(me, lengths, in_low, bias, *pieces)


def up_body(me_ref, in_ref, own_ref, other_ref, vec_ref, bias_ref, *rest):
    pieces, (w_ref, normed_ref, inverse_ref, low_ref, act_ref, slope_ref) = rest[:8], rest[8:]

    @pl.when(pl.program_id(0) == 0)
    def _():
        fill(me_ref[0], pieces, w_ref)

    vectors = vec_ref[...]
    attn = own_ref[...].astype(F32) + other_ref[...].astype(F32) + vectors[0:1]
    normed, inverse = normalize(in_ref[...].astype(F32) + attn)
    normed_ref[...] = normed
    inverse_ref[...] = jnp.broadcast_to(inverse, inverse_ref.shape)
    hidden = normed * vectors[1:2] + vectors[2:3]
    low_ref[...] = hidden.astype(B16)
    pre = dot(low_ref[...], w_ref[...]) + bias_ref[...]
    cdf = 0.5 + 0.5 * lax.erf(pre * (2.0**-0.5))
    act_ref[...] = (pre * cdf).astype(B16)
    density = jnp.exp(pre * pre * -0.5) * 0.3989422804014327
    slope_ref[...] = (cdf + pre * density).astype(B16)


def up(me, in_low, own, other, vectors, bias, pieces):
    count, width = in_low.shape
    units = bias.shape[1]
    rows = count // 4
    shape = jax.ShapeDtypeStruct
    return pl.pallas_call(
        up_body,
        grid=(4,),
        in_specs=[SMEM_SPEC]
        + [rows_of(rows, width)] * 3
        + [whole(vectors.shape), whole(bias.shape)]
        + [whole(piece.shape) for piece in pieces],
        out_specs=[
            whole((width, units)),
            rows_of(rows, width),
            rows_of(rows, 128),
            rows_of(rows, width),
            rows_of(rows, units),
            rows_of(rows, units),
        ],
        out_shape=[
            shape((width, units), B16),
            shape((count, width), F32),
            shape((count, 128), F32),
            shape((count, width), B16),
            shape((count, units), B16),
            shape((count, units), B16),
        ],
        compiler_params=pltpu.CompilerParams(vmem_limit_bytes=40 * MIB),
        cost_estimate=pl.CostEstimate(
            flops=2 * count * width * units, bytes_accessed=20 * MIB, transcendentals=0
        ),
        name="up",
    )(me, in_low, own, other, vectors, bias, *pieces)


def down_body(me_ref, act_ref, *rest):
    pieces, (w_ref, part_ref) = rest[:8], rest[8:]

    @pl.when(pl.program_id(0) == 0)
    def _():
        fill(me_ref[0], pieces, w_ref)

    part_ref[...] = dot_t(act_ref[...], w_ref[...]).astype(B16)


def down(me, act, pieces):
    count, units = act.shape
    width = BLOCKS * pieces[0].shape[1]
    rows = count // 4
    shape = jax.ShapeDtypeStruct
    return pl.pallas_call(
        down_body,
        grid=(4,),
        in_specs=[SMEM_SPEC, rows_of(rows, units)] + [whole(piece.shape) for piece in pieces],
        out_specs=[whole((width, units)), rows_of(rows, width)],
        out_shape=[shape((width, units), B16), shape((count, width), B16)],
        compiler_params=pltpu.CompilerParams(vmem_limit_bytes=24 * MIB),
        cost_estimate=pl.CostEstimate(
            flops=2 * count * width * units, bytes_accessed=8 * MIB, transcendentals=0
        ),
        name="down",
    )(me, act, *pieces)


def second_norm_body(normed_ref, own_ref, other_ref, grad_ref, vec_ref, out_ref, dz_ref, low_ref, sum_ref):
    vectors = vec_ref[...]
    hidden = normed_ref[...] * vectors[0:1] + vectors[1:2]
    ffn = own_ref[...].astype(F32) + other_ref[...].astype(F32) + vectors[2:3]
    normed, inverse = normalize(hidden + ffn)
    out_ref[...] = (normed * vectors[3:4] + vectors[4:5]).astype(B16)
    grad = grad_ref[...].astype(F32)
    dz = norm_back(grad * vectors[3:4], normed, inverse)
    dz_ref[...] = dz
    low_ref[...] = dz.astype(B16)

    @pl.when(pl.program_id(0) == 0)
    def _():
        sum_ref[...] = jnp.zeros_like(sum_ref)

    sum_ref[0:1] += col_sum(grad * normed)
    sum_ref[1:2] += col_sum(grad)
    sum_ref[2:3] += col_sum(dz)


def second_norm(normed, own, other, grad, vectors):
    count, width = own.shape
    rows = count // 4
    shape = jax.ShapeDtypeStruct
    return pl.pallas_call(
        second_norm_body,
        grid=(4,),
        in_specs=[rows_of(rows, width)] * 4 + [whole(vectors.shape)],
        out_specs=[rows_of(rows, width)] * 3 + [whole((8, width))],
        out_shape=[
            shape((count, width), B16),
            shape((count, width), F32),
            shape((count, width), B16),
            shape((8, width), F32),
        ],
        compiler_params=pltpu.CompilerParams(vmem_limit_bytes=24 * MIB),
        cost_estimate=pl.CostEstimate(flops=40 * count * width, bytes_accessed=14 * MIB, transcendentals=0),
        name="second_norm",
    )(normed, own, other, grad, vectors)


def weight_grad_body(me_ref, lefts, right_ref, outs, turned_ref, full_ref):
    x_ref, y_ref, x_late_ref, y_late_ref, own_ref = outs
    step = pl.program_id(0)
    rows = own_ref.shape[1]
    first = 0
    for left_ref, tiles in lefts:

        @pl.when(step == first)
        def _(left_ref=left_ref):
            turned_ref[...] = left_ref[...].T

        first += tiles
    full_ref[...] = dot(turned_ref[...], right_ref[...]).astype(B16)

    def block(offset):
        at = me_ref[0] ^ offset
        return full_ref[pl.ds(pl.multiple_of(at * rows, rows), rows), :]

    for k in range(2):
        x_ref[k] = block(3 + NEAR[k])
        x_ref[2 + k] = block(1 + NEAR[k])
        x_late_ref[k] = block(1 + MID[k])
        y_ref[k] = block(3 + MID[k])
        y_ref[2 + k] = block(2 + MID[k])
        y_late_ref[k] = block(2 + NEAR[k])
        own_ref[k] = block(NEAR[k])
        own_ref[2 + k] = block(MID[k])


def weight_grad(me, lefts, rights):
    count, width = lefts[0].shape
    tile = 384 if all(right.shape[1] % 384 == 0 for right in rights) else 128
    tiles = [right.shape[1] // tile for right in rights]
    total = sum(tiles)
    rows = width // BLOCKS
    firsts = [sum(tiles[:k]) for k in range(len(tiles))]
    shape = jax.ShapeDtypeStruct

    def body(me_ref, *refs):
        n = len(lefts)
        left_refs, right_refs, outs = refs[:n], refs[n : 2 * n], refs[2 * n : 2 * n + 5]
        turned_ref, full_ref = refs[2 * n + 5 :]
        if n == 1:
            weight_grad_body(me_ref, [(left_refs[0], total)], right_refs[0], outs, turned_ref, full_ref)
            return
        step = pl.program_id(0)
        for k in range(n):

            @pl.when(jnp.logical_and(step >= firsts[k], step < firsts[k] + tiles[k]))
            def _(k=k):
                @pl.when(step == firsts[k])
                def _():
                    turned_ref[...] = left_refs[k][...].T

                weight_grad_body(me_ref, [], right_refs[k], outs, turned_ref, full_ref)

    def tile_of(first, number):
        return lambda i: (0, jnp.clip(i - first, 0, number - 1))

    def out_spec(number):
        return pl.BlockSpec((number, rows, tile), lambda i: (0, 0, i))

    sizes = (4, 4, 2, 2, 4)
    return pl.pallas_call(
        body,
        grid=(total,),
        in_specs=[SMEM_SPEC]
        + [whole(left.shape) for left in lefts]
        + [pl.BlockSpec((count, tile), tile_of(firsts[k], tiles[k])) for k in range(len(rights))],
        out_specs=[out_spec(number) for number in sizes],
        out_shape=[shape((number, rows, total * tile), B16) for number in sizes],
        scratch_shapes=[pltpu.VMEM((width, count), B16), pltpu.VMEM((width, tile), B16)],
        compiler_params=pltpu.CompilerParams(vmem_limit_bytes=28 * MIB),
        cost_estimate=pl.CostEstimate(
            flops=2 * count * width * total * tile, bytes_accessed=9 * MIB, transcendentals=0
        ),
        name="weight_grad",
    )(me, *lefts, *rights)


def hidden_back_body(low_ref, slope_ref, down_ref, up_ref, pre_ref, part_ref, sum_ref):
    d_pre = dot(low_ref[...], down_ref[...]) * slope_ref[...].astype(F32)

    @pl.when(pl.program_id(0) == 0)
    def _():
        sum_ref[...] = jnp.zeros_like(sum_ref)

    sum_ref[0:1] += col_sum(d_pre)
    pre_ref[...] = d_pre.astype(B16)
    part_ref[...] = dot_t(pre_ref[...], up_ref[...]).astype(B16)


def hidden_back(dz_low, slope, w_down_t, w_up):
    count, width = dz_low.shape
    units = slope.shape[1]
    rows = count // 4
    shape = jax.ShapeDtypeStruct
    return pl.pallas_call(
        hidden_back_body,
        grid=(4,),
        in_specs=[
            rows_of(rows, width),
            rows_of(rows, units),
            whole((width, units)),
            whole((width, units)),
        ],
        out_specs=[rows_of(rows, units), rows_of(rows, width), whole((8, units))],
        out_shape=[
            shape((count, units), B16),
            shape((count, width), B16),
            shape((8, units), F32),
        ],
        compiler_params=pltpu.CompilerParams(vmem_limit_bytes=28 * MIB),
        cost_estimate=pl.CostEstimate(
            flops=4 * count * width * units, bytes_accessed=12 * MIB, transcendentals=0
        ),
        name="hidden_back",
    )(dz_low, slope, w_down_t, w_up)


def attend_back_body(chains, slots, dz_ref, own_ref, other_ref, normed_ref, inverse_ref, gain_ref,
                     qkv_ref, prob_ref, w_ref, dz_one_ref, low_ref, d_qkv_ref, part_ref, sum_ref,
                     sum_qkv_ref, d_att_ref):
    width = d_att_ref.shape[1]
    normed = normed_ref[...]
    d_hidden = dz_ref[...] + (own_ref[...].astype(F32) + other_ref[...].astype(F32))
    dz_one = norm_back(d_hidden * gain_ref[...], normed, inverse_ref[:, 0:1])
    dz_one_ref[...] = dz_one
    low_ref[...] = dz_one.astype(B16)

    @pl.when(pl.program_id(0) == 0)
    def _():
        sum_ref[...] = jnp.zeros_like(sum_ref)
        sum_qkv_ref[...] = jnp.zeros_like(sum_qkv_ref)

    sum_ref[0:1] += col_sum(d_hidden * normed)
    sum_ref[1:2] += col_sum(d_hidden)
    sum_ref[2:3] += col_sum(dz_one)
    d_att_ref[...] = dot(low_ref[...], w_ref[:, 3 * width :]).astype(B16)
    mask = two_heads(slots)
    for chain in range(chains):
        rows = pl.ds(chain * slots, slots)
        for pair in range(width // (2 * HEAD)):
            lanes = 2 * HEAD * pair
            query = qkv_ref[rows, lanes : lanes + 2 * HEAD]
            key = qkv_ref[rows, width + lanes : width + lanes + 2 * HEAD]
            value = qkv_ref[rows, 2 * width + lanes : 2 * width + lanes + 2 * HEAD]
            d_att = d_att_ref[rows, lanes : lanes + 2 * HEAD]
            prob = prob_ref[rows, 2 * slots * pair : 2 * slots * (pair + 1)]
            d_prob = dot_t(d_att, doubled(value, mask))
            weights = prob.astype(F32)
            products = weights * d_prob
            lows = []
            for head in range(2):
                half = slice(head * slots, (head + 1) * slots)
                total = jnp.sum(products[:, half], axis=-1, keepdims=True)
                lows.append((products[:, half] - weights[:, half] * total).astype(B16))
            low = jnp.concatenate(lows, axis=1)
            d_query = dot(low, doubled(key, mask)) * (HEAD**-0.5)
            tall = jnp.concatenate(lows, axis=0)
            d_key = t_dot(tall, doubled(query, mask)) * (HEAD**-0.5)
            tall = jnp.concatenate([prob[:, :slots], prob[:, slots:]], axis=0)
            d_value = t_dot(tall, doubled(d_att, mask))
            d_qkv_ref[rows, lanes : lanes + 2 * HEAD] = d_query.astype(B16)
            d_qkv_ref[rows, width + lanes : width + lanes + 2 * HEAD] = d_key.astype(B16)
            d_qkv_ref[rows, 2 * width + lanes : 2 * width + lanes + 2 * HEAD] = d_value.astype(B16)
    sum_qkv_ref[0:1] += col_sum(d_qkv_ref[...].astype(F32))
    part_ref[...] = dot_t(d_qkv_ref[...], w_ref[:, : 3 * width]).astype(B16)


def attend_back(chain_count, dz_two, own, other, normed, inverse, gain, qkv, prob, w_a):
    count, width = dz_two.shape
    heads = qkv.shape[1] // 3
    chains = 2 if chain_count % 2 == 0 else 1
    slots = count // chain_count
    rows = chains * slots
    shape = jax.ShapeDtypeStruct
    return pl.pallas_call(
        functools.partial(attend_back_body, chains, slots),
        grid=(count // rows,),
        in_specs=[
            rows_of(rows, width),
            rows_of(rows, width),
            rows_of(rows, width),
            rows_of(rows, width),
            rows_of(rows, 128),
            whole(gain.shape),
            rows_of(rows, 3 * heads),
            rows_of(rows, prob.shape[1]),
            whole(w_a.shape),
        ],
        out_specs=[
            rows_of(rows, width),
            rows_of(rows, width),
            rows_of(rows, 3 * heads),
            rows_of(rows, width),
            whole((8, width)),
            whole((8, 3 * heads)),
        ],
        out_shape=[
            shape((count, width), F32),
            shape((count, width), B16),
            shape((count, 3 * heads), B16),
            shape((count, width), B16),
            shape((8, width), F32),
            shape((8, 3 * heads), F32),
        ],
        scratch_shapes=[pltpu.VMEM((rows, heads), B16)],
        compiler_params=pltpu.CompilerParams(vmem_limit_bytes=32 * MIB),
        cost_estimate=pl.CostEstimate(
            flops=2 * count * width * 6 * heads, bytes_accessed=20 * MIB, transcendentals=0
        ),
        name="attend_back",
    )(dz_two, own, other, normed, inverse, gain, qkv, prob, w_a)


def last_body(dz_ref, own_ref, other_ref, flag_ref, out_ref, sum_ref):
    total = dz_ref[...] + (own_ref[...].astype(F32) + other_ref[...].astype(F32))
    flag = flag_ref[:, 0:1]
    masked = total * flag

    @pl.when(pl.program_id(0) == 0)
    def _():
        sum_ref[...] = jnp.zeros_like(sum_ref)

    sum_ref[0:1] += col_sum(masked)
    out_ref[...] = total - masked


def last(dz_one, own, other, flag):
    count, width = dz_one.shape
    rows = count // 4
    shape = jax.ShapeDtypeStruct
    return pl.pallas_call(
        last_body,
        grid=(4,),
        in_specs=[rows_of(rows, width)] * 3 + [rows_of(rows, 128)],
        out_specs=[rows_of(rows, width), whole((8, width))],
        out_shape=[shape((count, width), F32), shape((8, width), F32)],
        compiler_params=pltpu.CompilerParams(vmem_limit_bytes=20 * MIB),
        cost_estimate=pl.CostEstimate(flops=10 * count * width, bytes_accessed=10 * MIB, transcendentals=0),
        name="last",
    )(dz_one, own, other, flag)


def near_total(own, from_x, from_y):
    return own[:2].astype(F32) + from_x.astype(F32) + from_y.astype(F32)


def add_low(left, right):
    return (left.astype(F32) + right.astype(F32)).astype(B16)


def per_device(dp_size, tokens, masked, lengths, mask_vector, w_query, b_query, w_key, w_value,
               b_value, w_out, b_out, gain_one, shift_one, w_up, b_up, w_down, b_down, gain_two,
               shift_two, grad_out):
    head_cols = w_query.shape[1]
    width = tokens.shape[1]
    fast = dp_size == BLOCKS and w_query.shape[0] % 16 == 0
    me = lax.axis_index("dp").astype(jnp.int32).reshape(1)
    if not fast:
        me = jnp.zeros_like(me)

    (b_query, b_value, b_out, gain_one, shift_one, b_up, b_down, gain_two, shift_two) = (
        member.astype(F32)
        for member in (b_query, b_value, b_out, gain_one, shift_one, b_up, b_down, gain_two, shift_two)
    )
    is_masked = (masked == 1)[:, None]
    flag = jnp.broadcast_to(is_masked, (masked.shape[0], 128)).astype(F32)
    in_low = jnp.where(is_masked, mask_vector[None, :], tokens)
    bias_qkv = jnp.concatenate([b_query, jnp.zeros_like(b_query), b_value])[None, :]
    vectors_one = jnp.stack([b_out, gain_one, shift_one])
    vectors_two = jnp.stack([gain_one, shift_one, b_down, gain_two, shift_two])

    a = jnp.concatenate([w_query, w_key, w_value, w_out.T], axis=1)
    c = w_up
    d = w_down.T
    if fast:
        az = swap(a, 12)
        a, az, c = tie(a, az, c)
        an = jnp.stack([a, az])
        am, anx, any_ = swap(an, 4), swap(an, 1), swap(an, 2)
        cz = swap(c, 12)
        an, am, anx, any_, c, cz, d = tie(an, am, anx, any_, c, cz, d)
        cn = jnp.stack([c, cz])
        amx, amy = swap(am, 1), swap(am, 2)
        cm = swap(cn, 4)
        an, am, anx, any_, amx, amy, cn, cm, d = tie(an, am, anx, any_, amx, amy, cn, cm, d)
        and_, amd = swap(anx, 2), swap(amy, 1)
        cnx, cny = swap(cn, 1), swap(cn, 2)
        dz = swap(d, 12)
        an, am, anx, any_, amx, amy, and_, amd, cn, cm, cnx, cny, d, dz = tie(
            an, am, anx, any_, amx, amy, and_, amd, cn, cm, cnx, cny, d, dz
        )
        dn = jnp.stack([d, dz])
        cmx, cmy = swap(cm, 1), swap(cm, 2)
        dm = swap(dn, 4)
        pieces_a = [an, am, anx, amx, any_, amy, and_, amd]
    else:
        a, c, d = (lax.all_gather(piece, "dp", axis=0, tiled=True) for piece in (a, c, d))
        pieces_a, pieces_c, pieces_d = as_pieces(a), as_pieces(c), as_pieces(d)
    w_a, qkv, prob, attended, part = attend(me, lengths, in_low, bias_qkv, pieces_a)
    if fast:
        part, cn, cm, cnx, cny, cmx, cmy, dn, dm = tie(part, cn, cm, cnx, cny, cmx, cmy, dn, dm)
        other = pair_swap(part)
        cnd, cmd = swap(cnx, 2), swap(cmy, 1)
        dnx, dny = swap(dn, 1), swap(dn, 2)
        other, part, cnd, cmd, cn, cm, cnx, cny, cmx, cmy, dn, dm, dnx, dny = tie(
            other, part, cnd, cmd, cn, cm, cnx, cny, cmx, cmy, dn, dm, dnx, dny
        )
        dmx, dmy = swap(dm, 1), swap(dm, 2)
        dnd = swap(dnx, 2)
        pieces_c = [cn, cm, cnx, cmx, cny, cmy, cnd, cmd]
    else:
        other = pair_swap(part)
    w_u, normed_one, inverse_one, hidden_low, act_low, slope = up(
        me, in_low, part, other, vectors_one, b_up[None, :], pieces_c
    )
    if fast:
        act_low, dmx, dmy, dnd = tie(act_low, dmx, dmy, dnd)
        dmd = swap(dmy, 1)
        pieces_d = [dn, dm, dnx, dmx, dny, dmy, dnd, dmd]
    w_d, part = down(me, act_low, pieces_d)
    other = pair_swap(part)
    result, dz_two, dz_two_low, sums_two = second_norm(normed_one, part, other, grad_out, vectors_two)
    dx, dy, dxl, dyl, do = weight_grad(me, [dz_two_low], [act_low])
    if fast:
        dx, dy, dxl, dyl, dz_two_low = tie(dx, dy, dxl, dyl, dz_two_low)
        dxr, dyr = swap(dx, 1), swap(dy, 2)
    d_pre_low, part, sums_up = hidden_back(dz_two_low, slope, w_d, w_u)
    if fast:
        part, dxr, dyr, d_pre_low = tie(part, dxr, dyr, d_pre_low)
        other = pair_swap(part)
        dxlr, dylr = swap(add_low(dxl, dyr[:2]), 1), swap(add_low(dyl, dxr[:2]), 2)
        cx, cy, cxl, cyl, co = weight_grad(me, [hidden_low], [d_pre_low])
        other, dxlr, dylr, cx, cy = tie(other, dxlr, dylr, cx, cy)
        cxr, cyr = swap(cx, 1), swap(cy, 2)
        d_mid = (do[2:].astype(F32) + dxlr.astype(F32) + dyr[2:].astype(F32)).astype(B16)
        d_near = do[:2].astype(F32) + dxr[2:].astype(F32) + dylr.astype(F32)
        d_midr = swap(d_mid, 4)
    else:
        other = pair_swap(part)
        cx, cy, cxl, cyl, co = weight_grad(me, [hidden_low], [d_pre_low])
    dz_one, dz_one_low, d_qkv, part, sums_one, sums_qkv = attend_back(
        lengths.shape[0], dz_two, part, other, normed_one, inverse_one, gain_one[None, :], qkv, prob, w_a
    )
    if fast:
        part, d_qkv, cxr, cyr, d_midr, d_near = tie(part, d_qkv, cxr, cyr, d_midr, d_near)
        other = pair_swap(part)
        d_near = d_near + d_midr.astype(F32)
        d_far = swap(d_near[1].astype(B16), 12)
        cxlr, cylr = swap(add_low(cxl, cyr[:2]), 1), swap(add_low(cyl, cxr[:2]), 2)
        ax, ay, axl, ayl, ao = weight_grad(me, [in_low, dz_one_low], [d_qkv, attended])
        other, d_far, cxlr, cylr, ax, ay = tie(other, d_far, cxlr, cylr, ax, ay)
        axr, ayr = swap(ax, 1), swap(ay, 2)
        c_mid = (co[2:].astype(F32) + cxlr.astype(F32) + cyr[2:].astype(F32)).astype(B16)
        c_near = co[:2].astype(F32) + cxr[2:].astype(F32) + cylr.astype(F32)
        c_midr = swap(c_mid, 4)
    else:
        other = pair_swap(part)
        ax, ay, axl, ayl, ao = weight_grad(me, [in_low, dz_one_low], [d_qkv, attended])
    d_tokens, sums_mask = last(dz_one, part, other, flag)
    parts = (
        sums_mask[0],
        sums_qkv[0, :head_cols],
        sums_qkv[0, 2 * head_cols :],
        sums_one[2],
        sums_one[0],
        sums_one[1],
        sums_up[0],
        sums_two[2],
        sums_two[0],
        sums_two[1],
    )
    joined = jnp.concatenate(parts).reshape(-1, 128)
    if fast:
        joined, axr, ayr, c_midr, c_near = tie(joined, axr, ayr, c_midr, c_near)
        axlr, aylr = swap(add_low(axl, ayr[:2]), 1), swap(add_low(ayl, axr[:2]), 2)
        c_near = c_near + c_midr.astype(F32)
        c_far = swap(c_near[1].astype(B16), 12)
        joined = joined + swap(joined, 1)
        joined = joined + swap(joined, 2)
        axlr, aylr, c_far, joined = tie(axlr, aylr, c_far, joined)
        a_mid = (ao[2:].astype(F32) + axlr.astype(F32) + ayr[2:].astype(F32)).astype(B16)
        a_near = ao[:2].astype(F32) + axr[2:].astype(F32) + aylr.astype(F32)
        a_midr = swap(a_mid, 4)
        joined = joined + swap(joined, 4)
        a_midr, joined = tie(a_midr, joined)
        a_near = a_near + a_midr.astype(F32)
        a_far = swap(a_near[1].astype(B16), 12)
        joined = joined + swap(joined, 8)
        d_wa = a_near[0] + a_far.astype(F32)
        d_w_up = c_near[0] + c_far.astype(F32)
        d_w_down_t = d_near[0] + d_far.astype(F32)
    else:
        full = []
        for x, y, xl, yl, o in ((ax, ay, axl, ayl, ao), (cx, cy, cxl, cyl, co), (dx, dy, dxl, dyl, do)):
            blocks = [None] * BLOCKS
            for k in range(2):
                blocks[3 + NEAR[k]], blocks[1 + NEAR[k]], blocks[1 + MID[k]] = x[k], x[2 + k], xl[k]
                blocks[3 + MID[k]], blocks[2 + MID[k]], blocks[2 + NEAR[k]] = y[k], y[2 + k], yl[k]
                blocks[NEAR[k]], blocks[MID[k]] = o[k], o[2 + k]
            full.append(jnp.concatenate(blocks).astype(F32))
        joined = lax.psum(joined, "dp")
        d_wa, d_w_up, d_w_down_t = (
            lax.psum_scatter(member, "dp", scatter_dimension=0, tiled=True) for member in full
        )
    joined = joined.reshape(-1)
    summed = []
    start = 0
    for member in parts:
        summed.append(joined[start : start + member.shape[0]])
        start += member.shape[0]
    return (
        result,
        d_tokens,
        summed[0],
        d_wa[:, :head_cols],
        summed[1],
        d_wa[:, head_cols : 2 * head_cols],
        d_wa[:, 2 * head_cols : 3 * head_cols],
        summed[2],
        d_wa[:, 3 * head_cols :].T,
        summed[3],
        summed[4],
        summed[5],
        d_w_up,
        summed[6],
        d_w_down_t.T,
        summed[7],
        summed[8],
        summed[9],
    )


def solution(mesh):
    rows, flat, both = P("dp", None), P(), P("dp", "mp")
    return jax.shard_map(
        functools.partial(per_device, mesh.shape["dp"]),
        mesh=mesh,
        in_specs=(rows, P("dp"), P("dp"), flat, both, P("mp"), both, both, P("mp"), P("mp", "dp"),
                  flat, flat, flat, both, P("mp"), P("mp", "dp"), flat, flat, flat, rows),
        out_specs=(rows, rows, flat, both, P("mp"), both, both, P("mp"), P("mp", "dp"), flat, flat,
                   flat, both, P("mp"), P("mp", "dp"), flat, flat, flat),
        check_vma=False,
    )
```

time: 329 us -> 244 us (0.74); the launches traced: 323 us -> 243 us
  matrix products: 55.5 us -> 0 us
  Pallas kernels: 19.1 us -> 68.2 us
  waiting for transfers between devices: 114 us -> 74.6 us
  other arithmetic: 35.2 us -> 11 us
  local copies, waits for them, and re-layouts: 31.4 us -> 23 us
    dot_general x18 -> x0, matrix products: 55.5 us -> none  [the longest x1 10.1 us: per_device(): d_act = dot(dz_two_low, w_down_t)]
    pallas_call x6 -> x10, Pallas kernels: 19.1 us -> 68.2 us  [the longest x3 16.4 us: weight_grad(): pl.pallas_call(body, grid=(total,), in_specs=[SMEM_SPEC] + [whole(left.sh...]
    ppermute x50, waiting for transfers between devices: 114 us -> 74.6 us  [the longest x46 70.9 us: swap(): return lax.ppermute(values, 'dp', [(i, i ^ bit) for i in range(BLOCKS)])]
    reduce_sum x8 -> x0, other arithmetic: 17.6 us -> none  [the longest x2 5.81 us: layer_norm(): row_mean = jnp.mean(values, axis=-1, keepdims=True)]
    slice x15 -> x8, local copies, waits for them, and re-layouts: 6.98 us -> 1.93 us  [the longest x3 1.81 us: per_device(): summed.append(joined[start:start + member.shape[0]])]
    convert_element_type x8, other arithmetic: 8.11 us -> 3.35 us  [the longest x6 2.55 us: add_low(): return (left.astype(F32) + right.astype(F32)).astype(B16)]
    split x4 -> x0, local copies, waits for them, and re-layouts: 3.98 us -> none  [per_device(): jnp.split(qkv, 3, axis=1)]
    unnamed x163 -> x99, local copies, waits for them, and re-layouts: 17.2 us -> 20 us
  transfers between devices with their start and end apart: 50 -> 50, of which waited for: 27 -> 26; matrix products, arithmetic and copies ran while one was open for 16% -> 5% of each run, Pallas kernels for 3% -> 22%
where the time goes in v3:
time: 244 us; the launch traced here: 243 us
  waiting for transfers between devices  74.6 us (31%)
  Pallas kernels  68.2 us (28%)
  starting transfers between devices  65.1 us (27%)
  local copies, waits for them, and re-layouts  23 us (9%)
  other arithmetic  11 us (5%)
    ppermute x46, waiting for transfers between devices, swap(): return lax.ppermute(values, 'dp', [(i, i ^ bit) for i in range(BLOCKS)])  70.9 us
    ppermute x46, starting transfers between devices, swap(): return lax.ppermute(values, 'dp', [(i, i ^ bit) for i in range(BLOCKS)])  65 us
    unnamed x99, local copies, waits for them, and re-layouts  20 us
    pallas_call x3, Pallas kernels, weight_grad(): pl.pallas_call(body, grid=(total,), in_specs=[SMEM_SPEC] + [whole(left.sh...  16.4 us
    pallas_call x1, Pallas kernels, attend_back(): pl.pallas_call(functools.partial(attend_back_body, chains, slots), grid=(...  15.5 us
    pallas_call x1, Pallas kernels, attend(): pl.pallas_call(functools.partial(attend_body, chains, slots), grid=(count...  8.21 us
    pallas_call x1, Pallas kernels, hidden_back(): pl.pallas_call(hidden_back_body, grid=(4,), in_specs=[rows_of(rows, width...  7.99 us
    pallas_call x1, Pallas kernels, up(): pl.pallas_call(up_body, grid=(4,), in_specs=[SMEM_SPEC] + [rows_of(rows,...  7.55 us
  transfers between devices with their start and end apart: 50, of which 26 were waited for; matrix products, arithmetic and copies ran while one was open for 5% of the time, Pallas kernels for 22%

profile of v3, /device:TPU:0, one launch (start us, length us, event | category | flops | bytes accessed | tf_op | source)
XLA Modules:
  0.0 243.2 jit_solution(12614228847510130385)
XLA Ops:
  1.5 5.1 %collective-permute-start = (bf16[48,1536]{1,0:T(8,128)(2,1)S(1)}, bf16[48,1536]{1,0:T(8,128)(2,1)S(1)}, u32[]{:S(2)}, u32[]{:S(2)}) collective-permute-start(bf16[48,1536]{1,0:T(8,128)(2,1)S(1)} %pad_maximum_fusion.3), channel_id=1, source_target_pairs={{0,24},{2,26},{4,28},{6,30},{8,16},{10,18},{12,20},{14,22},{16,8},... | collective-permute-start | bytes 442376 | tf_op jit(solution)/shard_map/ppermute | solution.py:22
  6.6 4.0 %collective-permute-done = bf16[48,1536]{1,0:T(8,128)(2,1)S(1)} collective-permute-done((bf16[48,1536]{1,0:T(8,128)(2,1)S(1)}, bf16[48,1536]{1,0:T(8,128)(2,1)S(1)}, u32[]{:S(2)}, u32[]{:S(2)}) %collective-permute-start) | collective-permute-done | bytes 147488 | tf_op jit(solution)/shard_map/ppermute | solution.py:22
  18.9 4.9 %collective-permute-done.4 = bf16[48,1536]{1,0:T(8,128)(2,1)S(1)} collective-permute-done((bf16[48,1536]{1,0:T(8,128)(2,1)}, bf16[48,1536]{1,0:T(8,128)(2,1)S(1)}, u32[]{:S(2)}, u32[]{:S(2)}) %collective-permute-start.4) | collective-permute-done | bytes 147488 | tf_op jit(solution)/shard_map/ppermute | solution.py:22
  29.2 3.8 %collective-permute-done.7.rest_1_ = bf16[2,48,1536]{2,1,0:T(8,128)(2,1)S(1)} collective-permute-done((bf16[2,48,1536]{2,1,0:T(8,128)(2,1)S(1)}, bf16[2,48,1536]{2,1,0:T(8,128)(2,1)S(1)}, u32[]{:S(2)}, u32[]{:S(2)}) %collective-permute-start.7) | collective-permute-done | bytes 294944 | tf_op jit(solution)/shard_map/ppermute | solution.py:22
  42.4 3.1 %collective-permute-done.12 = bf16[48,1536]{1,0:T(8,128)(2,1)} collective-permute-done((bf16[48,1536]{1,0:T(8,128)(2,1)}, bf16[48,1536]{1,0:T(8,128)(2,1)}, u32[]{:S(2)}, u32[]{:S(2)}) %collective-permute-start.12) | collective-permute-done | bytes 147488 | tf_op jit(solution)/shard_map/ppermute | solution.py:22
  54.8 8.2 %attend.1 = (bf16[768,1536]{1,0:T(8,128)(2,1)S(1)}, bf16[1024,1152]{1,0:T(8,128)(2,1)S(1)}, bf16[1024,768]{1,0:T(8,128)(2,1)S(1)}, bf16[1024,384]{1,0:T(8,128)(2,1)S(1)}, bf16[1024,768]{1,0:T(8,128)(2,1)S(1)}) custom-call(s32[1]{0:T(128)} %bitcast.me_ref, s32[8]{0:T(128)S(1)} %copy-done.21, bf16[1024,768]{1,0:T(8,128)(2,1)S(1)} %broadcast_select_fusion.in_ref.refs_0_, ...), custom_call_target="tpu_custom_call" | custom-call | flops 2415919104 | bytes 12582912 | tf_op jit(solution)/shard_map/attend/pallas_call | solution.py:143
  72.3 5.7 %collective-permute-done.17.rest_6_ = bf16[2,48,1536]{2,1,0:T(8,128)(2,1)S(1)} collective-permute-done((bf16[2,48,1536]{2,1,0:T(8,128)(2,1)S(1)}, bf16[2,48,1536]{2,1,0:T(8,128)(2,1)S(1)}, u32[]{:S(2)}, u32[]{:S(2)}) %collective-permute-start.17) | collective-permute-done | bytes 294944 | tf_op jit(solution)/shard_map/ppermute | solution.py:22
  79.0 5.5 %collective-permute-done.19.rest_2_ = bf16[2,48,1536]{2,1,0:T(8,128)(2,1)S(1)} collective-permute-done((bf16[2,48,1536]{2,1,0:T(8,128)(2,1)S(1)}, bf16[2,48,1536]{2,1,0:T(8,128)(2,1)S(1)}, u32[]{:S(2)}, u32[]{:S(2)}) %collective-permute-start.19) | collective-permute-done | bytes 294944 | tf_op jit(solution)/shard_map/ppermute | solution.py:22
  87.8 7.5 %up.1 = (bf16[768,1536]{1,0:T(8,128)(2,1)S(1)}, f32[1024,768]{1,0:T(8,128)}, f32[1024,128]{1,0:T(8,128)S(1)}, bf16[1024,768]{1,0:T(8,128)(2,1)S(1)}, bf16[1024,1...) custom-call(s32[1]{0:T(128)} %bitcast.me_ref, bf16[1024,768]{1,0:T(8,128)(2,1)S(1)} %broadcast_select_fusion.in_ref.refs_0_, ...), custom_call_target="tpu_custom_call" | custom-call | flops 2415919104 | bytes 20971520 | tf_op jit(solution)/shard_map/up/pallas_call | solution.py:196
  95.7 4.7 %collective-permute-done.23.rest_6_ = bf16[2,48,1536]{2,1,0:T(8,128)(2,1)S(1)} collective-permute-done((bf16[2,48,1536]{2,1,0:T(8,128)(2,1)S(1)}, bf16[2,48,1536]{2,1,0:T(8,128)(2,1)S(1)}, u32[]{:S(2)}, u32[]{:S(2)}) %collective-permute-start.23) | collective-permute-done | bytes 294944 | tf_op jit(solution)/shard_map/ppermute | solution.py:22
  100.8 6.9 %collective-permute-done.24.rest_7_ = bf16[2,48,1536]{2,1,0:T(8,128)(2,1)S(1)} collective-permute-done((bf16[2,48,1536]{2,1,0:T(8,128)(2,1)S(1)}, bf16[2,48,1536]{2,1,0:T(8,128)(2,1)S(1)}, u32[]{:S(2)}, u32[]{:S(2)}) %collective-permute-start.24) | collective-permute-done | bytes 294944 | tf_op jit(solution)/shard_map/ppermute | solution.py:22
  109.6 4.3 %down.1 = (bf16[768,1536]{1,0:T(8,128)(2,1)S(1)}, bf16[1024,768]{1,0:T(8,128)(2,1)}) custom-call(s32[1]{0:T(128)} %bitcast.me_ref, bf16[1024,1536]{1,0:T(8,128)(2,1)S(1)} %copy-done.23, bf16[2,48,1536]{2,1,0:T(8,128)(2,1)S(1)} %pad_maximum_fusion.2.rest_0_, bf16[2,48,1536]{2,1,0:T(8,128)(2,1)S(1)} %collective-permute-done.15.rest_1_, ...), custom_call_target="tpu_custom_call" | custom-call | flops 2415919104 | bytes 8388608 | tf_op jit(solution)/shard_map/down/pallas_call | solution.py:242
  115.4 3.7 %collective-permute-done.25.other_ref = bf16[1024,768]{1,0:T(8,128)(2,1)} collective-permute-done((bf16[1024,768]{1,0:T(8,128)(2,1)}, bf16[1024,768]{1,0:T(8,128)(2,1)}, u32[]{:S(2)}, u32[]{:S(2)}) %collective-permute-start.25) | collective-permute-done | bytes 1572896 | tf_op jit(solution)/shard_map/ppermute | solution.py:30
  120.5 5.8 %second_norm.1 = (bf16[1024,768]{1,0:T(8,128)(2,1)}, f32[1024,768]{1,0:T(8,128)S(1)}, bf16[1024,768]{1,0:T(8,128)(2,1)S(1)}, f32[8,768]{1,0:T(8,128)S(1)}) custom-call(f32[1024,768]{1,0:T(8,128)S(1)} %copy-done, bf16[1024,768]{1,0:T(8,128)(2,1)} %get-tuple-element.221.own_ref, bf16[1024,768]{1,0:T(8,128)(2,1)} %collective-permute-done.25.other_ref, ...), custom_call_target="tpu_custom_call" | custom-call | flops 31457280 | bytes 14680064 | tf_op jit(solution)/shard_map/second_norm/pallas_call | solution.py:280
  128.0 5.3 %weight_grad.3 = (bf16[4,48,1536]{2,1,0:T(8,128)(2,1)S(1)}, bf16[4,48,1536]{2,1,0:T(8,128)(2,1)S(1)}, bf16[2,48,1536]{2,1,0:T(8,128)(2,1)S(1)}, bf16[2,48,1536]{2,1,0:T(8,128)(2,1)S(1)}, bf16[4,48,1536]{2,1,0:T(8,128)(2,1)S(1)}) custom-call(s32[1]{0:T(128)} %bitcast.me_ref, bf16[1024,768]{1,0:T(8,128)(2,1)S(1)} %get-tuple-element.229.refs_0_.low_ref, ...), custom_call_target="tpu_custom_call" | custom-call | flops 2415919104 | bytes 9437184 | tf_op jit(solution)/shard_map/weight_grad/pallas_call | solution.py:360
  136.6 8.0 %hidden_back.1 = (bf16[1024,1536]{1,0:T(8,128)(2,1)S(1)}, bf16[1024,768]{1,0:T(8,128)(2,1)S(1)}, f32[8,1536]{1,0:T(8,128)S(1)}) custom-call(bf16[1024,768]{1,0:T(8,128)(2,1)S(1)} %get-tuple-element.229.refs_0_.low_ref, bf16[1024,1536]{1,0:T(8,128)(2,1)S(1)} %copy-done.22, bf16[768,1536]{1,0:T(8,128)(2,1)S(1)} %copy-done.30, bf16[768,1536]{1,0:T(8,128)(2,1)S(1)} %copy-done.26), custom_call_target="tpu_custom_call" | custom-call | flops 4831838208 | bytes 12582912 | tf_op jit(solution)/shard_map/hidden_back/pallas_call | solution.py:394
  146.2 4.2 %collective-permute-done.26 = bf16[4,48,1536]{2,1,0:T(8,128)(2,1)} collective-permute-done((bf16[4,48,1536]{2,1,0:T(8,128)(2,1)S(1)}, bf16[4,48,1536]{2,1,0:T(8,128)(2,1)}, u32[]{:S(2)}, u32[]{:S(2)}) %collective-permute-start.26) | collective-permute-done | bytes 589856 | tf_op jit(solution)/shard_map/ppermute | solution.py:22
  157.6 5.3 %weight_grad.4 = (bf16[4,48,1536]{2,1,0:T(8,128)(2,1)S(1)}, bf16[4,48,1536]{2,1,0:T(8,128)(2,1)S(1)}, bf16[2,48,1536]{2,1,0:T(8,128)(2,1)S(1)}, bf16[2,48,1536]{2,1,0:T(8,128)(2,1)S(1)}, bf16[4,48,1536]{2,1,0:T(8,128)(2,1)S(1)}) custom-call(s32[1]{0:T(128)} %bitcast.me_ref, bf16[1024,768]{1,0:T(8,128)(2,1)S(1)} %copy-done.28, bf16[1024,1536]{1,0:T(8,128)(2,1)S(1)} %copy-done.32), custom_call_target="tpu_custom_call" | custom-call | flops 2415919104 | bytes 9437184 | tf_op jit(solution)/shard_map/weight_grad/pallas_call | solution.py:360
  167.2 15.5 %attend_back.1 = (f32[1024,768]{1,0:T(8,128)S(1)}, bf16[1024,768]{1,0:T(8,128)(2,1)S(1)}, bf16[1024,1152]{1,0:T(8,128)(2,1)S(1)}, bf16[1024,768]{1,0:T(8,128)(2,...) custom-call(f32[1024,768]{1,0:T(8,128)S(1)} %copy-done.2, bf16[1024,768]{1,0:T(8,128)(2,1)S(1)} %get-tuple-element.237.own_ref, ...), custom_call_target="tpu_custom_call" | custom-call | flops 3623878656 | bytes 20971520 | tf_op jit(solution)/shard_map/attend_back/pallas_call | solution.py:474
  184.8 2.9 %collective-permute-start.35 = (bf16[48,1536]{1,0:T(8,128)(2,1)S(1)}, bf16[48,1536]{1,0:T(8,128)(2,1)S(1)}, u32[]{:S(2)}, u32[]{:S(2)}) collective-permute-start(bf16[48,1536]{1,0:T(8,128)(2,1)S(1)} %fusion.4), channel_id=1, source_target_pairs={{0,24},{2,26},{4,28},{6,30},{8,16},{10,18},{12,20},{14,22},{16,8},... | collective-permute-start | bytes 442376 | tf_op jit(solution)/shard_map/ppermute | solution.py:22
  187.7 5.7 %weight_grad.5 = (bf16[4,48,1536]{2,1,0:T(8,128)(2,1)S(1)}, bf16[4,48,1536]{2,1,0:T(8,128)(2,1)S(1)}, bf16[2,48,1536]{2,1,0:T(8,128)(2,1)S(1)}, bf16[2,48,1536]{2,1,0:T(8,128)(2,1)S(1)}, bf16[4,48,1536]{2,1,0:T(8,128)(2,1)S(1)}) custom-call(s32[1]{0:T(128)} %bitcast.me_ref, bf16[1024,768]{1,0:T(8,128)(2,1)S(1)} %copy-done.10, ...), custom_call_target="tpu_custom_call" | custom-call | flops 2415919104 | bytes 9437184 | tf_op jit(solution)/shard_map/weight_grad/pallas_call | solution.py:360
  203.5 10.5 %collective-permute-done.38 = bf16[4,48,1536]{2,1,0:T(8,128)(2,1)S(1)} collective-permute-done((bf16[4,48,1536]{2,1,0:T(8,128)(2,1)S(1)}, bf16[4,48,1536]{2,1,0:T(8,128)(2,1)S(1)}, u32[]{:S(2)}, u32[]{:S(2)}) %collective-permute-start.38) | collective-permute-done | bytes 589856 | tf_op jit(solution)/shard_map/ppermute | solution.py:22
  222.7 3.2 %collective-permute-done.45 = f32[60,128]{1,0:T(8,128)S(1)} collective-permute-done((f32[60,128]{1,0:T(8,128)S(1)}, f32[60,128]{1,0:T(8,128)S(1)}, u32[]{:S(2)}, u32[]{:S(2)}) %collective-permute-start.45) | collective-permute-done | bytes 30752 | tf_op jit(solution)/shard_map/ppermute | solution.py:22
  229.9 3.5 %collective-permute-done.46 = bf16[2,48,1536]{2,1,0:T(8,128)(2,1)S(1)} collective-permute-done((bf16[2,48,1536]{2,1,0:T(8,128)(2,1)S(1)}, bf16[2,48,1536]{2,1,0:T(8,128)(2,1)S(1)}, u32[]{:S(2)}, u32[]{:S(2)}) %collective-permute-start.46) | collective-permute-done | bytes 294944 | tf_op jit(solution)/shard_map/ppermute | solution.py:22
  (239 shorter events, 104.5 us)
Async XLA Ops:
  10.6 13.3 %collective-permute-start.1 = (bf16[2,48,1536]{2,1,0:T(8,128)(2,1)S(1)}, bf16[2,48,1536]{2,1,0:T(8,128)(2,1)S(1)}, u32[]{:S(2)}, u32[]{:S(2)}) collective-permute-start(bf16[2,48,1536]{2,1,0:T(8,128)(2,1)S(1)} %pad_maximum_fusion.rest_0_), channel_id=1, source_target_pairs={{0,8},{2,10},{4,12},{6,14},{8,0},{10,2},{12,4},{14,6},{16,24},{18,... | collective-permute-start | bytes 884744 | tf_op jit(solution)/shard_map/ppermute | solution.py:22
  13.4 10.4 %collective-permute-start.2 = (bf16[2,48,1536]{2,1,0:T(8,128)(2,1)S(1)}, bf16[2,48,1536]{2,1,0:T(8,128)(2,1)}, u32[]{:S(2)}, u32[]{:S(2)}) collective-permute-start(bf16[2,48,1536]{2,1,0:T(8,128)(2,1)S(1)} %pad_maximum_fusion.rest_0_), channel_id=1, source_target_pairs={{0,2},{2,0},{4,6},{6,4},{8,10},{10,8},{12,14},{14,12},{16,18},{18,... | collective-permute-start | bytes 884744 | tf_op jit(solution)/shard_map/ppermute | solution.py:22
  34.1 11.4 %collective-permute-start.10 = (bf16[2,48,1536]{2,1,0:T(8,128)(2,1)S(1)}, bf16[2,48,1536]{2,1,0:T(8,128)(2,1)S(1)}, u32[]{:S(2)}, u32[]{:S(2)}) collective-permute-start(bf16[2,48,1536]{2,1,0:T(8,128)(2,1)S(1)} %pad_maximum_fusion.1.rest_0_), channel_id=1, source_target_pairs={{0,2},{2,0},{4,6},{6,4},{8,10},{10,8},{12,14},{14,12},{16,18},{18,... | collective-permute-start | bytes 884744 | tf_op jit(solution)/shard_map/ppermute | solution.py:22
  35.5 10.0 %collective-permute-start.11 = (bf16[2,48,1536]{2,1,0:T(8,128)(2,1)S(1)}, bf16[2,48,1536]{2,1,0:T(8,128)(2,1)S(1)}, u32[]{:S(2)}, u32[]{:S(2)}) collective-permute-start(bf16[2,48,1536]{2,1,0:T(8,128)(2,1)S(1)} %pad_maximum_fusion.1.rest_0_), channel_id=1, source_target_pairs={{0,4},{2,6},{4,0},{6,2},{8,12},{10,14},{12,8},{14,10},{16,20},{18,... | collective-permute-start | bytes 884744 | tf_op jit(solution)/shard_map/ppermute | solution.py:22
  36.3 10.6 %collective-permute-start.8 = (bf16[2,48,1536]{2,1,0:T(8,128)(2,1)}, bf16[2,48,1536]{2,1,0:T(8,128)(2,1)}, u32[]{:S(2)}, u32[]{:S(2)}) collective-permute-start(bf16[2,48,1536]{2,1,0:T(8,128)(2,1)} %collective-permute-done.2.rest_2_), channel_id=1, source_target_pairs={{0,4},{2,6},{4,0},{6,2},{8,12},{10,14},{12,8},{14,10},{16,20},{18,... | collective-permute-start | bytes 884744 | tf_op jit(solution)/shard_map/ppermute | solution.py:22
  37.5 10.2 %collective-permute-start.9 = (bf16[2,48,1536]{2,1,0:T(8,128)(2,1)}, bf16[2,48,1536]{2,1,0:T(8,128)(2,1)}, u32[]{:S(2)}, u32[]{:S(2)}) collective-permute-start(bf16[2,48,1536]{2,1,0:T(8,128)(2,1)} %collective-permute-done.6.rest_5_), channel_id=1, source_target_pairs={{0,2},{2,0},{4,6},{6,4},{8,10},{10,8},{12,14},{14,12},{16,18},{18,... | collective-permute-start | bytes 884744 | tf_op jit(solution)/shard_map/ppermute | solution.py:22
  47.7 20.4 %collective-permute-start.13 = (bf16[2,48,1536]{2,1,0:T(8,128)(2,1)S(1)}, bf16[2,48,1536]{2,1,0:T(8,128)(2,1)S(1)}, u32[]{:S(2)}, u32[]{:S(2)}) collective-permute-start(bf16[2,48,1536]{2,1,0:T(8,128)(2,1)S(1)} %collective-permute-done.7.rest_1_), channel_id=1, source_target_pairs={{0,2},{2,0},{4,6},{6,4},{8,10},{10,8},{12,14},{14,12},{16,18},{18,... | collective-permute-start | bytes 884744 | tf_op jit(solution)/shard_map/ppermute | solution.py:22
  49.4 18.6 %collective-permute-start.14 = (bf16[2,48,1536]{2,1,0:T(8,128)(2,1)S(1)}, bf16[2,48,1536]{2,1,0:T(8,128)(2,1)S(1)}, u32[]{:S(2)}, u32[]{:S(2)}) collective-permute-start(bf16[2,48,1536]{2,1,0:T(8,128)(2,1)S(1)} %collective-permute-done.7.rest_1_), channel_id=1, source_target_pairs={{0,4},{2,6},{4,0},{6,2},{8,12},{10,14},{12,8},{14,10},{16,20},{18,... | collective-permute-start | bytes 884744 | tf_op jit(solution)/shard_map/ppermute | solution.py:22
  50.6 17.5 %collective-permute-start.15 = (bf16[2,48,1536]{2,1,0:T(8,128)(2,1)S(1)}, bf16[2,48,1536]{2,1,0:T(8,128)(2,1)S(1)}, u32[]{:S(2)}, u32[]{:S(2)}) collective-permute-start(bf16[2,48,1536]{2,1,0:T(8,128)(2,1)S(1)} %pad_maximum_fusion.2.rest_0_), channel_id=1, source_target_pairs={{0,8},{2,10},{4,12},{6,14},{8,0},{10,2},{12,4},{14,6},{16,24},{18,... | collective-permute-start | bytes 884744 | tf_op jit(solution)/shard_map/ppermute | solution.py:22
  68.1 16.5 %collective-permute-start.16 = (bf16[1024,768]{1,0:T(8,128)(2,1)S(1)}, bf16[1024,768]{1,0:T(8,128)(2,1)S(1)}, u32[]{:S(2)}, u32[]{:S(2)}) collective-permute-start(bf16[1024,768]{1,0:T(8,128)(2,1)S(1)} %get-tuple-element.201.own_ref), channel_id=1, source_target_pairs={{0,1},{1,0},{2,3},{3,2},{4,5},{5,4},{6,7},{7,6},{8,9},{9,8},{10,11... | collective-permute-start | bytes 4718600 | tf_op jit(solution)/shard_map/ppermute | solution.py:30
  70.2 14.4 %collective-permute-start.19 = (bf16[2,48,1536]{2,1,0:T(8,128)(2,1)S(1)}, bf16[2,48,1536]{2,1,0:T(8,128)(2,1)S(1)}, u32[]{:S(2)}, u32[]{:S(2)}) collective-permute-start(bf16[2,48,1536]{2,1,0:T(8,128)(2,1)S(1)} %pad_maximum_fusion.2.rest_0_), channel_id=1, source_target_pairs={{0,2},{2,0},{4,6},{6,4},{8,10},{10,8},{12,14},{14,12},{16,18},{18,... | collective-permute-start | bytes 884744 | tf_op jit(solution)/shard_map/ppermute | solution.py:22
  71.1 13.4 %collective-permute-start.20 = (bf16[2,48,1536]{2,1,0:T(8,128)(2,1)S(1)}, bf16[2,48,1536]{2,1,0:T(8,128)(2,1)S(1)}, u32[]{:S(2)}, u32[]{:S(2)}) collective-permute-start(bf16[2,48,1536]{2,1,0:T(8,128)(2,1)S(1)} %pad_maximum_fusion.2.rest_0_), channel_id=1, source_target_pairs={{0,4},{2,6},{4,0},{6,2},{8,12},{10,14},{12,8},{14,10},{16,20},{18,... | collective-permute-start | bytes 884744 | tf_op jit(solution)/shard_map/ppermute | solution.py:22
  84.5 10.8 %collective-permute-start.21 = (bf16[2,48,1536]{2,1,0:T(8,128)(2,1)S(1)}, bf16[2,48,1536]{2,1,0:T(8,128)(2,1)S(1)}, u32[]{:S(2)}, u32[]{:S(2)}) collective-permute-start(bf16[2,48,1536]{2,1,0:T(8,128)(2,1)S(1)} %collective-permute-done.15.rest_1_), channel_id=1, source_target_pairs={{0,2},{2,0},{4,6},{6,4},{8,10},{10,8},{12,14},{14,12},{16,18},{18,... | collective-permute-start | bytes 884744 | tf_op jit(solution)/shard_map/ppermute | solution.py:22
  87.5 12.9 %collective-permute-start.23 = (bf16[2,48,1536]{2,1,0:T(8,128)(2,1)S(1)}, bf16[2,48,1536]{2,1,0:T(8,128)(2,1)S(1)}, u32[]{:S(2)}, u32[]{:S(2)}) collective-permute-start(bf16[2,48,1536]{2,1,0:T(8,128)(2,1)S(1)} %collective-permute-done.19.rest_2_), channel_id=1, source_target_pairs={{0,4},{2,6},{4,0},{6,2},{8,12},{10,14},{12,8},{14,10},{16,20},{18,... | collective-permute-start | bytes 884744 | tf_op jit(solution)/shard_map/ppermute | solution.py:22
  134.9 15.5 %collective-permute-start.26 = (bf16[4,48,1536]{2,1,0:T(8,128)(2,1)S(1)}, bf16[4,48,1536]{2,1,0:T(8,128)(2,1)}, u32[]{:S(2)}, u32[]{:S(2)}) collective-permute-start(bf16[4,48,1536]{2,1,0:T(8,128)(2,1)S(1)} %get-tuple-element.234), channel_id=1, source_target_pairs={{0,2},{2,0},{4,6},{6,4},{8,10},{10,8},{12,14},{14,12},{16,18},{18,... | collective-permute-start | bytes 1769480 | tf_op jit(solution)/shard_map/ppermute | solution.py:22
  135.2 15.2 %collective-permute-start.27 = (bf16[4,48,1536]{2,1,0:T(8,128)(2,1)S(1)}, bf16[4,48,1536]{2,1,0:T(8,128)(2,1)}, u32[]{:S(2)}, u32[]{:S(2)}) collective-permute-start(bf16[4,48,1536]{2,1,0:T(8,128)(2,1)S(1)} %get-tuple-element.235), channel_id=1, source_target_pairs={{0,4},{2,6},{4,0},{6,2},{8,12},{10,14},{12,8},{14,10},{16,20},{18,... | collective-permute-start | bytes 1769480 | tf_op jit(solution)/shard_map/ppermute | solution.py:22
  150.4 13.0 %collective-permute-start.28 = (bf16[1024,768]{1,0:T(8,128)(2,1)S(1)}, bf16[1024,768]{1,0:T(8,128)(2,1)S(1)}, u32[]{:S(2)}, u32[]{:S(2)}) collective-permute-start(bf16[1024,768]{1,0:T(8,128)(2,1)S(1)} %get-tuple-element.237.own_ref), channel_id=1, source_target_pairs={{0,1},{1,0},{2,3},{3,2},{4,5},{5,4},{6,7},{7,6},{8,9},{9,8},{10,11... | collective-permute-start | bytes 4718600 | tf_op jit(solution)/shard_map/ppermute | solution.py:30
  151.7 11.3 %collective-permute-start.30 = (bf16[2,48,1536]{2,1,0:T(8,128)(2,1)S(1)}, bf16[2,48,1536]{2,1,0:T(8,128)(2,1)S(1)}, u32[]{:S(2)}, u32[]{:S(2)}) collective-permute-start(bf16[2,48,1536]{2,1,0:T(8,128)(2,1)S(1)} %add_convert_fusion.7), channel_id=1, source_target_pairs={{0,4},{2,6},{4,0},{6,2},{8,12},{10,14},{12,8},{14,10},{16,20},{18,... | collective-permute-start | bytes 884744 | tf_op jit(solution)/shard_map/ppermute | solution.py:22
  163.4 19.4 %collective-permute-start.31 = (bf16[4,48,1536]{2,1,0:T(8,128)(2,1)S(1)}, bf16[4,48,1536]{2,1,0:T(8,128)(2,1)S(1)}, u32[]{:S(2)}, u32[]{:S(2)}) collective-permute-start(bf16[4,48,1536]{2,1,0:T(8,128)(2,1)S(1)} %get-tuple-element.254), channel_id=1, source_target_pairs={{0,2},{2,0},{4,6},{6,4},{8,10},{10,8},{12,14},{14,12},{16,18},{18,... | collective-permute-start | bytes 1769480 | tf_op jit(solution)/shard_map/ppermute | solution.py:22
  164.8 17.9 %collective-permute-start.32 = (bf16[4,48,1536]{2,1,0:T(8,128)(2,1)S(1)}, bf16[4,48,1536]{2,1,0:T(8,128)(2,1)S(1)}, u32[]{:S(2)}, u32[]{:S(2)}) collective-permute-start(bf16[4,48,1536]{2,1,0:T(8,128)(2,1)S(1)} %get-tuple-element.255), channel_id=1, source_target_pairs={{0,4},{2,6},{4,0},{6,2},{8,12},{10,14},{12,8},{14,10},{16,20},{18,... | collective-permute-start | bytes 1769480 | tf_op jit(solution)/shard_map/ppermute | solution.py:22
  167.0 15.7 %collective-permute-start.33 = (bf16[2,48,1536]{2,1,0:T(8,128)(2,1)S(1)}, bf16[2,48,1536]{2,1,0:T(8,128)(2,1)S(1)}, u32[]{:S(2)}, u32[]{:S(2)}) collective-permute-start(bf16[2,48,1536]{2,1,0:T(8,128)(2,1)S(1)} %get-tuple-element.311), channel_id=1, source_target_pairs={{0,8},{2,10},{4,12},{6,14},{8,0},{10,2},{12,4},{14,6},{16,24},{18,... | collective-permute-start | bytes 884744 | tf_op jit(solution)/shard_map/ppermute | solution.py:22
  182.9 10.6 %collective-permute-start.37 = (bf16[2,48,1536]{2,1,0:T(8,128)(2,1)S(1)}, bf16[2,48,1536]{2,1,0:T(8,128)(2,1)S(1)}, u32[]{:S(2)}, u32[]{:S(2)}) collective-permute-start(bf16[2,48,1536]{2,1,0:T(8,128)(2,1)S(1)} %add_convert_fusion.4), channel_id=1, source_target_pairs={{0,4},{2,6},{4,0},{6,2},{8,12},{10,14},{12,8},{14,10},{16,20},{18,... | collective-permute-start | bytes 884744 | tf_op jit(solution)/shard_map/ppermute | solution.py:22
  199.2 14.9 %collective-permute-start.38 = (bf16[4,48,1536]{2,1,0:T(8,128)(2,1)S(1)}, bf16[4,48,1536]{2,1,0:T(8,128)(2,1)S(1)}, u32[]{:S(2)}, u32[]{:S(2)}) collective-permute-start(bf16[4,48,1536]{2,1,0:T(8,128)(2,1)S(1)} %get-tuple-element.280), channel_id=1, source_target_pairs={{0,2},{2,0},{4,6},{6,4},{8,10},{10,8},{12,14},{14,12},{16,18},{18,... | collective-permute-start | bytes 1769480 | tf_op jit(solution)/shard_map/ppermute | solution.py:22
  200.6 14.3 %collective-permute-start.39 = (bf16[4,48,1536]{2,1,0:T(8,128)(2,1)S(1)}, bf16[4,48,1536]{2,1,0:T(8,128)(2,1)S(1)}, u32[]{:S(2)}, u32[]{:S(2)}) collective-permute-start(bf16[4,48,1536]{2,1,0:T(8,128)(2,1)S(1)} %get-tuple-element.281), channel_id=1, source_target_pairs={{0,4},{2,6},{4,0},{6,2},{8,12},{10,14},{12,8},{14,10},{16,20},{18,... | collective-permute-start | bytes 1769480 | tf_op jit(solution)/shard_map/ppermute | solution.py:22
  (71 other events, 540.5 us)

commit v4 on v3

--- a/solution.py
+++ b/solution.py
@@ -24,6 +24,10 @@
 
 def tie(*values):
     return lax.optimization_barrier(values)
+
+
+def after(value, *earlier):
+    return tie(value, *earlier)[0]
 
 
 def pair_swap(partial):
@@ -41,6 +45,28 @@
 
 
 SMEM_SPEC = pl.BlockSpec(memory_space=pltpu.SMEM)
+BIG = 1 << 18
+LIGHT = pl.CostEstimate(flops=1, bytes_accessed=1, transcendentals=0)
+
+
+def call(body, *, out_shape, received=(), **options):
+    def place(member):
+        if member.size * member.dtype.itemsize < BIG:
+            return member
+        return pltpu.HBM(member.shape, member.dtype)
+
+    def keep(member):
+        if member.size * member.dtype.itemsize < BIG:
+            return member
+        return pltpu.with_memory_space_constraint(member, pltpu.HBM)
+
+    kernel = pl.pallas_call(body, out_shape=[place(member) for member in out_shape], **options)
+    return lambda *operands: kernel(
+        *[
+            member if member.ndim == 3 or index in received else keep(member)
+            for index, member in enumerate(operands)
+        ]
+    )
 
 
 def whole(shape):
@@ -140,7 +166,7 @@
     slots = count // lengths.shape[0]
     rows = chains * slots
     shape = jax.ShapeDtypeStruct
-    return pl.pallas_call(
+    return call(
         functools.partial(attend_body, chains, slots),
         grid=(count // rows,),
         in_specs=[SMEM_SPEC, SMEM_SPEC, rows_of(rows, width), whole(bias.shape)]
@@ -160,9 +186,7 @@
             shape((count, width), B16),
         ],
         compiler_params=pltpu.CompilerParams(vmem_limit_bytes=32 * MIB),
-        cost_estimate=pl.CostEstimate(
-            flops=2 * count * width * 4 * heads, bytes_accessed=12 * MIB, transcendentals=0
-        ),
+        cost_estimate=LIGHT,
         name="attend",
     )(me, lengths, in_low, bias, *pieces)
 
@@ -193,8 +217,9 @@
     units = bias.shape[1]
     rows = count // 4
     shape = jax.ShapeDtypeStruct
-    return pl.pallas_call(
+    return call(
         up_body,
+        received=(3,),
         grid=(4,),
         in_specs=[SMEM_SPEC]
         + [rows_of(rows, width)] * 3
@@ -217,9 +242,7 @@
             shape((count, units), B16),
         ],
         compiler_params=pltpu.CompilerParams(vmem_limit_bytes=40 * MIB),
-        cost_estimate=pl.CostEstimate(
-            flops=2 * count * width * units, bytes_accessed=20 * MIB, transcendentals=0
-        ),
+        cost_estimate=LIGHT,
         name="up",
     )(me, in_low, own, other, vectors, bias, *pieces)
 
@@ -239,16 +262,14 @@
     width = BLOCKS * pieces[0].shape[1]
     rows = count // 4
     shape = jax.ShapeDtypeStruct
-    return pl.pallas_call(
+    return call(
         down_body,
         grid=(4,),
         in_specs=[SMEM_SPEC, rows_of(rows, units)] + [whole(piece.shape) for piece in pieces],
         out_specs=[whole((width, units)), rows_of(rows, width)],
         out_shape=[shape((width, units), B16), shape((count, width), B16)],
         compiler_params=pltpu.CompilerParams(vmem_limit_bytes=24 * MIB),
-        cost_estimate=pl.CostEstimate(
-            flops=2 * count * width * units, bytes_accessed=8 * MIB, transcendentals=0
-        ),
+        cost_estimate=LIGHT,
         name="down",
     )(me, act, *pieces)
 
@@ -277,8 +298,9 @@
     count, width = own.shape
     rows = count // 4
     shape = jax.ShapeDtypeStruct
-    return pl.pallas_call(
+    return call(
         second_norm_body,
+        received=(2,),
         grid=(4,),
         in_specs=[rows_of(rows, width)] * 4 + [whole(vectors.shape)],
         out_specs=[rows_of(rows, width)] * 3 + [whole((8, width))],
@@ -289,7 +311,7 @@
             shape((8, width), F32),
         ],
         compiler_params=pltpu.CompilerParams(vmem_limit_bytes=24 * MIB),
-        cost_estimate=pl.CostEstimate(flops=40 * count * width, bytes_accessed=14 * MIB, transcendentals=0),
+        cost_estimate=LIGHT,
         name="second_norm",
     )(normed, own, other, grad, vectors)
 
@@ -357,7 +379,7 @@
         return pl.BlockSpec((number, rows, tile), lambda i: (0, 0, i))
 
     sizes = (4, 4, 2, 2, 4)
-    return pl.pallas_call(
+    return call(
         body,
         grid=(total,),
         in_specs=[SMEM_SPEC]
@@ -367,9 +389,7 @@
         out_shape=[shape((number, rows, total * tile), B16) for number in sizes],
         scratch_shapes=[pltpu.VMEM((width, count), B16), pltpu.VMEM((width, tile), B16)],
         compiler_params=pltpu.CompilerParams(vmem_limit_bytes=28 * MIB),
-        cost_estimate=pl.CostEstimate(
-            flops=2 * count * width * total * tile, bytes_accessed=9 * MIB, transcendentals=0
-        ),
+        cost_estimate=LIGHT,
         name="weight_grad",
     )(me, *lefts, *rights)
 
@@ -391,7 +411,7 @@
     units = slope.shape[1]
     rows = count // 4
     shape = jax.ShapeDtypeStruct
-    return pl.pallas_call(
+    return call(
         hidden_back_body,
         grid=(4,),
         in_specs=[
@@ -407,9 +427,7 @@
             shape((8, units), F32),
         ],
         compiler_params=pltpu.CompilerParams(vmem_limit_bytes=28 * MIB),
-        cost_estimate=pl.CostEstimate(
-            flops=4 * count * width * units, bytes_accessed=12 * MIB, transcendentals=0
-        ),
+        cost_estimate=LIGHT,
         name="hidden_back",
     )(dz_low, slope, w_down_t, w_up)
 
@@ -471,8 +489,9 @@
     slots = count // chain_count
     rows = chains * slots
     shape = jax.ShapeDtypeStruct
-    return pl.pallas_call(
+    return call(
         functools.partial(attend_back_body, chains, slots),
+        received=(2,),
         grid=(count // rows,),
         in_specs=[
             rows_of(rows, width),
@@ -503,48 +522,98 @@
         ],
         scratch_shapes=[pltpu.VMEM((rows, heads), B16)],
         compiler_params=pltpu.CompilerParams(vmem_limit_bytes=32 * MIB),
-        cost_estimate=pl.CostEstimate(
-            flops=2 * count * width * 6 * heads, bytes_accessed=20 * MIB, transcendentals=0
-        ),
+        cost_estimate=LIGHT,
         name="attend_back",
     )(dz_two, own, other, normed, inverse, gain, qkv, prob, w_a)
 
 
-def last_body(dz_ref, own_ref, other_ref, flag_ref, out_ref, sum_ref):
+def last_body(dz_ref, own_ref, other_ref, flag_ref, one_ref, two_ref, up_ref, qkv_ref, out_ref, sum_ref):
     total = dz_ref[...] + (own_ref[...].astype(F32) + other_ref[...].astype(F32))
     flag = flag_ref[:, 0:1]
     masked = total * flag
+    width = total.shape[1]
+    heads = qkv_ref.shape[1] // 3
 
     @pl.when(pl.program_id(0) == 0)
     def _():
         sum_ref[...] = jnp.zeros_like(sum_ref)
+        sum_ref[1:4] = one_ref[0:3]
+        sum_ref[4:7] = two_ref[0:3]
+        sum_ref[7:8, :heads] = qkv_ref[0:1, :heads]
+        sum_ref[7:8, heads : 2 * heads] = qkv_ref[0:1, 2 * heads :]
+        for k in range(up_ref.shape[1] // width):
+            sum_ref[8 + k : 9 + k] = up_ref[0:1, k * width : (k + 1) * width]
 
     sum_ref[0:1] += col_sum(masked)
     out_ref[...] = total - masked
 
 
-def last(dz_one, own, other, flag):
+def last(dz_one, own, other, flag, sums_one, sums_two, sums_up, sums_qkv):
     count, width = dz_one.shape
     rows = count // 4
+    sums = [sums_one, sums_two, sums_up, sums_qkv]
     shape = jax.ShapeDtypeStruct
+    joined = (8 + 8 * pl.cdiv(sums_up.shape[1], 8 * width), width)
+    return call(
+        last_body,
+        received=(2,),
+        grid=(4,),
+        in_specs=[rows_of(rows, width)] * 3
+        + [rows_of(rows, 128)]
+        + [whole(member.shape) for member in sums],
+        out_specs=[rows_of(rows, width), whole(joined)],
+        out_shape=[shape((count, width), F32), shape(joined, F32)],
+        compiler_params=pltpu.CompilerParams(vmem_limit_bytes=20 * MIB),
+        cost_estimate=LIGHT,
+        name="last",
+    )(dz_one, own, other, flag, *sums)
+
+
+def add_late_body(x_ref, y_ref, from_x_ref, from_y_ref, out_x_ref, out_y_ref):
+    out_x_ref[...] = (x_ref[...].astype(F32) + from_y_ref[:2].astype(F32)).astype(B16)
+    out_y_ref[...] = (y_ref[...].astype(F32) + from_x_ref[:2].astype(F32)).astype(B16)
+
+
+def add_own_body(own_ref, from_x_ref, from_y_ref, late_x_ref, late_y_ref, near_ref, mid_ref):
+    near_ref[...] = (
+        own_ref[:2].astype(F32) + from_x_ref[2:].astype(F32) + late_y_ref[...].astype(F32)
+    )
+    mid_ref[...] = (
+        own_ref[2:].astype(F32) + late_x_ref[...].astype(F32) + from_y_ref[2:].astype(F32)
+    ).astype(B16)
+
+
+def add_mid_body(near_ref, mid_ref, own_ref, far_ref):
+    own_ref[...] = near_ref[0] + mid_ref[0].astype(F32)
+    far_ref[...] = (near_ref[1] + mid_ref[1].astype(F32)).astype(B16)
+
+
+def add_up(body, name, shapes, *operands):
+    vmem = pl.BlockSpec(memory_space=pltpu.VMEM)
     return pl.pallas_call(
-        last_body,
-        grid=(4,),
-        in_specs=[rows_of(rows, width)] * 3 + [rows_of(rows, 128)],
-        out_specs=[rows_of(rows, width), whole((8, width))],
-        out_shape=[shape((count, width), F32), shape((8, width), F32)],
-        compiler_params=pltpu.CompilerParams(vmem_limit_bytes=20 * MIB),
-        cost_estimate=pl.CostEstimate(flops=10 * count * width, bytes_accessed=10 * MIB, transcendentals=0),
-        name="last",
-    )(dz_one, own, other, flag)
-
-
-def near_total(own, from_x, from_y):
-    return own[:2].astype(F32) + from_x.astype(F32) + from_y.astype(F32)
-
-
-def add_low(left, right):
-    return (left.astype(F32) + right.astype(F32)).astype(B16)
+        body,
+        in_specs=[vmem] * len(operands),
+        out_specs=[vmem] * len(shapes),
+        out_shape=[jax.ShapeDtypeStruct(shape, dtype) for shape, dtype in shapes],
+        compiler_params=pltpu.CompilerParams(vmem_limit_bytes=8 * MIB),
+        cost_estimate=LIGHT,
+        name=name,
+    )(*operands)
+
+
+def add_late(late_x, late_y, from_x, from_y):
+    shape = (late_x.shape, B16)
+    return add_up(add_late_body, "add_late", [shape, shape], late_x, late_y, from_x, from_y)
+
+
+def add_own(own, from_x, from_y, late_x, late_y):
+    shapes = [(late_x.shape, F32), (late_x.shape, B16)]
+    return add_up(add_own_body, "add_own", shapes, own, from_x, from_y, late_x, late_y)
+
+
+def add_mid(near, mid):
+    shapes = [(near.shape[1:], F32), (near.shape[1:], B16)]
+    return add_up(add_mid_body, "add_mid", shapes, near, mid)
 
 
 def per_device(dp_size, tokens, masked, lengths, mask_vector, w_query, b_query, w_key, w_value,
@@ -573,48 +642,40 @@
     d = w_down.T
     if fast:
         az = swap(a, 12)
-        a, az, c = tie(a, az, c)
         an = jnp.stack([a, az])
-        am, anx, any_ = swap(an, 4), swap(an, 1), swap(an, 2)
-        cz = swap(c, 12)
-        an, am, anx, any_, c, cz, d = tie(an, am, anx, any_, c, cz, d)
+        anx, any_, am = swap(an, 1), swap(an, 2), swap(an, 4)
+        cz = swap(after(c, az), 12)
+        amx, amy = swap(am, 1), swap(am, 2)
         cn = jnp.stack([c, cz])
-        amx, amy = swap(am, 1), swap(am, 2)
-        cm = swap(cn, 4)
-        an, am, anx, any_, amx, amy, cn, cm, d = tie(an, am, anx, any_, amx, amy, cn, cm, d)
-        and_, amd = swap(anx, 2), swap(amy, 1)
-        cnx, cny = swap(cn, 1), swap(cn, 2)
-        dz = swap(d, 12)
-        an, am, anx, any_, amx, amy, and_, amd, cn, cm, cnx, cny, d, dz = tie(
-            an, am, anx, any_, amx, amy, and_, amd, cn, cm, cnx, cny, d, dz
+        cm = swap(after(cn, am), 4)
+        cnx, cny = swap(after(cn, anx), 1), swap(after(cn, any_), 2)
+        dz = swap(after(d, cz), 12)
+        dn = jnp.stack([d, dz])
+        amd, and_ = swap(amy, 1), swap(after(anx, amy), 2)
+        in_low, an, am, anx, amx, any_, amy, and_, amd, cn, cm, cnx, cny, dn = tie(
+            in_low, an, am, anx, amx, any_, amy, and_, amd, cn, cm, cnx, cny, dn
         )
-        dn = jnp.stack([d, dz])
-        cmx, cmy = swap(cm, 1), swap(cm, 2)
-        dm = swap(dn, 4)
         pieces_a = [an, am, anx, amx, any_, amy, and_, amd]
+        cmx, cmy, dm = swap(cm, 1), swap(cm, 2), swap(dn, 4)
+        dnx, cnd = swap(dn, 1), swap(cnx, 2)
     else:
         a, c, d = (lax.all_gather(piece, "dp", axis=0, tiled=True) for piece in (a, c, d))
         pieces_a, pieces_c, pieces_d = as_pieces(a), as_pieces(c), as_pieces(d)
     w_a, qkv, prob, attended, part = attend(me, lengths, in_low, bias_qkv, pieces_a)
     if fast:
-        part, cn, cm, cnx, cny, cmx, cmy, dn, dm = tie(part, cn, cm, cnx, cny, cmx, cmy, dn, dm)
-        other = pair_swap(part)
-        cnd, cmd = swap(cnx, 2), swap(cmy, 1)
-        dnx, dny = swap(dn, 1), swap(dn, 2)
-        other, part, cnd, cmd, cn, cm, cnx, cny, cmx, cmy, dn, dm, dnx, dny = tie(
-            other, part, cnd, cmd, cn, cm, cnx, cny, cmx, cmy, dn, dm, dnx, dny
-        )
+        part, cmx, cmy, cnd, dn, dm, dnx = tie(part, cmx, cmy, cnd, dn, dm, dnx)
+        cmd, dny = swap(cmy, 1), swap(dn, 2)
+    other = pair_swap(part)
+    if fast:
+        other, cmd, dny, dm = tie(other, cmd, dny, dm)
+        pieces_c = [cn, cm, cnx, cmx, cny, cmy, cnd, cmd]
         dmx, dmy = swap(dm, 1), swap(dm, 2)
-        dnd = swap(dnx, 2)
-        pieces_c = [cn, cm, cnx, cmx, cny, cmy, cnd, cmd]
-    else:
-        other = pair_swap(part)
     w_u, normed_one, inverse_one, hidden_low, act_low, slope = up(
         me, in_low, part, other, vectors_one, b_up[None, :], pieces_c
     )
     if fast:
-        act_low, dmx, dmy, dnd = tie(act_low, dmx, dmy, dnd)
-        dmd = swap(dmy, 1)
+        act_low, dnx, dmx, dmy = tie(act_low, dnx, dmx, dmy)
+        dmd, dnd = swap(dmy, 1), swap(dnx, 2)
         pieces_d = [dn, dm, dnx, dmx, dny, dmy, dnd, dmd]
     w_d, part = down(me, act_low, pieces_d)
     other = pair_swap(part)
@@ -624,70 +685,50 @@
         dx, dy, dxl, dyl, dz_two_low = tie(dx, dy, dxl, dyl, dz_two_low)
         dxr, dyr = swap(dx, 1), swap(dy, 2)
     d_pre_low, part, sums_up = hidden_back(dz_two_low, slope, w_d, w_u)
-    if fast:
-        part, dxr, dyr, d_pre_low = tie(part, dxr, dyr, d_pre_low)
-        other = pair_swap(part)
-        dxlr, dylr = swap(add_low(dxl, dyr[:2]), 1), swap(add_low(dyl, dxr[:2]), 2)
-        cx, cy, cxl, cyl, co = weight_grad(me, [hidden_low], [d_pre_low])
-        other, dxlr, dylr, cx, cy = tie(other, dxlr, dylr, cx, cy)
-        cxr, cyr = swap(cx, 1), swap(cy, 2)
-        d_mid = (do[2:].astype(F32) + dxlr.astype(F32) + dyr[2:].astype(F32)).astype(B16)
-        d_near = do[:2].astype(F32) + dxr[2:].astype(F32) + dylr.astype(F32)
-        d_midr = swap(d_mid, 4)
-    else:
-        other = pair_swap(part)
-        cx, cy, cxl, cyl, co = weight_grad(me, [hidden_low], [d_pre_low])
+    cx, cy, cxl, cyl, co = weight_grad(me, [hidden_low], [d_pre_low])
+    if fast:
+        part, dxr, dyr, cx, cy = tie(part, dxr, dyr, cx, cy)
+        dxl, dyl = add_late(dxl, dyl, dxr, dyr)
+        dxlr, dylr, cxr, cyr = swap(dxl, 1), swap(dyl, 2), swap(cx, 1), swap(cy, 2)
+    other = pair_swap(part)
     dz_one, dz_one_low, d_qkv, part, sums_one, sums_qkv = attend_back(
         lengths.shape[0], dz_two, part, other, normed_one, inverse_one, gain_one[None, :], qkv, prob, w_a
     )
     if fast:
-        part, d_qkv, cxr, cyr, d_midr, d_near = tie(part, d_qkv, cxr, cyr, d_midr, d_near)
-        other = pair_swap(part)
-        d_near = d_near + d_midr.astype(F32)
-        d_far = swap(d_near[1].astype(B16), 12)
-        cxlr, cylr = swap(add_low(cxl, cyr[:2]), 1), swap(add_low(cyl, cxr[:2]), 2)
-        ax, ay, axl, ayl, ao = weight_grad(me, [in_low, dz_one_low], [d_qkv, attended])
-        other, d_far, cxlr, cylr, ax, ay = tie(other, d_far, cxlr, cylr, ax, ay)
+        part, d_qkv, dxlr, dylr, cxr, cyr = tie(part, d_qkv, dxlr, dylr, cxr, cyr)
+        cxl, cyl = add_late(cxl, cyl, cxr, cyr)
+        cxlr, cylr = swap(cxl, 1), swap(cyl, 2)
+        d_near, d_mid = add_own(do, dxr, dyr, dxlr, dylr)
+        d_midr = swap(d_mid, 4)
+    other = pair_swap(part)
+    ax, ay, axl, ayl, ao = weight_grad(me, [in_low, dz_one_low], [d_qkv, attended])
+    if fast:
+        other, ax, ay, cxlr, cylr, d_midr = tie(other, ax, ay, cxlr, cylr, d_midr)
         axr, ayr = swap(ax, 1), swap(ay, 2)
-        c_mid = (co[2:].astype(F32) + cxlr.astype(F32) + cyr[2:].astype(F32)).astype(B16)
-        c_near = co[:2].astype(F32) + cxr[2:].astype(F32) + cylr.astype(F32)
+        c_near, c_mid = add_own(co, cxr, cyr, cxlr, cylr)
         c_midr = swap(c_mid, 4)
-    else:
-        other = pair_swap(part)
-        ax, ay, axl, ayl, ao = weight_grad(me, [in_low, dz_one_low], [d_qkv, attended])
-    d_tokens, sums_mask = last(dz_one, part, other, flag)
-    parts = (
-        sums_mask[0],
-        sums_qkv[0, :head_cols],
-        sums_qkv[0, 2 * head_cols :],
-        sums_one[2],
-        sums_one[0],
-        sums_one[1],
-        sums_up[0],
-        sums_two[2],
-        sums_two[0],
-        sums_two[1],
-    )
-    joined = jnp.concatenate(parts).reshape(-1, 128)
-    if fast:
-        joined, axr, ayr, c_midr, c_near = tie(joined, axr, ayr, c_midr, c_near)
-        axlr, aylr = swap(add_low(axl, ayr[:2]), 1), swap(add_low(ayl, axr[:2]), 2)
-        c_near = c_near + c_midr.astype(F32)
-        c_far = swap(c_near[1].astype(B16), 12)
+        d_near, d_far = add_mid(d_near, d_midr)
+        d_farr = swap(d_far, 12)
+        other, axr, ayr, c_midr, d_farr = tie(other, axr, ayr, c_midr, d_farr)
+        axl, ayl = add_late(axl, ayl, axr, ayr)
+        axlr, aylr = swap(axl, 1), swap(ayl, 2)
+        c_near, c_far = add_mid(c_near, c_midr)
+        c_farr = swap(c_far, 12)
+        d_w_down_t = d_near + d_farr.astype(F32)
+    d_tokens, joined = last(dz_one, part, other, flag, sums_one, sums_two, sums_up, sums_qkv)
+    if fast:
+        axlr, aylr, c_farr, joined = tie(axlr, aylr, c_farr, joined)
+        a_near, a_mid = add_own(ao, axr, ayr, axlr, aylr)
+        a_midr = swap(a_mid, 4)
         joined = joined + swap(joined, 1)
         joined = joined + swap(joined, 2)
-        axlr, aylr, c_far, joined = tie(axlr, aylr, c_far, joined)
-        a_mid = (ao[2:].astype(F32) + axlr.astype(F32) + ayr[2:].astype(F32)).astype(B16)
-        a_near = ao[:2].astype(F32) + axr[2:].astype(F32) + aylr.astype(F32)
-        a_midr = swap(a_mid, 4)
+        d_w_up = c_near + c_farr.astype(F32)
+        a_midr, joined = tie(a_midr, joined)
+        a_near, a_far = add_mid(a_near, a_midr)
+        a_farr = swap(a_far, 12)
         joined = joined + swap(joined, 4)
-        a_midr, joined = tie(a_midr, joined)
-        a_near = a_near + a_midr.astype(F32)
-        a_far = swap(a_near[1].astype(B16), 12)
         joined = joined + swap(joined, 8)
-        d_wa = a_near[0] + a_far.astype(F32)
-        d_w_up = c_near[0] + c_far.astype(F32)
-        d_w_down_t = d_near[0] + d_far.astype(F32)
+        d_wa = a_near + a_farr.astype(F32)
     else:
         full = []
         for x, y, xl, yl, o in ((ax, ay, axl, ayl, ao), (cx, cy, cxl, cyl, co), (dx, dy, dxl, dyl, do)):
@@ -701,31 +742,26 @@
         d_wa, d_w_up, d_w_down_t = (
             lax.psum_scatter(member, "dp", scatter_dimension=0, tiled=True) for member in full
         )
-    joined = joined.reshape(-1)
-    summed = []
-    start = 0
-    for member in parts:
-        summed.append(joined[start : start + member.shape[0]])
-        start += member.shape[0]
+    units = w_up.shape[1]
     return (
         result,
         d_tokens,
-        summed[0],
+        joined[0],
         d_wa[:, :head_cols],
-        summed[1],
+        joined[7, :head_cols],
         d_wa[:, head_cols : 2 * head_cols],
         d_wa[:, 2 * head_cols : 3 * head_cols],
-        summed[2],
+        joined[7, head_cols : 2 * head_cols],
         d_wa[:, 3 * head_cols :].T,
-        summed[3],
-        summed[4],
-        summed[5],
+        joined[3],
+        joined[1],
+        joined[2],
         d_w_up,
-        summed[6],
+        joined[8:].reshape(-1)[:units],
         d_w_down_t.T,
-        summed[7],
-        summed[8],
-        summed[9],
+        joined[6],
+        joined[4],
+        joined[5],
     )
 
 

time: 244 us -> 228 us (0.934)
  Pallas kernels: 68.2 us -> 90.6 us
  waiting for transfers between devices: 74.6 us -> 58.4 us
  local copies, waits for them, and re-layouts: 23 us -> 8.82 us
  other arithmetic: 11 us -> 4.89 us
    pallas_call x10 -> x19, Pallas kernels: 68.2 us -> 90.6 us  [the longest x10 89.4 us: call(): kernel(*[member if member.ndim == 3 or index in received else keep(member...]
    ppermute x46, waiting for transfers between devices: 70.9 us -> 54.9 us  [swap(): return lax.ppermute(values, 'dp', [(i, i ^ bit) for i in range(BLOCKS)])]
    unnamed x99 -> x60, local copies, waits for them, and re-layouts: 20 us -> 5.13 us
    convert_element_type x7 -> x0, other arithmetic: 2.65 us -> none  [the longest x6 2.55 us: add_low(): return (left.astype(F32) + right.astype(F32)).astype(B16)]
  transfers between devices with their start and end apart: 50 -> 50, of which waited for: 26 -> 21; matrix products, arithmetic and copies ran while one was open for 5% -> 3% of each run, Pallas kernels for 22% -> 31%
where the time goes in v4:
time: 228 us; the launch traced here: 227 us
  Pallas kernels  90.6 us (40%)
  starting transfers between devices  62.8 us (28%)
  waiting for transfers between devices  58.4 us (26%)
  local copies, waits for them, and re-layouts  8.82 us (4%)
  other arithmetic  4.89 us (2%)
    pallas_call x10, Pallas kernels, call(): kernel(*[member if member.ndim == 3 or index in received else keep(member...  89.4 us
    ppermute x46, starting transfers between devices, swap(): return lax.ppermute(values, 'dp', [(i, i ^ bit) for i in range(BLOCKS)])  62.7 us
    ppermute x46, waiting for transfers between devices, swap(): return lax.ppermute(values, 'dp', [(i, i ^ bit) for i in range(BLOCKS)])  54.9 us
    unnamed x60, local copies, waits for them, and re-layouts  5.13 us
  transfers between devices with their start and end apart: 50, of which 21 were waited for; matrix products, arithmetic and copies ran while one was open for 3% of the time, Pallas kernels for 31%

profile of v4, /device:TPU:0, one launch (start us, length us, event | category | flops | bytes accessed | tf_op | source)
XLA Modules:
  0.0 226.7 jit_solution(10377513190811882445)
XLA Ops:
  1.7 5.1 %collective-permute-start = (bf16[48,1536]{1,0:T(8,128)(2,1)S(1)}, bf16[48,1536]{1,0:T(8,128)(2,1)S(1)}, u32[]{:S(2)}, u32[]{:S(2)}) collective-permute-start(bf16[48,1536]{1,0:T(8,128)(2,1)S(1)} %get-tuple-element.292), channel_id=1, source_target_pairs={{0,24},{2,26},{4,28},{6,30},{8,16},{10,18},{12,20},{14,22},{16,8},... | collective-permute-start | bytes 442376 | tf_op jit(solution)/shard_map/ppermute | solution.py:22
  6.8 4.0 %collective-permute-done = bf16[48,1536]{1,0:T(8,128)(2,1)S(1)} collective-permute-done((bf16[48,1536]{1,0:T(8,128)(2,1)S(1)}, bf16[48,1536]{1,0:T(8,128)(2,1)S(1)}, u32[]{:S(2)}, u32[]{:S(2)}) %collective-permute-start) | collective-permute-done | bytes 147488 | tf_op jit(solution)/shard_map/ppermute | solution.py:22
  10.8 2.8 %collective-permute-start.1 = (bf16[2,48,1536]{2,1,0:T(8,128)(2,1)S(1)}, bf16[2,48,1536]{2,1,0:T(8,128)(2,1)S(1)}, u32[]{:S(2)}, u32[]{:S(2)}) collective-permute-start(bf16[2,48,1536]{2,1,0:T(8,128)(2,1)S(1)} %pad_maximum_fusion.rest_0_), channel_id=1, source_target_pairs={{0,8},{2,10},{4,12},{6,14},{8,0},{10,2},{12,4},{14,6},{16,24},{18,... | collective-permute-start | bytes 884744 | tf_op jit(solution)/shard_map/ppermute | solution.py:22
  13.6 2.5 %collective-permute-start.8 = (bf16[48,1536]{1,0:T(8,128)(2,1)}, bf16[48,1536]{1,0:T(8,128)(2,1)S(1)}, u32[]{:S(2)}, u32[]{:S(2)}) collective-permute-start(bf16[48,1536]{1,0:T(8,128)(2,1)} %param.33), channel_id=1, source_target_pairs={{0,24},{2,26},{4,28},{6,30},{8,16},{10,18},{12,20},{14,22},{16,8},... | collective-permute-start | bytes 442376 | tf_op jit(solution)/shard_map/ppermute | solution.py:22
  32.4 3.5 %collective-permute-done.12 = bf16[48,1536]{1,0:T(8,128)(2,1)S(1)} collective-permute-done((bf16[48,1536]{1,0:T(8,128)(2,1)}, bf16[48,1536]{1,0:T(8,128)(2,1)S(1)}, u32[]{:S(2)}, u32[]{:S(2)}) %collective-permute-start.12) | collective-permute-done | bytes 147488 | tf_op jit(solution)/shard_map/ppermute | solution.py:22
  40.4 3.6 %collective-permute-done.3.rest_3_ = bf16[2,48,1536]{2,1,0:T(8,128)(2,1)S(1)} collective-permute-done((bf16[2,48,1536]{2,1,0:T(8,128)(2,1)S(1)}, bf16[2,48,1536]{2,1,0:T(8,128)(2,1)S(1)}, u32[]{:S(2)}, u32[]{:S(2)}) %collective-permute-start.3) | collective-permute-done | bytes 294944 | tf_op jit(solution)/shard_map/ppermute | solution.py:22
  55.7 8.7 %attend.1 = (bf16[768,1536]{1,0:T(8,128)(2,1)}, bf16[1024,1152]{1,0:T(8,128)(2,1)}, bf16[1024,768]{1,0:T(8,128)(2,1)}, bf16[1024,384]{1,0:T(8,128)(2,1)}, bf16[1024,768]{1,0:T(8,128)(2,1)}) custom-call(s32[1]{0:T(128)} %bitcast.me_ref, s32[8]{0:T(128)S(1)} %copy-done.15, bf16[1024,768]{1,0:T(8,128)(2,1)} %broadcast_select_fusion.in_ref.refs_0_, ...), custom_call_target="tpu_custom_call" | custom-call | flops 1 | bytes 1 | tf_op jit(solution)/shard_map/attend/pallas_call | solution.py:64
  67.8 6.4 %collective-permute-done.19.rest_7_ = bf16[2,48,1536]{2,1,0:T(8,128)(2,1)S(1)} collective-permute-done((bf16[2,48,1536]{2,1,0:T(8,128)(2,1)}, bf16[2,48,1536]{2,1,0:T(8,128)(2,1)S(1)}, u32[]{:S(2)}, u32[]{:S(2)}) %collective-permute-start.19) | collective-permute-done | bytes 294944 | tf_op jit(solution)/shard_map/ppermute | solution.py:22
  77.5 9.2 %up.1 = (bf16[768,1536]{1,0:T(8,128)(2,1)}, f32[1024,768]{1,0:T(8,128)}, f32[1024,128]{1,0:T(8,128)}, bf16[1024,768]{1,0:T(8,128)(2,1)}, bf16[1024,1536]{1,0:T(8,128)(2,1)}, /*index=5*/bf16[1024,1536]{1,0:T(8,128)(2,1)}) custom-call(s32[1]{0:T(128)} %bitcast.me_ref, bf16[1024,768]{1,0:T(8,128)(2,1)} %broadcast_select_fusion.in_ref.refs_0_, ...), custom_call_target="tpu_custom_call" | custom-call | flops 1 | bytes 1 | tf_op jit(solution)/shard_map/up/pallas_call | solution.py:64
  88.6 6.2 %collective-permute-done.23.rest_6_ = bf16[2,48,1536]{2,1,0:T(8,128)(2,1)S(1)} collective-permute-done((bf16[2,48,1536]{2,1,0:T(8,128)(2,1)S(1)}, bf16[2,48,1536]{2,1,0:T(8,128)(2,1)S(1)}, u32[]{:S(2)}, u32[]{:S(2)}) %collective-permute-start.23) | collective-permute-done | bytes 294944 | tf_op jit(solution)/shard_map/ppermute | solution.py:22
  94.9 5.9 %down.1 = (bf16[768,1536]{1,0:T(8,128)(2,1)}, bf16[1024,768]{1,0:T(8,128)(2,1)}) custom-call(s32[1]{0:T(128)} %bitcast.me_ref, bf16[1024,1536]{1,0:T(8,128)(2,1)} %get-tuple-element.180.act_ref.refs_1_, bf16[2,48,1536]{2,1,0:T(8,128)(2,1)S(1)} %pad_maximum_fusion.2.rest_0_, bf16[2,48,1536]{2,1,0:T(8,128)(2,1)S(1)} %collective-permute-done.16.rest_1_, ...), custom_call_target="tpu_custom_call" | custom-call | flops 1 | bytes 1 | tf_op jit(solution)/shard_map/down/pallas_call | solution.py:64
  100.9 3.5 %collective-permute-done.25.other_ref = bf16[1024,768]{1,0:T(8,128)(2,1)S(1)} collective-permute-done((bf16[1024,768]{1,0:T(8,128)(2,1)}, bf16[1024,768]{1,0:T(8,128)(2,1)S(1)}, u32[]{:S(2)}, u32[]{:S(2)}) %collective-permute-start.25) | collective-permute-done | bytes 1572896 | tf_op jit(solution)/shard_map/ppermute | solution.py:34
  104.4 7.0 %second_norm.1 = (bf16[1024,768]{1,0:T(8,128)(2,1)}, f32[1024,768]{1,0:T(8,128)}, bf16[1024,768]{1,0:T(8,128)(2,1)}, f32[8,768]{1,0:T(8,128)S(1)}) custom-call(f32[1024,768]{1,0:T(8,128)} %get-tuple-element.176.normed_ref, bf16[1024,768]{1,0:T(8,128)(2,1)} %get-tuple-element.185.own_ref, bf16[1024,768]{1,0:T(8,128)(2,1)S(1)} %collective-permute-done.25.other_ref, ...), custom_call_target="tpu_custom_call" | custom-call | flops 1 | bytes 1 | tf_op jit(solution)/shard_map/second_norm/pallas_call | solution.py:64
  111.4 7.5 %weight_grad.3 = (bf16[4,48,1536]{2,1,0:T(8,128)(2,1)}, bf16[4,48,1536]{2,1,0:T(8,128)(2,1)}, bf16[2,48,1536]{2,1,0:T(8,128)(2,1)}, bf16[2,48,1536]{2,1,0:T(8,128)(2,1)}, bf16[4,48,1536]{2,1,0:T(8,128)(2,1)}) custom-call(s32[1]{0:T(128)} %bitcast.me_ref, bf16[1024,768]{1,0:T(8,128)(2,1)} %get-tuple-element.193.refs_0_.low_ref, ...), custom_call_target="tpu_custom_call" | custom-call | flops 1 | bytes 1 | tf_op jit(solution)/shard_map/weight_grad/pallas_call | solution.py:64
  121.8 11.6 %hidden_back.1 = (bf16[1024,1536]{1,0:T(8,128)(2,1)}, bf16[1024,768]{1,0:T(8,128)(2,1)}, f32[8,1536]{1,0:T(8,128)S(1)}) custom-call(bf16[1024,768]{1,0:T(8,128)(2,1)} %get-tuple-element.193.refs_0_.low_ref, bf16[1024,1536]{1,0:T(8,128)(2,1)} %get-tuple-element.194.slope_ref, bf16[768,1536]{1,0:T(8,128)(2,1)} %get-tuple-element.195.down_ref, ...), custom_call_target="tpu_custom_call" | custom-call | flops 1 | bytes 1 | tf_op jit(solution)/shard_map/hidden_back/pallas_call | solution.py:64
  133.5 7.6 %weight_grad.4 = (bf16[4,48,1536]{2,1,0:T(8,128)(2,1)}, bf16[4,48,1536]{2,1,0:T(8,128)(2,1)}, bf16[2,48,1536]{2,1,0:T(8,128)(2,1)}, bf16[2,48,1536]{2,1,0:T(8,128)(2,1)}, bf16[4,48,1536]{2,1,0:T(8,128)(2,1)}) custom-call(s32[1]{0:T(128)} %bitcast.me_ref, bf16[1024,768]{1,0:T(8,128)(2,1)} %get-tuple-element.200.refs_0_, ...), custom_call_target="tpu_custom_call" | custom-call | flops 1 | bytes 1 | tf_op jit(solution)/shard_map/weight_grad/pallas_call | solution.py:64
  145.5 18.1 %attend_back.1 = (f32[1024,768]{1,0:T(8,128)}, bf16[1024,768]{1,0:T(8,128)(2,1)}, bf16[1024,1152]{1,0:T(8,128)(2,1)}, bf16[1024,768]{1,0:T(8,128)(2,1)}, f32[8,768]{1,0:T(8,128)S(1)}, /*index=5*/f32[8,1152]{1,0:T(8,128)S(1)}) custom-call(f32[1024,768]{1,0:T(8,128)} %get-tuple-element.187.dz_ref, bf16[1024,768]{1,0:T(8,128)(2,1)} %get-tuple-element.204.own_ref, ...), custom_call_target="tpu_custom_call" | custom-call | flops 1 | bytes 1 | tf_op jit(solution)/shard_map/attend_back/pallas_call | solution.py:64
  167.1 8.8 %weight_grad.5 = (bf16[4,48,1536]{2,1,0:T(8,128)(2,1)}, bf16[4,48,1536]{2,1,0:T(8,128)(2,1)}, bf16[2,48,1536]{2,1,0:T(8,128)(2,1)}, bf16[2,48,1536]{2,1,0:T(8,128)(2,1)}, bf16[4,48,1536]{2,1,0:T(8,128)(2,1)}) custom-call(s32[1]{0:T(128)} %bitcast.me_ref, bf16[1024,768]{1,0:T(8,128)(2,1)} %broadcast_select_fusion.in_ref.refs_0_, ...), custom_call_target="tpu_custom_call" | custom-call | flops 1 | bytes 1 | tf_op jit(solution)/shard_map/weight_grad/pallas_call | solution.py:64
  180.8 9.1 %collective-permute-done.40 = bf16[48,1536]{1,0:T(8,128)(2,1)S(1)} collective-permute-done((bf16[48,1536]{1,0:T(8,128)(2,1)S(1)}, bf16[48,1536]{1,0:T(8,128)(2,1)S(1)}, u32[]{:S(2)}, u32[]{:S(2)}) %collective-permute-start.40) | collective-permute-done | bytes 147488 | tf_op jit(solution)/shard_map/ppermute | solution.py:22
  196.5 5.0 %last.1 = (f32[1024,768]{1,0:T(8,128)}, f32[16,768]{1,0:T(8,128)S(1)}) custom-call(f32[1024,768]{1,0:T(8,128)} %get-tuple-element.209.dz_ref, bf16[1024,768]{1,0:T(8,128)(2,1)} %get-tuple-element.220.own_ref, bf16[1024,768]{1,0:T(8,128)(2,1)S(1)} %collective-permute-done.33.other_ref, f32[1024,128]{1,0:T(8,128)} %broadcast_in_dim.41.flag_ref, ...), custom_call_target="tpu_custom_call" | custom-call | flops 1 | bytes 1 | tf_op jit(solution)/shard_map/last/pallas_call | solution.py:64
  203.7 3.3 %collective-permute-done.45 = f32[16,768]{1,0:T(8,128)S(1)} collective-permute-done((f32[16,768]{1,0:T(8,128)S(1)}, f32[16,768]{1,0:T(8,128)S(1)}, u32[]{:S(2)}, u32[]{:S(2)}) %collective-permute-start.45) | collective-permute-done | bytes 49184 | tf_op jit(solution)/shard_map/ppermute | solution.py:22
  207.4 3.7 %collective-permute-done.46 = f32[16,768]{1,0:T(8,128)S(1)} collective-permute-done((f32[16,768]{1,0:T(8,128)S(1)}, f32[16,768]{1,0:T(8,128)S(1)}, u32[]{:S(2)}, u32[]{:S(2)}) %collective-permute-start.46) | collective-permute-done | bytes 49184 | tf_op jit(solution)/shard_map/ppermute | solution.py:22
  215.4 2.8 %collective-permute-start.48 = (f32[16,768]{1,0:T(8,128)S(1)}, f32[16,768]{1,0:T(8,128)S(1)}, u32[]{:S(2)}, u32[]{:S(2)}) collective-permute-start(f32[16,768]{1,0:T(8,128)S(1)} %add.23), channel_id=1, source_target_pairs={{0,16},{2,18},{4,20},{6,22},{8,24},{10,26},{12,28},{14,30},{16,0},... | collective-permute-start | bytes 147464 | tf_op jit(solution)/shard_map/ppermute | solution.py:22
  222.3 3.7 %collective-permute-done.49 = bf16[48,1536]{1,0:T(8,128)(2,1)S(1)} collective-permute-done((bf16[48,1536]{1,0:T(8,128)(2,1)S(1)}, bf16[48,1536]{1,0:T(8,128)(2,1)S(1)}, u32[]{:S(2)}, u32[]{:S(2)}) %collective-permute-start.49) | collective-permute-done | bytes 147488 | tf_op jit(solution)/shard_map/ppermute | solution.py:22
  (188 shorter events, 76.1 us)
Async XLA Ops:
  16.1 11.6 %collective-permute-start.2 = (bf16[2,48,1536]{2,1,0:T(8,128)(2,1)S(1)}, bf16[2,48,1536]{2,1,0:T(8,128)(2,1)S(1)}, u32[]{:S(2)}, u32[]{:S(2)}) collective-permute-start(bf16[2,48,1536]{2,1,0:T(8,128)(2,1)S(1)} %pad_maximum_fusion.rest_0_), channel_id=1, source_target_pairs={{0,2},{2,0},{4,6},{6,4},{8,10},{10,8},{12,14},{14,12},{16,18},{18,... | collective-permute-start | bytes 884744 | tf_op jit(solution)/shard_map/ppermute | solution.py:22
  17.6 11.7 %collective-permute-start.4 = (bf16[2,48,1536]{2,1,0:T(8,128)(2,1)S(1)}, bf16[2,48,1536]{2,1,0:T(8,128)(2,1)S(1)}, u32[]{:S(2)}, u32[]{:S(2)}) collective-permute-start(bf16[2,48,1536]{2,1,0:T(8,128)(2,1)S(1)} %pad_maximum_fusion.rest_0_), channel_id=1, source_target_pairs={{0,4},{2,6},{4,0},{6,2},{8,12},{10,14},{12,8},{14,10},{16,20},{18,... | collective-permute-start | bytes 884744 | tf_op jit(solution)/shard_map/ppermute | solution.py:22
  24.6 12.8 %collective-permute-start.9 = (bf16[2,48,1536]{2,1,0:T(8,128)(2,1)S(1)}, bf16[2,48,1536]{2,1,0:T(8,128)(2,1)S(1)}, u32[]{:S(2)}, u32[]{:S(2)}) collective-permute-start(bf16[2,48,1536]{2,1,0:T(8,128)(2,1)S(1)} %pad_maximum_fusion.1.rest_0_), channel_id=1, source_target_pairs={{0,8},{2,10},{4,12},{6,14},{8,0},{10,2},{12,4},{14,6},{16,24},{18,... | collective-permute-start | bytes 884744 | tf_op jit(solution)/shard_map/ppermute | solution.py:22
  27.7 12.6 %collective-permute-start.10 = (bf16[2,48,1536]{2,1,0:T(8,128)(2,1)S(1)}, bf16[2,48,1536]{2,1,0:T(8,128)(2,1)S(1)}, u32[]{:S(2)}, u32[]{:S(2)}) collective-permute-start(bf16[2,48,1536]{2,1,0:T(8,128)(2,1)S(1)} %pad_maximum_fusion.1.rest_0_), channel_id=1, source_target_pairs={{0,2},{2,0},{4,6},{6,4},{8,10},{10,8},{12,14},{14,12},{16,18},{18,... | collective-permute-start | bytes 884744 | tf_op jit(solution)/shard_map/ppermute | solution.py:22
  29.3 11.1 %collective-permute-start.11 = (bf16[2,48,1536]{2,1,0:T(8,128)(2,1)S(1)}, bf16[2,48,1536]{2,1,0:T(8,128)(2,1)S(1)}, u32[]{:S(2)}, u32[]{:S(2)}) collective-permute-start(bf16[2,48,1536]{2,1,0:T(8,128)(2,1)S(1)} %pad_maximum_fusion.1.rest_0_), channel_id=1, source_target_pairs={{0,4},{2,6},{4,0},{6,2},{8,12},{10,14},{12,8},{14,10},{16,20},{18,... | collective-permute-start | bytes 884744 | tf_op jit(solution)/shard_map/ppermute | solution.py:22
  31.9 12.0 %collective-permute-start.3 = (bf16[2,48,1536]{2,1,0:T(8,128)(2,1)S(1)}, bf16[2,48,1536]{2,1,0:T(8,128)(2,1)S(1)}, u32[]{:S(2)}, u32[]{:S(2)}) collective-permute-start(bf16[2,48,1536]{2,1,0:T(8,128)(2,1)S(1)} %collective-permute-done.1.rest_1_), channel_id=1, source_target_pairs={{0,2},{2,0},{4,6},{6,4},{8,10},{10,8},{12,14},{14,12},{16,18},{18,... | collective-permute-start | bytes 884744 | tf_op jit(solution)/shard_map/ppermute | solution.py:22
  47.9 16.5 %collective-permute-start.13 = (bf16[2,48,1536]{2,1,0:T(8,128)(2,1)S(1)}, bf16[2,48,1536]{2,1,0:T(8,128)(2,1)}, u32[]{:S(2)}, u32[]{:S(2)}) collective-permute-start(bf16[2,48,1536]{2,1,0:T(8,128)(2,1)S(1)} %collective-permute-done.9.rest_1_), channel_id=1, source_target_pairs={{0,2},{2,0},{4,6},{6,4},{8,10},{10,8},{12,14},{14,12},{16,18},{18,... | collective-permute-start | bytes 884744 | tf_op jit(solution)/shard_map/ppermute | solution.py:22
  49.2 15.2 %collective-permute-start.14 = (bf16[2,48,1536]{2,1,0:T(8,128)(2,1)S(1)}, bf16[2,48,1536]{2,1,0:T(8,128)(2,1)}, u32[]{:S(2)}, u32[]{:S(2)}) collective-permute-start(bf16[2,48,1536]{2,1,0:T(8,128)(2,1)S(1)} %collective-permute-done.9.rest_1_), channel_id=1, source_target_pairs={{0,4},{2,6},{4,0},{6,2},{8,12},{10,14},{12,8},{14,10},{16,20},{18,... | collective-permute-start | bytes 884744 | tf_op jit(solution)/shard_map/ppermute | solution.py:22
  50.8 13.6 %collective-permute-start.16 = (bf16[2,48,1536]{2,1,0:T(8,128)(2,1)S(1)}, bf16[2,48,1536]{2,1,0:T(8,128)(2,1)S(1)}, u32[]{:S(2)}, u32[]{:S(2)}) collective-permute-start(bf16[2,48,1536]{2,1,0:T(8,128)(2,1)S(1)} %pad_maximum_fusion.2.rest_0_), channel_id=1, source_target_pairs={{0,8},{2,10},{4,12},{6,14},{8,0},{10,2},{12,4},{14,6},{16,24},{18,... | collective-permute-start | bytes 884744 | tf_op jit(solution)/shard_map/ppermute | solution.py:22
  51.8 12.6 %collective-permute-start.17 = (bf16[2,48,1536]{2,1,0:T(8,128)(2,1)S(1)}, bf16[2,48,1536]{2,1,0:T(8,128)(2,1)S(1)}, u32[]{:S(2)}, u32[]{:S(2)}) collective-permute-start(bf16[2,48,1536]{2,1,0:T(8,128)(2,1)S(1)} %pad_maximum_fusion.2.rest_0_), channel_id=1, source_target_pairs={{0,2},{2,0},{4,6},{6,4},{8,10},{10,8},{12,14},{14,12},{16,18},{18,... | collective-permute-start | bytes 884744 | tf_op jit(solution)/shard_map/ppermute | solution.py:22
  52.4 12.0 %collective-permute-start.15 = (bf16[2,48,1536]{2,1,0:T(8,128)(2,1)S(1)}, bf16[2,48,1536]{2,1,0:T(8,128)(2,1)}, u32[]{:S(2)}, u32[]{:S(2)}) collective-permute-start(bf16[2,48,1536]{2,1,0:T(8,128)(2,1)S(1)} %collective-permute-done.10.rest_2_), channel_id=1, source_target_pairs={{0,4},{2,6},{4,0},{6,2},{8,12},{10,14},{12,8},{14,10},{16,20},{18,... | collective-permute-start | bytes 884744 | tf_op jit(solution)/shard_map/ppermute | solution.py:22
  75.2 11.5 %collective-permute-start.21 = (bf16[2,48,1536]{2,1,0:T(8,128)(2,1)S(1)}, bf16[2,48,1536]{2,1,0:T(8,128)(2,1)S(1)}, u32[]{:S(2)}, u32[]{:S(2)}) collective-permute-start(bf16[2,48,1536]{2,1,0:T(8,128)(2,1)S(1)} %collective-permute-done.16.rest_1_), channel_id=1, source_target_pairs={{0,2},{2,0},{4,6},{6,4},{8,10},{10,8},{12,14},{14,12},{16,18},{18,... | collective-permute-start | bytes 884744 | tf_op jit(solution)/shard_map/ppermute | solution.py:22
  75.7 11.0 %collective-permute-start.22 = (bf16[2,48,1536]{2,1,0:T(8,128)(2,1)S(1)}, bf16[2,48,1536]{2,1,0:T(8,128)(2,1)S(1)}, u32[]{:S(2)}, u32[]{:S(2)}) collective-permute-start(bf16[2,48,1536]{2,1,0:T(8,128)(2,1)S(1)} %collective-permute-done.16.rest_1_), channel_id=1, source_target_pairs={{0,4},{2,6},{4,0},{6,2},{8,12},{10,14},{12,8},{14,10},{16,20},{18,... | collective-permute-start | bytes 884744 | tf_op jit(solution)/shard_map/ppermute | solution.py:22
  118.9 22.1 %collective-permute-start.26 = (bf16[4,48,1536]{2,1,0:T(8,128)(2,1)}, bf16[4,48,1536]{2,1,0:T(8,128)(2,1)S(1)}, u32[]{:S(2)}, u32[]{:S(2)}) collective-permute-start(bf16[4,48,1536]{2,1,0:T(8,128)(2,1)} %get-tuple-element.198), channel_id=1, source_target_pairs={{0,2},{2,0},{4,6},{6,4},{8,10},{10,8},{12,14},{14,12},{16,18},{18,... | collective-permute-start | bytes 1769480 | tf_op jit(solution)/shard_map/ppermute | solution.py:22
  120.2 20.9 %collective-permute-start.27 = (bf16[4,48,1536]{2,1,0:T(8,128)(2,1)}, bf16[4,48,1536]{2,1,0:T(8,128)(2,1)S(1)}, u32[]{:S(2)}, u32[]{:S(2)}) collective-permute-start(bf16[4,48,1536]{2,1,0:T(8,128)(2,1)} %get-tuple-element.199), channel_id=1, source_target_pairs={{0,4},{2,6},{4,0},{6,2},{8,12},{10,14},{12,8},{14,10},{16,20},{18,... | collective-permute-start | bytes 1769480 | tf_op jit(solution)/shard_map/ppermute | solution.py:22
  141.2 22.8 %collective-permute-start.31 = (bf16[4,48,1536]{2,1,0:T(8,128)(2,1)}, bf16[4,48,1536]{2,1,0:T(8,128)(2,1)S(1)}, u32[]{:S(2)}, u32[]{:S(2)}) collective-permute-start(bf16[4,48,1536]{2,1,0:T(8,128)(2,1)} %get-tuple-element.218), channel_id=1, source_target_pairs={{0,2},{2,0},{4,6},{6,4},{8,10},{10,8},{12,14},{14,12},{16,18},{18,... | collective-permute-start | bytes 1769480 | tf_op jit(solution)/shard_map/ppermute | solution.py:22
  142.0 21.9 %collective-permute-start.32 = (bf16[4,48,1536]{2,1,0:T(8,128)(2,1)}, bf16[4,48,1536]{2,1,0:T(8,128)(2,1)S(1)}, u32[]{:S(2)}, u32[]{:S(2)}) collective-permute-start(bf16[4,48,1536]{2,1,0:T(8,128)(2,1)} %get-tuple-element.219), channel_id=1, source_target_pairs={{0,4},{2,6},{4,0},{6,2},{8,12},{10,14},{12,8},{14,10},{16,20},{18,... | collective-permute-start | bytes 1769480 | tf_op jit(solution)/shard_map/ppermute | solution.py:22
  142.5 21.0 %collective-permute-start.29 = (bf16[2,48,1536]{2,1,0:T(8,128)(2,1)S(1)}, bf16[2,48,1536]{2,1,0:T(8,128)(2,1)S(1)}, u32[]{:S(2)}, u32[]{:S(2)}) collective-permute-start(bf16[2,48,1536]{2,1,0:T(8,128)(2,1)S(1)} %get-tuple-element.216), channel_id=1, source_target_pairs={{0,2},{2,0},{4,6},{6,4},{8,10},{10,8},{12,14},{14,12},{16,18},{18,... | collective-permute-start | bytes 884744 | tf_op jit(solution)/shard_map/ppermute | solution.py:22
  143.8 20.1 %collective-permute-start.30 = (bf16[2,48,1536]{2,1,0:T(8,128)(2,1)S(1)}, bf16[2,48,1536]{2,1,0:T(8,128)(2,1)S(1)}, u32[]{:S(2)}, u32[]{:S(2)}) collective-permute-start(bf16[2,48,1536]{2,1,0:T(8,128)(2,1)S(1)} %get-tuple-element.217), channel_id=1, source_target_pairs={{0,4},{2,6},{4,0},{6,2},{8,12},{10,14},{12,8},{14,10},{16,20},{18,... | collective-permute-start | bytes 884744 | tf_op jit(solution)/shard_map/ppermute | solution.py:22
  164.0 11.9 %collective-permute-start.33 = (bf16[1024,768]{1,0:T(8,128)(2,1)}, bf16[1024,768]{1,0:T(8,128)(2,1)S(1)}, u32[]{:S(2)}, u32[]{:S(2)}) collective-permute-start(bf16[1024,768]{1,0:T(8,128)(2,1)} %get-tuple-element.220.own_ref), channel_id=1, source_target_pairs={{0,1},{1,0},{2,3},{3,2},{4,5},{5,4},{6,7},{7,6},{8,9},{9,8},{10,11... | collective-permute-start | bytes 4718600 | tf_op jit(solution)/shard_map/ppermute | solution.py:34
  164.2 11.7 %collective-permute-start.36 = (bf16[2,48,1536]{2,1,0:T(8,128)(2,1)S(1)}, bf16[2,48,1536]{2,1,0:T(8,128)(2,1)S(1)}, u32[]{:S(2)}, u32[]{:S(2)}) collective-permute-start(bf16[2,48,1536]{2,1,0:T(8,128)(2,1)S(1)} %get-tuple-element.235), channel_id=1, source_target_pairs={{0,8},{2,10},{4,12},{6,14},{8,0},{10,2},{12,4},{14,6},{16,24},{18,... | collective-permute-start | bytes 884744 | tf_op jit(solution)/shard_map/ppermute | solution.py:22
  175.9 15.2 %collective-permute-start.37 = (bf16[4,48,1536]{2,1,0:T(8,128)(2,1)}, bf16[4,48,1536]{2,1,0:T(8,128)(2,1)S(1)}, u32[]{:S(2)}, u32[]{:S(2)}) collective-permute-start(bf16[4,48,1536]{2,1,0:T(8,128)(2,1)} %get-tuple-element.237), channel_id=1, source_target_pairs={{0,2},{2,0},{4,6},{6,4},{8,10},{10,8},{12,14},{14,12},{16,18},{18,... | collective-permute-start | bytes 1769480 | tf_op jit(solution)/shard_map/ppermute | solution.py:22
  176.8 14.8 %collective-permute-start.38 = (bf16[4,48,1536]{2,1,0:T(8,128)(2,1)}, bf16[4,48,1536]{2,1,0:T(8,128)(2,1)S(1)}, u32[]{:S(2)}, u32[]{:S(2)}) collective-permute-start(bf16[4,48,1536]{2,1,0:T(8,128)(2,1)} %get-tuple-element.238), channel_id=1, source_target_pairs={{0,4},{2,6},{4,0},{6,2},{8,12},{10,14},{12,8},{14,10},{16,20},{18,... | collective-permute-start | bytes 1769480 | tf_op jit(solution)/shard_map/ppermute | solution.py:22
  178.6 11.2 %collective-permute-start.39 = (bf16[2,48,1536]{2,1,0:T(8,128)(2,1)S(1)}, bf16[2,48,1536]{2,1,0:T(8,128)(2,1)S(1)}, u32[]{:S(2)}, u32[]{:S(2)}) collective-permute-start(bf16[2,48,1536]{2,1,0:T(8,128)(2,1)S(1)} %get-tuple-element.242), channel_id=1, source_target_pairs={{0,8},{2,10},{4,12},{6,14},{8,0},{10,2},{12,4},{14,6},{16,24},{18,... | collective-permute-start | bytes 884744 | tf_op jit(solution)/shard_map/ppermute | solution.py:22
  (56 other events, 582.6 us)
